TPU v7x, 128 devices: a whole 4x4x4 slice. The times are simulated.
128 devices in a mesh: scene: 4 (over x_lo, core), frame: 32 (over y, z, x_hi).
Axes of the slice: x: 4 (x_hi: 2, x_lo: 2; x = x_hi * 2 + x_lo), y: 4, z: 4, core: 2. Of those that a mesh axis runs over, the one named last changes fastest.
Arguments:
- features: bfloat16 [32768, 1024], P(('scene', 'frame')), parts along dimension 0, may hold values from -1.5 to 1.5
- norm_gain: float32 [1024], replicated, may hold values from 0.1 to 1.9
- w_qkv: bfloat16 [1024, 3072], replicated, may hold values from -1.3125 to 1.3125
- w_out: bfloat16 [1024, 1024], replicated, may hold values from -0.1875 to 0.1875
- counts: int32 [128], P('scene'), parts along dimension 0, may hold values from 1 to 32, as said below
- query_index: int32 [128, 32], P(('scene', 'frame')), parts along dimension 0, may hold values from 0 to 255
- owner: int32 [128], P('scene'), parts along dimension 0, may hold values from 0 to 31
Outputs:
- mixed: bfloat16 [32768, 1024], P(('scene', 'frame')), parts along dimension 0
- correlation: float32 [128, 32, 32, 256], P(('scene', 'frame')), parts along dimension 0
There are 4 independent parts, one for each index of `scene`. A program takes and returns all parts, laid end to end along the dimension named above; an argument that names none is the same for every part. Nothing has to cross between parts.
Inputs may be any that keep to these rules, and one draw needn't show every extreme that they name: `counts`: every frame has at least one query and some frame has exactly 32.
All inputs are finite; a program needn't handle non-finite values.
Results may differ from a plain program's by a relative error of at most 0.017.
The roundings to bfloat16 on the way count: a program that leaves them out, or rounds other values in their place, can miss the bound.
Values may be sent and summed in bfloat16 or wider, within the bound.
No kernel may reach another device: no remote copies, remote signals or barrier semaphores. Data moves between devices by JAX's collectives and lax.ppermute only.
A program may use at most 256 MiB of HBM per device.

v0:
```python
import jax
import jax.numpy as jnp
from jax import lax
from jax.sharding import PartitionSpec as P

D = 1024
HEADS = 16


def normalize(x, gain):
    xf = x.astype(jnp.float32)
    mean = jnp.mean(xf, axis=-1, keepdims=True)
    var = jnp.mean((xf - mean) ** 2, axis=-1, keepdims=True)
    return ((xf - mean) * lax.rsqrt(var + 1e-05) * gain).astype(jnp.bfloat16)


def per_device(features, norm_gain, w_qkv, w_out, counts, query_index, owner):
    tok = features.shape[0]
    frames = counts.shape[0]
    head_dim = D // HEADS
    normed = normalize(features, norm_gain)
    proj = jnp.dot(normed, w_qkv, preferred_element_type=jnp.float32)
    queries = (
        (proj[:, :D] * (1.0 / head_dim**0.5)).astype(jnp.bfloat16).reshape(tok, HEADS, head_dim)
    )
    keys = proj[:, D : 2 * D].astype(jnp.bfloat16)
    values = proj[:, 2 * D :].astype(jnp.bfloat16)

    def absorb(carry, piece):
        top, total, accum = carry
        kpart, vpart = piece
        count = kpart.shape[0]
        scores = jnp.einsum(
            "thd,shd->hts",
            queries,
            kpart.reshape(count, HEADS, head_dim),
            preferred_element_type=jnp.float32,
        )
        newtop = jnp.maximum(top, jnp.max(scores, axis=-1))
        factor = jnp.exp(top - newtop)
        weights = jnp.exp(scores - newtop[:, :, None])
        total = total * factor + jnp.sum(weights, axis=-1)
        accum = accum * factor[:, :, None] + jnp.einsum(
            "hts,shd->htd",
            weights.astype(jnp.bfloat16),
            vpart.reshape(count, HEADS, head_dim),
            preferred_element_type=jnp.float32,
        )
        return (newtop, total, accum)

    start_state = (
        jnp.full((HEADS, tok), -1e30, jnp.float32),
        jnp.zeros((HEADS, tok), jnp.float32),
        jnp.zeros((HEADS, tok, head_dim), jnp.float32),
    )
    joined = lax.all_gather(jnp.stack([keys, values]), "frame", axis=1, tiled=True)
    stacked = joined.reshape(2, frames, tok, D)

    def step(carry, pair):
        return (absorb(carry, (pair[0], pair[1])), None)

    (top, total, accum), unused = lax.scan(step, start_state, jnp.transpose(stacked, (1, 0, 2, 3)))
    attended = (
        jnp.transpose(accum / total[:, :, None], (1, 0, 2)).reshape(tok, D).astype(jnp.bfloat16)
    )
    mixed = (
        features.astype(jnp.float32) + jnp.dot(attended, w_out, preferred_element_type=jnp.float32)
    ).astype(jnp.bfloat16)
    mine = lax.axis_index("frame")
    slots = query_index[0]
    picked = mixed[slots]
    valid = jnp.arange(slots.shape[0]) < counts[mine]
    picked = jnp.where(valid[:, None], picked, jnp.zeros_like(picked))
    arrived = lax.all_gather(picked[None], "frame", axis=0, tiled=True)
    corr = jnp.einsum("fqd,td->fqt", arrived, mixed, preferred_element_type=jnp.float32) * (
        1.0 / D**0.5
    )
    owned = owner == mine
    corr = jnp.where(owned[:, None, None], corr, jnp.float32(0.0))
    return (mixed, corr[None])


def solution(mesh):
    in_specs = (
        P(("scene", "frame"), None),
        P(),
        P(),
        P(),
        P("scene"),
        P(("scene", "frame"), None),
        P("scene"),
    )
    out_specs = (P(("scene", "frame"), None), P(("scene", "frame"), None, None, None))
    return jax.shard_map(
        per_device, mesh=mesh, in_specs=in_specs, out_specs=out_specs, check_vma=False
    )
```

profile of v0, /device:TPU:0, one launch (start us, length us, event | category | flops | bytes accessed | tf_op | source)
XLA Modules:
  0.0 745.5 jit_solution(9825440337620059144)
XLA Ops:
  9.9 6.5 fusion.26
  20.5 262.4 %all-gather.3.cloned.1.call-done = bf16[2,8192,1024]{2,1,0:T(8,128)(2,1)} async-done(((bf16[2,256,1024]{2,1,0:T(8,128)(2,1)}), bf16[2,8192,1024]{2,1,0:T(8,128)(2,1)}) %all-gather.3.cloned.1.call-update) | async-done | bytes 33554448 | tf_op jit(solution)/shard_map/all_gather | solution.py:56
  282.9 44.2 %copy.16 = bf16[2,32,256,1024]{2,3,0,1:T(8,128)(2,1)} copy(bf16[2,32,256,1024]{3,2,1,0:T(8,128)(2,1)} %bitcast.62) | data formatting | bytes 67108864 | tf_op jit(solution)/shard_map/reshape | solution.py:57
  327.1 334.9 %while.15 = (s32[]{:T(128)}, f32[16,256]{1,0:T(8,128)S(1)}, f32[16,256]{1,0:T(8,128)S(1)}, f32[16,256,64]{1,2,0:T(8,128)}, bf16[32,2,256,1024]{2,3,1,0:T(8,128)(...) while((s32[]{:T(128)}, f32[16,256]{1,0:T(8,128)S(1)}, ...), condition=%wide.region_5.6_spmd.clone, body=%wide.region_2.5_spmd.clone.sunk | while | flops 274485248 | bytes 35389592 | solution.py:62
  343.8 3.1 fusion.47
  354.3 3.1 fusion.47
  364.8 3.1 fusion.47
  385.8 3.1 fusion.47
  396.3 3.1 fusion.47
  417.3 3.1 fusion.47
  427.8 3.1 fusion.47
  448.9 3.1 fusion.47
  459.4 3.1 fusion.47
  480.4 3.1 fusion.47
  490.9 3.1 fusion.47
  511.9 3.1 fusion.47
  522.4 3.1 fusion.47
  543.4 3.1 fusion.47
  553.9 3.1 fusion.47
  585.4 3.1 fusion.47
  616.9 3.1 fusion.47
  648.4 3.1 fusion.47
  666.5 68.8 %all-gather.5.cloned.1.call-done = bf16[32,32,1024]{2,1,0:T(8,128)(2,1)} async-done(((bf16[1,32,1024]{2,1,0:T(8,128)(2,1)}), bf16[32,32,1024]{2,1,0:T(8,128)(2,1)}) %all-gather.5.cloned.1.call-update) | async-done | bytes 2097168 | tf_op jit(solution)/shard_map/all_gather | solution.py:74
  735.3 3.3 fusion.11
  (304 shorter events, 290.2 us)
Async XLA Ops:
  7.2 656.2 %copy-start = (bf16[1024,1024]{1,0:T(8,128)(2,1)S(1)}, bf16[1024,1024]{1,0:T(8,128)(2,1)}, u32[]{:S(2)}) copy-start(bf16[1024,1024]{1,0:T(8,128)(2,1)} %param.12) | copy-start | bytes 6291460
  7.2 275.7 %all-gather.3.cloned.1.call-start = ((), (), s32[]{:S(2)}) async-start(), calls=%async_computation | async-start | bytes 34603008 | tf_op jit(solution)/shard_map/all_gather | solution.py:56
  16.4 4.1 copy-start.4
  17.6 717.7 %all-gather.5.cloned.1.call-start = ((), (), s32[]{:S(2)}) async-start(), calls=%async_computation.1 | async-start | bytes 2162688 | tf_op jit(solution)/shard_map/all_gather | solution.py:74
  331.1 3.4 copy-start.1
  340.4 3.4 copy-start.1
  361.4 3.4 copy-start.1
  371.9 3.4 copy-start.1
  392.9 3.4 copy-start.1
  403.4 3.4 copy-start.1
  413.9 3.4 copy-start.1
  424.4 3.4 copy-start.1
  434.9 3.4 copy-start.1
  445.4 3.4 copy-start.1
  455.9 3.4 copy-start.1
  466.4 3.4 copy-start.1
  476.9 3.4 copy-start.1
  497.9 3.4 copy-start.1
  508.4 3.4 copy-start.1
  539.9 3.4 copy-start.1
  571.4 3.4 copy-start.1
  603.0 3.4 copy-start.1
  662.0 4.5 copy-start.5
  665.1 73.5 %copy-start.2 = (bf16[256,1024]{1,0:T(8,128)(2,1)}, bf16[256,1024]{1,0:T(8,128)(2,1)S(1)}, u32[]{:S(2)}) copy-start(bf16[256,1024]{1,0:T(8,128)(2,1)S(1)} %fusion.12) | copy-start | bytes 1572868
  (15 other events, 51.1 us)
Sparse Core Ops, SparseCore 0:
  17.8 265.0 all-gather.2
  666.6 68.6 all-gather.4
where the time goes:
time: 749 us; the launch traced here: 745 us
  waiting for transfers between devices  331 us (44%)
  matrix products  195 us (26%)
  local copies, waits for them, and re-layouts  102 us (14%)
  other arithmetic  102 us (14%)
  between operations  14.2 us (2%)
    all_gather x1, waiting for transfers between devices, per_device(): lax.all_gather(jnp.stack([keys, values]), 'frame', axis=1, tiled=True)  262 us
    dot_general x32, matrix products, absorb(): jnp.einsum('hts,shd->htd', weights.astype(jnp.bfloat16), vpart.reshape(co...  97.1 us
    reduce_sum x32, other arithmetic, absorb(): total = total * factor + jnp.sum(weights, axis=-1)  93.3 us
    dot_general x32, matrix products, absorb(): jnp.einsum('thd,shd->hts', queries, kpart.reshape(count, HEADS, head_dim)...  86.6 us
    all_gather x1, waiting for transfers between devices, per_device(): arrived = lax.all_gather(picked[None], 'frame', axis=0, tiled=True)  68.8 us
    reshape x1, local copies, waits for them, and re-layouts, per_device(): stacked = joined.reshape(2, frames, tok, D)  44.2 us
    slice x32, local copies, waits for them, and re-layouts, step(): return (absorb(carry, (pair[0], pair[1])), None)  40.6 us
    while x96, local copies, waits for them, and re-layouts  16.1 us
  transfers between devices with their start and end apart: 2, of which 2 were waited for; matrix products, arithmetic and copies ran while one was open for 0% of the time, Pallas kernels for 0%

commit v1 on v0

v1 whole, which is shorter than its diff:
```python
import functools

import jax
import jax.numpy as jnp
from jax import lax
from jax.experimental import pallas as pl
from jax.experimental.pallas import tpu as pltpu
from jax.sharding import PartitionSpec as P

D = 1024
HEADS = 16
HDIM = 64
TOK = 256
FRAMES = 32
QMAX = 32
LANES = 128
LOG2E = 1.4426950408889634
MARGIN = 64.0
NT = (((1,), (1,)), ((), ()))
F32 = jnp.float32
BF16 = jnp.bfloat16


def low_half(rows):
    return lax.broadcasted_iota(jnp.int32, (rows, LANES), 1) < HDIM


def swap(x):
    return pltpu.roll(x, HDIM, 1)


def project_kernel(x_ref, g_ref, wq_ref, wk_ref, wv_ref, o_ref, n_ref):
    @pl.when(pl.program_id(0) == 0)
    def _():
        xf = x_ref[...].astype(F32)
        mean = jnp.mean(xf, axis=-1, keepdims=True)
        cen = xf - mean
        var = jnp.mean(cen * cen, axis=-1, keepdims=True)
        n_ref[...] = (cen * lax.rsqrt(var + 1e-05) * g_ref[...]).astype(BF16)

    n = n_ref[...]
    q = jnp.dot(n, wq_ref[...], preferred_element_type=F32) * (1.0 / HDIM**0.5)
    k = jnp.dot(n, wk_ref[...], preferred_element_type=F32)
    v = jnp.dot(n, wv_ref[...], preferred_element_type=F32)
    half = TOK // 2
    low = low_half(TOK)
    lowh = low_half(half)
    for c in range(wq_ref.shape[1] // LANES):
        cols = slice(c * LANES, (c + 1) * LANES)
        kp, vp = k[:, cols], v[:, cols]
        qa, qb = q[:half, cols], q[half:, cols]
        o_ref[2 * c, :TOK] = jnp.where(low, kp, swap(vp)).astype(BF16)
        o_ref[2 * c + 1, :TOK] = jnp.where(low, swap(kp), vp).astype(BF16)
        o_ref[2 * c, TOK:] = jnp.where(lowh, qa, swap(qb)).astype(BF16)
        o_ref[2 * c + 1, TOK:] = jnp.where(lowh, swap(qa), qb).astype(BF16)


def project(x, gain, w_qkv):
    steps = 4
    width = D // steps
    return pl.pallas_call(
        project_kernel,
        grid=(steps,),
        in_specs=[
            pl.BlockSpec((TOK, D), lambda i: (0, 0)),
            pl.BlockSpec((1, D), lambda i: (0, 0)),
            pl.BlockSpec((D, width), lambda i: (0, i)),
            pl.BlockSpec((D, width), lambda i: (0, i + steps)),
            pl.BlockSpec((D, width), lambda i: (0, i + 2 * steps)),
        ],
        out_specs=pl.BlockSpec((HEADS // steps, TOK + TOK // 2, LANES), lambda i: (i, 0, 0)),
        out_shape=jax.ShapeDtypeStruct((HEADS, TOK + TOK // 2, LANES), BF16),
        scratch_shapes=[pltpu.VMEM((TOK, D), BF16)],
        compiler_params=pltpu.CompilerParams(vmem_limit_bytes=32 << 20),
        name="project",
    )(x, gain.reshape(1, D), w_qkv, w_qkv, w_qkv)


TILE_FRAMES = 4
BLOCK_FRAMES = 4
GROUP = FRAMES // 2


def load_queries(q_ref):
    packed = q_ref[...].reshape(TILE_FRAMES * TOK // 2, LANES).astype(F32)
    low = low_half(packed.shape[0])
    zero = jnp.zeros_like(packed)
    both = [jnp.where(low, packed, zero), jnp.where(low, swap(packed), zero)]
    return jnp.concatenate(both, axis=0).astype(BF16)


def kv_block(kv_ref, j, count):
    return kv_ref[pl.ds(j * count, count), :TOK].reshape(count * TOK, LANES)


def with_ones(kv):
    low = low_half(kv.shape[0])
    return jnp.where(low, jnp.ones_like(kv), kv)


def fill_values(kv_ref, va_ref):
    @pl.when(pl.program_id(0) == 0)
    def _():
        for j in range(GROUP):
            va_ref[j] = with_ones(kv_ref[j, :TOK])


def partial_sums(q, ref_point, kv_ref, va_ref):
    acc = jnp.zeros((q.shape[0], LANES), F32)
    for j in range(GROUP // BLOCK_FRAMES):
        s = lax.dot_general(q, kv_block(kv_ref, j, BLOCK_FRAMES), NT, preferred_element_type=F32)
        p = jnp.exp2(s * LOG2E - ref_point).astype(BF16)
        acc += jnp.dot(p, kv_block(va_ref, j, BLOCK_FRAMES), preferred_element_type=F32)
    return acc


def first_kernel(q_ref, kv_ref, acc_ref, va_ref):
    fill_values(kv_ref, va_ref)
    q = load_queries(q_ref)
    s = lax.dot_general(q, kv_block(kv_ref, 0, 2), NT, preferred_element_type=F32)
    ref_point = jnp.max(s, axis=-1, keepdims=True) * LOG2E + MARGIN
    acc = partial_sums(q, ref_point, kv_ref, va_ref)
    lane = lax.broadcasted_iota(jnp.int32, acc.shape, 1)
    acc_ref[...] = jnp.where(lane == 1, ref_point, acc)


def second_kernel(q_ref, kv_ref, kv2_ref, first_ref, o_ref, va_ref):
    fill_values(kv2_ref, va_ref)
    q = load_queries(q_ref)
    rows = q.shape[0]

    def store(total):
        out = total / total[:, :1]
        packed = jnp.where(low_half(rows // 2), swap(out[: rows // 2]), out[rows // 2 :])
        o_ref[...] = packed.astype(BF16).reshape(o_ref.shape)

    ref_point = first_ref[:, 1:2]
    total = first_ref[...] + partial_sums(q, ref_point, kv2_ref, va_ref)
    sums = total[:, :1]
    store(total)
    safe = jnp.min(jnp.where((sums < 2.0**100) & (sums > 2.0**-100), 1.0, 0.0)) > 0.5

    @pl.when(jnp.logical_not(safe))
    def _():
        def absorb(ref):
            def step(j, carry):
                top, acc = carry
                kv = ref[j, :TOK]
                s = lax.dot_general(q, kv, NT, preferred_element_type=F32)
                newtop = jnp.maximum(top, jnp.max(s, axis=-1, keepdims=True))
                p = jnp.exp(s - newtop).astype(BF16)
                acc = acc * jnp.exp(top - newtop)
                acc += jnp.dot(p, with_ones(kv), preferred_element_type=F32)
                return newtop, acc

            return step

        start = (jnp.full((rows, 1), -1e30, F32), jnp.zeros((rows, LANES), F32))
        carry = lax.fori_loop(0, GROUP, absorb(kv_ref), start)
        top, acc = lax.fori_loop(0, GROUP, absorb(kv2_ref), carry)
        store(acc)


def attend(mine, other):
    tiles = GROUP // TILE_FRAMES
    rows = TILE_FRAMES * TOK
    q_spec = pl.BlockSpec((TILE_FRAMES, TOK // 2, LANES), lambda i: (i, 2, 0))
    own_spec = pl.BlockSpec((GROUP, TOK + TOK // 2, LANES), lambda i: (0, 0, 0))
    other_spec = pl.BlockSpec((GROUP, TOK, LANES), lambda i: (0, 0, 0))
    acc_spec = pl.BlockSpec((rows, LANES), lambda i: (i, 0))
    params = pltpu.CompilerParams(vmem_limit_bytes=56 << 20)
    pairs = GROUP * TOK * GROUP * TOK
    cost = pl.CostEstimate(
        flops=4 * pairs * LANES * 2, bytes_accessed=8 << 20, transcendentals=pairs
    )
    scratch = [pltpu.VMEM((GROUP, TOK, LANES), BF16)]
    first = pl.pallas_call(
        first_kernel,
        grid=(tiles,),
        in_specs=[q_spec, own_spec],
        out_specs=acc_spec,
        out_shape=jax.ShapeDtypeStruct((GROUP * TOK, LANES), F32),
        scratch_shapes=scratch,
        compiler_params=params,
        cost_estimate=cost,
        name="attend_first",
    )(mine, mine)
    return pl.pallas_call(
        second_kernel,
        grid=(tiles,),
        in_specs=[q_spec, own_spec, other_spec, acc_spec],
        out_specs=pl.BlockSpec((TILE_FRAMES, TOK // 2, LANES), lambda i: (i, 0, 0)),
        out_shape=jax.ShapeDtypeStruct((GROUP, TOK // 2, LANES), BF16),
        scratch_shapes=scratch,
        compiler_params=params,
        cost_estimate=cost,
        name="attend_second",
    )(mine, mine, other, first)


def mix_kernel(at_ref, x_ref, w_ref, slots_ref, counts_ref, owner_ref, me_ref, mixed_ref, send_ref):
    half = TOK // 2
    low = low_half(half)
    top, bottom = [], []
    for i in range(HEADS // 2):
        even, odd = at_ref[2 * i].astype(F32), at_ref[2 * i + 1].astype(F32)
        top.append(jnp.where(low, even, swap(odd)).astype(BF16))
        bottom.append(jnp.where(low, swap(even), odd).astype(BF16))
    att = jnp.concatenate([jnp.concatenate(top, axis=1), jnp.concatenate(bottom, axis=1)], axis=0)
    mixed = (
        x_ref[...].astype(F32) + jnp.dot(att, w_ref[...], preferred_element_type=F32)
    ).astype(BF16)
    mixed_ref[...] = mixed
    me = me_ref[0]
    count = counts_ref[me]
    token = lax.broadcasted_iota(jnp.int32, (TOK, QMAX), 0)
    slot = lax.broadcasted_iota(jnp.int32, (TOK, QMAX), 1)
    chosen = (token == slots_ref[...]) & (slot < count)
    rows = lax.dot_general(
        jnp.where(chosen, 1.0, 0.0).astype(BF16),
        mixed,
        (((0,), (0,)), ((), ())),
        preferred_element_type=F32,
    ).astype(BF16)
    dest = owner_ref[me]
    send_ref[...] = jnp.zeros_like(send_ref)
    send_ref[dest] = rows


def mix(att, x, w_out, slots, counts, owner, me):
    smem = pl.BlockSpec(memory_space=pltpu.SMEM)
    vmem = pl.BlockSpec(memory_space=pltpu.VMEM)
    return pl.pallas_call(
        mix_kernel,
        in_specs=[vmem, vmem, vmem, vmem, smem, smem, smem],
        out_specs=[vmem, vmem],
        out_shape=[
            jax.ShapeDtypeStruct((TOK, D), BF16),
            jax.ShapeDtypeStruct((FRAMES, QMAX, D), BF16),
        ],
        compiler_params=pltpu.CompilerParams(vmem_limit_bytes=32 << 20),
        name="mix",
    )(att, x, w_out, slots, counts, owner, me)


def correlate_kernel(rows_ref, mixed_ref, o_ref):
    rows = rows_ref[...].reshape(-1, D)
    corr = lax.dot_general(rows, mixed_ref[...], NT, preferred_element_type=F32)
    o_ref[...] = (corr * (1.0 / D**0.5)).reshape(o_ref.shape)


def correlate(arrived, mixed):
    step = 8
    return pl.pallas_call(
        correlate_kernel,
        grid=(FRAMES // step,),
        in_specs=[
            pl.BlockSpec((step, QMAX, D), lambda i: (i, 0, 0)),
            pl.BlockSpec((TOK, D), lambda i: (0, 0)),
        ],
        out_specs=pl.BlockSpec((1, step, QMAX, TOK), lambda i: (0, i, 0, 0)),
        out_shape=jax.ShapeDtypeStruct((1, FRAMES, QMAX, TOK), F32),
        name="correlate",
    )(arrived, mixed)


def per_device(features, norm_gain, w_qkv, w_out, counts, query_index, owner):
    groups = [[2 * i + side for i in range(GROUP)] for side in range(2)]
    packed = project(features, norm_gain, w_qkv)
    mine = lax.all_to_all(packed, "frame", 0, 0, tiled=True, axis_index_groups=groups)
    other = lax.ppermute(mine[:, :TOK], "frame", [(d, d ^ 1) for d in range(FRAMES)])
    out = attend(mine, other)
    att = lax.all_to_all(out, "frame", 0, 0, tiled=True, axis_index_groups=groups)
    me = lax.axis_index("frame").astype(jnp.int32).reshape(1)
    mixed, send = mix(att, features, w_out, query_index, counts, owner, me)
    arrived = lax.all_to_all(send, "frame", 0, 0, tiled=True)
    return mixed, correlate(arrived, mixed)


def solution(mesh):
    rows = P(("scene", "frame"), None)
    in_specs = (rows, P(), P(), P(), P("scene"), rows, P("scene"))
    out_specs = (rows, P(("scene", "frame"), None, None, None))
    return jax.shard_map(
        per_device, mesh=mesh, in_specs=in_specs, out_specs=out_specs, check_vma=False
    )
```

time: 749 us -> 238 us (0.32)
  waiting for transfers between devices: 331 us -> 10.1 us
  matrix products: 195 us -> 0 us
  other arithmetic: 102 us -> 0 us
  starting transfers between devices: 0.08 us -> 98.8 us
  local copies, waits for them, and re-layouts: 102 us -> 5.58 us
  blocking collectives: 0 us -> 62.6 us
  Pallas kernels: 0 us -> 60.3 us
  between operations: 14.2 us -> 0.72 us
    all_gather x2 -> x0, waiting for transfers between devices: 331 us -> none  [the longest x1 262 us: per_device(): lax.all_gather(jnp.stack([keys, values]), 'frame', axis=1, tiled=True)]
    dot_general x67 -> x0, matrix products: 195 us -> none  [the longest x32 97.1 us: absorb(): jnp.einsum('hts,shd->htd', weights.astype(jnp.bfloat16), vpart.reshape(co...]
    reduce_sum x34 -> x0, other arithmetic: 96 us -> none  [the longest x32 93.3 us: absorb(): total = total * factor + jnp.sum(weights, axis=-1)]
    all_to_all x0 -> x1, starting transfers between devices: none -> 95.7 us  [per_device(): lax.all_to_all(out, 'frame', 0, 0, tiled=True, axis_index_groups=groups)]
    all_to_all x0 -> x2, blocking collectives: none -> 62.6 us  [the longest x1 32.1 us: per_device(): arrived = lax.all_to_all(send, 'frame', 0, 0, tiled=True)]
    pallas_call x0 -> x5, Pallas kernels: none -> 60.3 us  [the longest x1 27.7 us: attend(): pl.pallas_call(first_kernel, grid=(tiles,), in_specs=[q_spec, own_spec],...]
    reshape x1 -> x0, local copies, waits for them, and re-layouts: 44.2 us -> none  [per_device(): stacked = joined.reshape(2, frames, tok, D)]
    slice x32 -> x1, local copies, waits for them, and re-layouts: 40.6 us -> 0.09 us  [per_device(): mine[:, :TOK]]
  transfers between devices with their start and end apart: 2 -> 2, of which waited for: 2 -> 1; matrix products, arithmetic and copies ran while one was open for 0% -> 0% of each run, Pallas kernels for 0% -> 12%
where the time goes in v1:
time: 238 us
  starting transfers between devices  98.8 us (42%)
  blocking collectives  62.6 us (26%)
  Pallas kernels  60.3 us (25%)
  waiting for transfers between devices  10.1 us (4%)
  local copies, waits for them, and re-layouts  5.58 us (2%)
    all_to_all x1, starting transfers between devices, per_device(): lax.all_to_all(out, 'frame', 0, 0, tiled=True, axis_index_groups=groups)  95.7 us
    all_to_all x1, blocking collectives, per_device(): arrived = lax.all_to_all(send, 'frame', 0, 0, tiled=True)  32.1 us
    all_to_all x1, blocking collectives, per_device(): lax.all_to_all(packed, 'frame', 0, 0, tiled=True, axis_index_groups=groups)  30.5 us
    pallas_call x1, Pallas kernels, attend(): pl.pallas_call(first_kernel, grid=(tiles,), in_specs=[q_spec, own_spec],...  27.7 us
    pallas_call x1, Pallas kernels, attend(): pl.pallas_call(second_kernel, grid=(tiles,), in_specs=[q_spec, own_spec,...  22.1 us
    all_to_all x1, waiting for transfers between devices, per_device(): lax.all_to_all(out, 'frame', 0, 0, tiled=True, axis_index_groups=groups)  10.1 us
    unnamed x20, local copies, waits for them, and re-layouts  5.49 us
  transfers between devices with their start and end apart: 2, of which 1 were waited for; matrix products, arithmetic and copies ran while one was open for 0% of the time, Pallas kernels for 12%

profile of v1, /device:TPU:0, one launch (start us, length us, event | category | flops | bytes accessed | tf_op | source)
XLA Modules:
  0.0 238.0 jit_solution(2152918404328448063)
XLA Ops:
  0.6 0.0 copy-start
  0.6 2.8 %copy-done = bf16[1024,3072]{1,0:T(8,128)(2,1)S(1)} copy-done((bf16[1024,3072]{1,0:T(8,128)(2,1)S(1)}, bf16[1024,3072]{1,0:T(8,128)(2,1)}, u32[]{:S(2)}) %copy-start) | copy-done | bytes 6291480
  3.4 1.0 copy-done.2
  4.5 0.7 copy-done.4
  5.1 3.9 %project.1 = bf16[16,384,128]{2,1,0:T(8,128)(2,1)S(1)} custom-call(bf16[256,1024]{1,0:T(8,128)(2,1)S(1)} %copy-done.2, f32[1,1024]{1,0:T(1,128)S(1)} %bitcast.2, bf16[1024,3072]{1,0:T(8,128)(2,1)S(1)} %copy-done, bf16[1024,3072]{1,0:T(8,128)(2,1)S(1)} %copy-done, bf16[1024,3072]{1,0:T(8,128)(2,1)S(1)} %copy-done), custom_call_target="tpu_custom_call" | custom-call | tf_op jit(solution)/shard_map/project/pallas_call | solution.py:61
  9.1 30.5 %all_to_all.15.q_ref.kv_ref = bf16[16,384,128]{2,1,0:T(8,128)(2,1)S(1)} all-to-all(bf16[16,384,128]{2,1,0:T(8,128)(2,1)S(1)} %project.1), channel_id=1, replica_groups={{0,2,4,6,8,10,12,14,16,18,20,22,24,26,28,30},{1,3,5,7,9,11,13,15,17,19,..., dimensions={0} | all-to-all | bytes 3145728 | tf_op jit(solution)/shard_map/all_to_all | solution.py:270
  39.6 0.1 slice.4
  39.6 3.1 %collective-permute-start = (bf16[16,256,128]{2,1,0:T(8,128)(2,1)S(1)}, bf16[16,256,128]{2,1,0:T(8,128)(2,1)S(1)}, u32[]{:S(2)}, u32[]{:S(2)}) collective-permute-start(bf16[16,256,128]{2,1,0:T(8,128)(2,1)S(1)} %slice.4), channel_id=1, source_target_pairs={{0,1},{1,0},{2,3},{3,2},{4,5},{5,4},{6,7},{7,6},{8,9},{9,8},{10,11... | collective-permute-start | bytes 3145736 | tf_op jit(solution)/shard_map/ppermute | solution.py:271
  42.8 0.0 copy-done.8
  42.8 27.7 %attend_first.1.first_ref = f32[4096,128]{1,0:T(8,128)} custom-call(bf16[16,384,128]{2,1,0:T(8,128)(2,1)} %copy-done.8, bf16[16,384,128]{2,1,0:T(8,128)(2,1)} %copy-done.8), custom_call_target="tpu_custom_call" | custom-call | flops 17179869184 | bytes 8388608 | tf_op jit(solution)/shard_map/attend_first/pallas_call | solution.py:177
  70.5 0.0 copy-start.7
  70.5 0.0 collective-permute-done.kv2_ref
  70.5 0.0 copy-start.9
  70.5 1.0 copy-done.9
  71.5 22.1 %attend_second.1 = bf16[16,128,128]{2,1,0:T(8,128)(2,1)} custom-call(bf16[16,384,128]{2,1,0:T(8,128)(2,1)} %copy-done.8, bf16[16,384,128]{2,1,0:T(8,128)(2,1)} %copy-done.8, bf16[16,256,128]{2,1,0:T(8,128)(2,1)} %copy-done.9, f32[4096,128]{1,0:T(8,128)} %attend_first.1.first_ref), custom_call_target="tpu_custom_call" | custom-call | flops 17179869184 | bytes 8388608 | tf_op jit(solution)/shard_map/attend_second/pallas_call | solution.py:188
  93.5 95.7 %all-to-all-start.1 = ((bf16[16,128,128]{2,1,0:T(8,128)(2,1)}), bf16[16,128,128]{2,1,0:T(8,128)(2,1)S(1)}, u32[]{:S(2)}, u32[]{:S(2)}) async-start(bf16[16,128,128]{2,1,0:T(8,128)(2,1)} %attend_second.1), calls=%async_computation.1 | async-start | bytes 1048576 | tf_op jit(solution)/shard_map/all_to_all | solution.py:273
  189.2 10.1 %all-to-all-done.1.at_ref = bf16[16,128,128]{2,1,0:T(8,128)(2,1)S(1)} async-done(((bf16[16,128,128]{2,1,0:T(8,128)(2,1)}), bf16[16,128,128]{2,1,0:T(8,128)(2,1)S(1)}, u32[]{:S(2)}, u32[]{:S(2)}) %all-to-all-start.1) | async-done | bytes 524320 | tf_op jit(solution)/shard_map/all_to_all | solution.py:273
  199.3 0.0 copy-done.3
  199.3 0.0 copy-done.5
  199.3 0.0 copy-done.7
  199.3 0.0 copy-done.1
  199.3 2.2 mix.1
  201.5 32.1 %all_to_all.16.rows_ref = bf16[32,32,1024]{2,1,0:T(8,128)(2,1)} all-to-all(bf16[32,32,1024]{2,1,0:T(8,128)(2,1)S(1)} %get-tuple-element.5), channel_id=1, replica_groups=mesh['scene'=4,'frame'=32] {'frame'}, dimensions={0} | all-to-all | bytes 4194304 | tf_op jit(solution)/shard_map/all_to_all | solution.py:276
  233.6 4.4 %correlate.1 = f32[1,32,32,256]{3,2,1,0:T(8,128)} custom-call(bf16[32,32,1024]{2,1,0:T(8,128)(2,1)} %all_to_all.16.rows_ref, bf16[256,1024]{1,0:T(8,128)(2,1)} %get-tuple-element.2.mixed_ref), custom_call_target="tpu_custom_call" | custom-call | tf_op jit(solution)/shard_map/correlate/pallas_call | solution.py:254
  (8 shorter events, 0.0 us)
Async XLA Ops:
  0.6 2.8 %copy-start = (bf16[1024,3072]{1,0:T(8,128)(2,1)S(1)}, bf16[1024,3072]{1,0:T(8,128)(2,1)}, u32[]{:S(2)}) copy-start(bf16[1024,3072]{1,0:T(8,128)(2,1)} %wv_ref.1) | copy-start | bytes 18874372
  3.4 1.0 copy-start.2
  4.5 0.7 copy-start.4
  39.6 3.2 %copy-start.8 = (bf16[16,384,128]{2,1,0:T(8,128)(2,1)}, bf16[16,384,128]{2,1,0:T(8,128)(2,1)S(1)}, u32[]{:S(2)}) copy-start(bf16[16,384,128]{2,1,0:T(8,128)(2,1)S(1)} %all_to_all.15.q_ref.kv_ref) | copy-start | bytes 4718596
  39.6 30.8 %collective-permute-start = (bf16[16,256,128]{2,1,0:T(8,128)(2,1)S(1)}, bf16[16,256,128]{2,1,0:T(8,128)(2,1)S(1)}, u32[]{:S(2)}, u32[]{:S(2)}) collective-permute-start(bf16[16,256,128]{2,1,0:T(8,128)(2,1)S(1)} %slice.4), channel_id=1, source_target_pairs={{0,1},{1,0},{2,3},{3,2},{4,5},{5,4},{6,7},{7,6},{8,9},{9,8},{10,11... | collective-permute-start | bytes 3145736 | tf_op jit(solution)/shard_map/ppermute | solution.py:271
  70.5 128.8 %copy-start.3 = (bf16[256,1024]{1,0:T(8,128)(2,1)S(1)}, bf16[256,1024]{1,0:T(8,128)(2,1)}, u32[]{:S(2)}) copy-start(bf16[256,1024]{1,0:T(8,128)(2,1)} %x_ref.3) | copy-start | bytes 1572868
  70.5 128.8 %copy-start.5 = (s32[1,32]{1,0:T(1,128)S(1)}, s32[1,32]{1,0:T(1,128)}, u32[]{:S(2)}) copy-start(s32[1,32]{1,0:T(1,128)} %slots_ref.1) | copy-start | bytes 388
  70.5 128.8 %copy-start.6 = (s32[32]{0:T(128)S(1)}, s32[32]{0:T(128)}, u32[]{:S(2)}) copy-start(s32[32]{0:T(128)} %counts_ref.1) | copy-start | bytes 388
  70.5 128.8 %copy-start.7 = (s32[32]{0:T(128)S(1)}, s32[32]{0:T(128)}, u32[]{:S(2)}) copy-start(s32[32]{0:T(128)} %owner_ref.1) | copy-start | bytes 388
  70.5 1.0 copy-start.9
  71.5 127.9 %copy-start.1 = (bf16[1024,1024]{1,0:T(8,128)(2,1)S(1)}, bf16[1024,1024]{1,0:T(8,128)(2,1)}, u32[]{:S(2)}) copy-start(bf16[1024,1024]{1,0:T(8,128)(2,1)} %w_ref.1) | copy-start | bytes 6291460
  93.5 105.8 %all-to-all-start.1 = ((bf16[16,128,128]{2,1,0:T(8,128)(2,1)}), bf16[16,128,128]{2,1,0:T(8,128)(2,1)S(1)}, u32[]{:S(2)}, u32[]{:S(2)}) async-start(bf16[16,128,128]{2,1,0:T(8,128)(2,1)} %attend_second.1), calls=%async_computation.1 | async-start | bytes 1048576 | tf_op jit(solution)/shard_map/all_to_all | solution.py:273

commit v2 on v1

--- a/solution.py
+++ b/solution.py
@@ -15,7 +15,6 @@
 QMAX = 32
 LANES = 128
 LOG2E = 1.4426950408889634
-MARGIN = 64.0
 NT = (((1,), (1,)), ((), ()))
 F32 = jnp.float32
 BF16 = jnp.bfloat16
@@ -71,7 +70,7 @@
         out_specs=pl.BlockSpec((HEADS // steps, TOK + TOK // 2, LANES), lambda i: (i, 0, 0)),
         out_shape=jax.ShapeDtypeStruct((HEADS, TOK + TOK // 2, LANES), BF16),
         scratch_shapes=[pltpu.VMEM((TOK, D), BF16)],
-        compiler_params=pltpu.CompilerParams(vmem_limit_bytes=32 << 20),
+        compiler_params=pltpu.CompilerParams(vmem_limit_bytes=60 << 20),
         name="project",
     )(x, gain.reshape(1, D), w_qkv, w_qkv, w_qkv)
 
@@ -105,60 +104,41 @@
             va_ref[j] = with_ones(kv_ref[j, :TOK])
 
 
-def partial_sums(q, ref_point, kv_ref, va_ref):
-    acc = jnp.zeros((q.shape[0], LANES), F32)
-    for j in range(GROUP // BLOCK_FRAMES):
-        s = lax.dot_general(q, kv_block(kv_ref, j, BLOCK_FRAMES), NT, preferred_element_type=F32)
-        p = jnp.exp2(s * LOG2E - ref_point).astype(BF16)
-        acc += jnp.dot(p, kv_block(va_ref, j, BLOCK_FRAMES), preferred_element_type=F32)
-    return acc
+def absorb(q, kv_ref, va_ref, top, acc):
+    def scores(j):
+        block = kv_block(kv_ref, j, BLOCK_FRAMES)
+        return lax.dot_general(q, block, NT, preferred_element_type=F32)
+
+    blocks = GROUP // BLOCK_FRAMES
+    s = scores(0)
+    for j in range(blocks):
+        ahead = scores(j + 1) if j + 1 < blocks else None
+        newtop = jnp.max(s, axis=-1, keepdims=True) * LOG2E
+        if top is not None:
+            newtop = jnp.maximum(top, newtop)
+        p = jnp.exp2(s * LOG2E - newtop).astype(BF16)
+        pv = jnp.dot(p, kv_block(va_ref, j, BLOCK_FRAMES), preferred_element_type=F32)
+        acc = pv if top is None else acc * jnp.exp2(top - newtop) + pv
+        top, s = newtop, ahead
+    return top, acc
 
 
 def first_kernel(q_ref, kv_ref, acc_ref, va_ref):
     fill_values(kv_ref, va_ref)
-    q = load_queries(q_ref)
-    s = lax.dot_general(q, kv_block(kv_ref, 0, 2), NT, preferred_element_type=F32)
-    ref_point = jnp.max(s, axis=-1, keepdims=True) * LOG2E + MARGIN
-    acc = partial_sums(q, ref_point, kv_ref, va_ref)
+    top, acc = absorb(load_queries(q_ref), kv_ref, va_ref, None, None)
     lane = lax.broadcasted_iota(jnp.int32, acc.shape, 1)
-    acc_ref[...] = jnp.where(lane == 1, ref_point, acc)
-
-
-def second_kernel(q_ref, kv_ref, kv2_ref, first_ref, o_ref, va_ref):
-    fill_values(kv2_ref, va_ref)
+    acc_ref[...] = jnp.where(lane == 1, top, acc)
+
+
+def second_kernel(q_ref, kv_ref, first_ref, o_ref, va_ref):
+    fill_values(kv_ref, va_ref)
     q = load_queries(q_ref)
     rows = q.shape[0]
-
-    def store(total):
-        out = total / total[:, :1]
-        packed = jnp.where(low_half(rows // 2), swap(out[: rows // 2]), out[rows // 2 :])
-        o_ref[...] = packed.astype(BF16).reshape(o_ref.shape)
-
-    ref_point = first_ref[:, 1:2]
-    total = first_ref[...] + partial_sums(q, ref_point, kv2_ref, va_ref)
-    sums = total[:, :1]
-    store(total)
-    safe = jnp.min(jnp.where((sums < 2.0**100) & (sums > 2.0**-100), 1.0, 0.0)) > 0.5
-
-    @pl.when(jnp.logical_not(safe))
-    def _():
-        def absorb(ref):
-            def step(j, carry):
-                top, acc = carry
-                kv = ref[j, :TOK]
-                s = lax.dot_general(q, kv, NT, preferred_element_type=F32)
-                newtop = jnp.maximum(top, jnp.max(s, axis=-1, keepdims=True))
-                p = jnp.exp(s - newtop).astype(BF16)
-                acc = acc * jnp.exp(top - newtop)
-                acc += jnp.dot(p, with_ones(kv), preferred_element_type=F32)
-                return newtop, acc
-
-            return step
-
-        start = (jnp.full((rows, 1), -1e30, F32), jnp.zeros((rows, LANES), F32))
-        carry = lax.fori_loop(0, GROUP, absorb(kv_ref), start)
-        top, acc = lax.fori_loop(0, GROUP, absorb(kv2_ref), carry)
-        store(acc)
+    first = first_ref[...]
+    top, acc = absorb(q, kv_ref, va_ref, first[:, 1:2], first)
+    out = acc / acc[:, :1]
+    packed = jnp.where(low_half(rows // 2), swap(out[: rows // 2]), out[rows // 2 :])
+    o_ref[...] = packed.astype(BF16).reshape(o_ref.shape)
 
 
 def attend(mine, other):
@@ -188,14 +168,14 @@
     return pl.pallas_call(
         second_kernel,
         grid=(tiles,),
-        in_specs=[q_spec, own_spec, other_spec, acc_spec],
+        in_specs=[q_spec, other_spec, acc_spec],
         out_specs=pl.BlockSpec((TILE_FRAMES, TOK // 2, LANES), lambda i: (i, 0, 0)),
         out_shape=jax.ShapeDtypeStruct((GROUP, TOK // 2, LANES), BF16),
         scratch_shapes=scratch,
         compiler_params=params,
         cost_estimate=cost,
         name="attend_second",
-    )(mine, mine, other, first)
+    )(mine, other, first)
 
 
 def mix_kernel(at_ref, x_ref, w_ref, slots_ref, counts_ref, owner_ref, me_ref, mixed_ref, send_ref):

time: 238 us -> 144 us (0.61)
  starting transfers between devices: 98.8 us -> 6.95 us
  local copies, waits for them, and re-layouts: 5.58 us -> 1.08 us
    all_to_all x1, starting transfers between devices: 95.7 us -> 3.85 us  [per_device(): lax.all_to_all(out, 'frame', 0, 0, tiled=True, axis_index_groups=groups)]
    pallas_call x1, Pallas kernels: 27.7 us -> 22.6 us  [attend(): pl.pallas_call(first_kernel, grid=(tiles,), in_specs=[q_spec, own_spec],...]
    unnamed x20 -> x14, local copies, waits for them, and re-layouts: 5.49 us -> 0.99 us
    pallas_call x1, Pallas kernels: 22.1 us -> 25.6 us  [attend(): pl.pallas_call(second_kernel, grid=(tiles,), in_specs=[q_spec, other_spec...]
    pallas_call x1, Pallas kernels: 3.91 us -> 6.54 us  [project(): pl.pallas_call(project_kernel, grid=(steps,), in_specs=[pl.BlockSpec((TOK...]
  transfers between devices with their start and end apart: 2 -> 2, of which waited for: 1 -> 1; matrix products, arithmetic and copies ran while one was open for 0% -> 0% of each run, Pallas kernels for 12% -> 16%
where the time goes in v2:
time: 144 us
  blocking collectives  63.8 us (44%)
  Pallas kernels  61.3 us (43%)
  waiting for transfers between devices  10.1 us (7%)
  starting transfers between devices  6.95 us (5%)
    all_to_all x1, blocking collectives, per_device(): arrived = lax.all_to_all(send, 'frame', 0, 0, tiled=True)  33.1 us
    all_to_all x1, blocking collectives, per_device(): lax.all_to_all(packed, 'frame', 0, 0, tiled=True, axis_index_groups=groups)  30.7 us
    pallas_call x1, Pallas kernels, attend(): pl.pallas_call(second_kernel, grid=(tiles,), in_specs=[q_spec, other_spec...  25.6 us
    pallas_call x1, Pallas kernels, attend(): pl.pallas_call(first_kernel, grid=(tiles,), in_specs=[q_spec, own_spec],...  22.6 us
    all_to_all x1, waiting for transfers between devices, per_device(): lax.all_to_all(out, 'frame', 0, 0, tiled=True, axis_index_groups=groups)  10.1 us
    pallas_call x1, Pallas kernels, project(): pl.pallas_call(project_kernel, grid=(steps,), in_specs=[pl.BlockSpec((TOK...  6.54 us
    pallas_call x1, Pallas kernels, correlate(): pl.pallas_call(correlate_kernel, grid=(FRAMES // step,), in_specs=[pl.Blo...  4.35 us
    all_to_all x1, starting transfers between devices, per_device(): lax.all_to_all(out, 'frame', 0, 0, tiled=True, axis_index_groups=groups)  3.85 us
  transfers between devices with their start and end apart: 2, of which 1 were waited for; matrix products, arithmetic and copies ran while one was open for 0% of the time, Pallas kernels for 16%

profile of v2, /device:TPU:0, one launch (start us, length us, event | category | flops | bytes accessed | tf_op | source)
XLA Modules:
  0.0 143.9 jit_solution(5539282698482110422)
XLA Ops:
  0.6 6.5 %project.1 = bf16[16,384,128]{2,1,0:T(8,128)(2,1)} custom-call(bf16[256,1024]{1,0:T(8,128)(2,1)} %x_ref.3, f32[1,1024]{1,0:T(1,128)} %bitcast.2, bf16[1024,3072]{1,0:T(8,128)(2,1)} %wv_ref.1, bf16[1024,3072]{1,0:T(8,128)(2,1)} %wv_ref.1, bf16[1024,3072]{1,0:T(8,128)(2,1)} %wv_ref.1), custom_call_target="tpu_custom_call" | custom-call | tf_op jit(solution)/shard_map/project/pallas_call | solution.py:60
  7.2 30.7 %all_to_all.15.q_ref.kv_ref = bf16[16,384,128]{2,1,0:T(8,128)(2,1)S(1)} all-to-all(bf16[16,384,128]{2,1,0:T(8,128)(2,1)} %project.1), channel_id=1, replica_groups={{0,2,4,6,8,10,12,14,16,18,20,22,24,26,28,30},{1,3,5,7,9,11,13,15,17,19,..., dimensions={0} | all-to-all | bytes 3145728 | tf_op jit(solution)/shard_map/all_to_all | solution.py:250
  37.9 0.0 copy-start.5
  37.9 0.1 slice.4
  38.0 3.1 %collective-permute-start = (bf16[16,256,128]{2,1,0:T(8,128)(2,1)S(1)}, bf16[16,256,128]{2,1,0:T(8,128)(2,1)S(1)}, u32[]{:S(2)}, u32[]{:S(2)}) collective-permute-start(bf16[16,256,128]{2,1,0:T(8,128)(2,1)S(1)} %slice.4), channel_id=1, source_target_pairs={{0,1},{1,0},{2,3},{3,2},{4,5},{5,4},{6,7},{7,6},{8,9},{9,8},{10,11... | collective-permute-start | bytes 3145736 | tf_op jit(solution)/shard_map/ppermute | solution.py:251
  41.1 0.0 copy-done.5
  41.1 22.6 %attend_first.1.first_ref = f32[4096,128]{1,0:T(8,128)} custom-call(bf16[16,384,128]{2,1,0:T(8,128)(2,1)} %copy-done.5, bf16[16,384,128]{2,1,0:T(8,128)(2,1)} %copy-done.5), custom_call_target="tpu_custom_call" | custom-call | flops 17179869184 | bytes 8388608 | tf_op jit(solution)/shard_map/attend_first/pallas_call | solution.py:157
  63.6 0.0 copy-start.1
  63.6 0.0 copy-start.2
  63.7 0.0 copy-start.4
  63.7 0.0 collective-permute-done.kv_ref
  63.7 0.0 copy-start.6
  63.7 1.0 copy-done.6
  64.7 25.6 %attend_second.1 = bf16[16,128,128]{2,1,0:T(8,128)(2,1)} custom-call(bf16[16,384,128]{2,1,0:T(8,128)(2,1)} %copy-done.5, bf16[16,256,128]{2,1,0:T(8,128)(2,1)} %copy-done.6, f32[4096,128]{1,0:T(8,128)} %attend_first.1.first_ref), custom_call_target="tpu_custom_call" | custom-call | flops 17179869184 | bytes 8388608 | tf_op jit(solution)/shard_map/attend_second/pallas_call | solution.py:168
  90.2 3.8 %all-to-all-start.1 = ((bf16[16,128,128]{2,1,0:T(8,128)(2,1)}), bf16[16,128,128]{2,1,0:T(8,128)(2,1)S(1)}, u32[]{:S(2)}, u32[]{:S(2)}) async-start(bf16[16,128,128]{2,1,0:T(8,128)(2,1)} %attend_second.1), calls=%async_computation.1 | async-start | bytes 1048576 | tf_op jit(solution)/shard_map/all_to_all | solution.py:253
  94.1 10.1 %all-to-all-done.1.at_ref = bf16[16,128,128]{2,1,0:T(8,128)(2,1)S(1)} async-done(((bf16[16,128,128]{2,1,0:T(8,128)(2,1)}), bf16[16,128,128]{2,1,0:T(8,128)(2,1)S(1)}, u32[]{:S(2)}, u32[]{:S(2)}) %all-to-all-start.1) | async-done | bytes 524320 | tf_op jit(solution)/shard_map/all_to_all | solution.py:253
  104.2 0.0 copy-done.1
  104.2 0.0 copy-done.2
  104.2 0.0 copy-done.3
  104.2 0.0 copy-done.4
  104.2 0.0 copy-done
  104.2 2.2 %mix.1 = (bf16[256,1024]{1,0:T(8,128)(2,1)}, bf16[32,32,1024]{2,1,0:T(8,128)(2,1)S(1)}) custom-call(bf16[16,128,128]{2,1,0:T(8,128)(2,1)S(1)} %all-to-all-done.1.at_ref, bf16[256,1024]{1,0:T(8,128)(2,1)S(1)} %copy-done.1, bf16[1024,1024]{1,0:T(8,128)(2,1)S(1)} %copy-done, s32[1,32]{1,0:T(1,128)S(1)} %copy-done.2, s32[32]{0:T(128)S(1)} %copy-done.3, ...), custom_call_target="tpu_custom_call" | custom-call | tf_op jit(solution)/shard_map/mix/pallas_call | solution.py:213
  106.4 33.1 %all_to_all.16.rows_ref = bf16[32,32,1024]{2,1,0:T(8,128)(2,1)} all-to-all(bf16[32,32,1024]{2,1,0:T(8,128)(2,1)S(1)} %get-tuple-element.5), channel_id=1, replica_groups=mesh['scene'=4,'frame'=32] {'frame'}, dimensions={0} | all-to-all | bytes 4194304 | tf_op jit(solution)/shard_map/all_to_all | solution.py:256
  139.5 4.4 %correlate.1 = f32[1,32,32,256]{3,2,1,0:T(8,128)} custom-call(bf16[32,32,1024]{2,1,0:T(8,128)(2,1)} %all_to_all.16.rows_ref, bf16[256,1024]{1,0:T(8,128)(2,1)} %get-tuple-element.2.mixed_ref), custom_call_target="tpu_custom_call" | custom-call | tf_op jit(solution)/shard_map/correlate/pallas_call | solution.py:234
  (2 shorter events, 0.0 us)
Async XLA Ops:
  37.9 3.2 %copy-start.5 = (bf16[16,384,128]{2,1,0:T(8,128)(2,1)}, bf16[16,384,128]{2,1,0:T(8,128)(2,1)S(1)}, u32[]{:S(2)}) copy-start(bf16[16,384,128]{2,1,0:T(8,128)(2,1)S(1)} %all_to_all.15.q_ref.kv_ref) | copy-start | bytes 4718596
  38.0 25.7 %collective-permute-start = (bf16[16,256,128]{2,1,0:T(8,128)(2,1)S(1)}, bf16[16,256,128]{2,1,0:T(8,128)(2,1)S(1)}, u32[]{:S(2)}, u32[]{:S(2)}) collective-permute-start(bf16[16,256,128]{2,1,0:T(8,128)(2,1)S(1)} %slice.4), channel_id=1, source_target_pairs={{0,1},{1,0},{2,3},{3,2},{4,5},{5,4},{6,7},{7,6},{8,9},{9,8},{10,11... | collective-permute-start | bytes 3145736 | tf_op jit(solution)/shard_map/ppermute | solution.py:251
  63.6 40.5 %copy-start.1 = (bf16[256,1024]{1,0:T(8,128)(2,1)S(1)}, bf16[256,1024]{1,0:T(8,128)(2,1)}, u32[]{:S(2)}) copy-start(bf16[256,1024]{1,0:T(8,128)(2,1)} %x_ref.3) | copy-start | bytes 1572868
  63.6 40.5 %copy-start.2 = (s32[1,32]{1,0:T(1,128)S(1)}, s32[1,32]{1,0:T(1,128)}, u32[]{:S(2)}) copy-start(s32[1,32]{1,0:T(1,128)} %slots_ref.1) | copy-start | bytes 388
  63.6 40.5 %copy-start.3 = (s32[32]{0:T(128)S(1)}, s32[32]{0:T(128)}, u32[]{:S(2)}) copy-start(s32[32]{0:T(128)} %counts_ref.1) | copy-start | bytes 388
  63.7 40.5 %copy-start.4 = (s32[32]{0:T(128)S(1)}, s32[32]{0:T(128)}, u32[]{:S(2)}) copy-start(s32[32]{0:T(128)} %owner_ref.1) | copy-start | bytes 388
  63.7 1.0 copy-start.6
  64.6 39.6 %copy-start = (bf16[1024,1024]{1,0:T(8,128)(2,1)S(1)}, bf16[1024,1024]{1,0:T(8,128)(2,1)}, u32[]{:S(2)}) copy-start(bf16[1024,1024]{1,0:T(8,128)(2,1)} %w_ref.1) | copy-start | bytes 6291460
  90.2 14.0 %all-to-all-start.1 = ((bf16[16,128,128]{2,1,0:T(8,128)(2,1)}), bf16[16,128,128]{2,1,0:T(8,128)(2,1)S(1)}, u32[]{:S(2)}, u32[]{:S(2)}) async-start(bf16[16,128,128]{2,1,0:T(8,128)(2,1)} %attend_second.1), calls=%async_computation.1 | async-start | bytes 1048576 | tf_op jit(solution)/shard_map/all_to_all | solution.py:253

commit v3 on v2

v3 whole, which is shorter than its diff:
```python
import functools

import jax
import jax.numpy as jnp
from jax import lax
from jax.experimental import pallas as pl
from jax.experimental.pallas import tpu as pltpu
from jax.sharding import PartitionSpec as P

D = 1024
HEADS = 16
HDIM = 64
TOK = 256
FRAMES = 32
QMAX = 32
LANES = 128
LOG2E = 1.4426950408889634
NT = (((1,), (1,)), ((), ()))
TN = (((0,), (0,)), ((), ()))
CHUNK = 16
F32 = jnp.float32
BF16 = jnp.bfloat16


def low_half(rows):
    return lax.broadcasted_iota(jnp.int32, (rows, LANES), 1) < HDIM


def swap(x):
    return pltpu.roll(x, HDIM, 1)


def slot_of_token(slots):
    return lax.broadcasted_iota(jnp.int32, (TOK, QMAX), 0) == slots


def arrange(slots):
    picked = jnp.max(jnp.where(slot_of_token(slots), 1.0, 0.0), axis=1, keepdims=True)
    row = lax.broadcasted_iota(jnp.int32, (TOK, TOK), 0)
    col = lax.broadcasted_iota(jnp.int32, (TOK, TOK), 1)
    wide = jnp.broadcast_to(picked, (TOK, LANES)).astype(BF16)
    before = jnp.dot(jnp.where(col < row, 1.0, 0.0).astype(BF16), wide, preferred_element_type=F32)
    before = before[:, :1].astype(jnp.int32)
    total = jnp.sum(picked).astype(jnp.int32)
    token = lax.broadcasted_iota(jnp.int32, (TOK, 1), 0)
    rank = jnp.where(picked > 0.5, before, total + token - before)
    within = rank & 31
    place = (rank >> 5) * CHUNK + (within & 15) + jnp.where(within >= CHUNK, TOK // 2, 0)
    return jnp.where(place == col, 1.0, 0.0).astype(BF16)


def project_kernel(x_ref, g_ref, slots_ref, wq_ref, wk_ref, wv_ref, o_ref, place_ref, n_ref):
    @pl.when(pl.program_id(0) == 0)
    def _():
        place = arrange(slots_ref[...])
        place_ref[...] = place
        xf = x_ref[...].astype(F32)
        mean = jnp.mean(xf, axis=-1, keepdims=True)
        cen = xf - mean
        var = jnp.mean(cen * cen, axis=-1, keepdims=True)
        normed = (cen * lax.rsqrt(var + 1e-05) * g_ref[...]).astype(BF16)
        n_ref[...] = lax.dot_general(place, normed, TN, preferred_element_type=F32).astype(BF16)

    n = n_ref[...]
    q = jnp.dot(n, wq_ref[...], preferred_element_type=F32) * (1.0 / HDIM**0.5)
    k = jnp.dot(n, wk_ref[...], preferred_element_type=F32)
    v = jnp.dot(n, wv_ref[...], preferred_element_type=F32)
    half = TOK // 2
    low = low_half(TOK)
    lowh = low_half(half)
    for c in range(wq_ref.shape[1] // LANES):
        cols = slice(c * LANES, (c + 1) * LANES)
        kp, vp = k[:, cols], v[:, cols]
        qa, qb = q[:half, cols], q[half:, cols]
        o_ref[2 * c, :TOK] = jnp.where(low, kp, swap(vp)).astype(BF16)
        o_ref[2 * c + 1, :TOK] = jnp.where(low, swap(kp), vp).astype(BF16)
        o_ref[2 * c, TOK:] = jnp.where(lowh, qa, swap(qb)).astype(BF16)
        o_ref[2 * c + 1, TOK:] = jnp.where(lowh, swap(qa), qb).astype(BF16)


def project(x, gain, slots, w_qkv):
    steps = 4
    width = D // steps
    return pl.pallas_call(
        project_kernel,
        grid=(steps,),
        in_specs=[
            pl.BlockSpec((TOK, D), lambda i: (0, 0)),
            pl.BlockSpec((1, D), lambda i: (0, 0)),
            pl.BlockSpec((1, QMAX), lambda i: (0, 0)),
            pl.BlockSpec((D, width), lambda i: (0, i)),
            pl.BlockSpec((D, width), lambda i: (0, i + steps)),
            pl.BlockSpec((D, width), lambda i: (0, i + 2 * steps)),
        ],
        out_specs=[
            pl.BlockSpec((HEADS // steps, TOK + TOK // 2, LANES), lambda i: (i, 0, 0)),
            pl.BlockSpec((TOK, TOK), lambda i: (0, 0)),
        ],
        out_shape=[
            jax.ShapeDtypeStruct((HEADS, TOK + TOK // 2, LANES), BF16),
            jax.ShapeDtypeStruct((TOK, TOK), BF16),
        ],
        scratch_shapes=[pltpu.VMEM((TOK, D), BF16)],
        compiler_params=pltpu.CompilerParams(vmem_limit_bytes=60 << 20),
        name="project",
    )(x, gain.reshape(1, D), slots, w_qkv, w_qkv, w_qkv)


BLOCK_FRAMES = 4
GROUP = FRAMES // 2
CHUNKS = TOK // (2 * CHUNK)
ROWS = GROUP * 2 * CHUNK
SPLIT = 6


def unpack_queries(packed):
    packed = packed.reshape(GROUP * CHUNK, LANES).astype(F32)
    low = low_half(packed.shape[0])
    zero = jnp.zeros_like(packed)
    both = [jnp.where(low, packed, zero), jnp.where(low, swap(packed), zero)]
    return jnp.concatenate(both, axis=0).astype(BF16)


def load_queries(mine_ref, chunk):
    start = pl.multiple_of(TOK + chunk * CHUNK, CHUNK)
    return unpack_queries(mine_ref[:, pl.ds(start, CHUNK), :])


def kv_block(kv_ref, j, count):
    return kv_ref[pl.ds(j * count, count), :TOK].reshape(count * TOK, LANES)


def fill_values(kv_ref, va_ref):
    @pl.when(pl.program_id(0) == 0)
    def _():
        for j in range(GROUP):
            kv = kv_ref[j, :TOK]
            va_ref[j] = jnp.where(low_half(TOK), jnp.ones_like(kv), kv)


def absorb(q, kv_ref, va_ref, top, acc):
    def scores(j):
        block = kv_block(kv_ref, j, BLOCK_FRAMES)
        return lax.dot_general(q, block, NT, preferred_element_type=F32)

    blocks = GROUP // BLOCK_FRAMES
    s = scores(0)
    for j in range(blocks):
        ahead = scores(j + 1) if j + 1 < blocks else None
        newtop = jnp.max(s, axis=-1, keepdims=True) * LOG2E
        if top is not None:
            newtop = jnp.maximum(top, newtop)
        p = jnp.exp2(s * LOG2E - newtop).astype(BF16)
        pv = jnp.dot(p, kv_block(va_ref, j, BLOCK_FRAMES), preferred_element_type=F32)
        acc = pv if top is None else acc * jnp.exp2(top - newtop) + pv
        top, s = newtop, ahead
    return top, acc


def own_kernel(first, mine_ref, *rest):
    state_ref, va_ref = rest[-2:]
    fill_values(mine_ref, va_ref)
    q = load_queries(mine_ref, pl.program_id(0) + first)
    top, acc = absorb(q, mine_ref, va_ref, None, None)
    lane = lax.broadcasted_iota(jnp.int32, acc.shape, 1)
    state_ref[...] = jnp.where(lane == 1, top, acc)


def other_kernel(starts, mine_ref, other_ref, *rest):
    state_refs = rest[: len(starts)]
    o_ref, va_ref = rest[-2:]
    fill_values(other_ref, va_ref)
    chunk = pl.program_id(0) + starts[0]
    q = load_queries(mine_ref, chunk)
    state = state_refs[0][...]
    for start, ref in zip(starts[1:], state_refs[1:], strict=True):
        state = jnp.where(chunk >= start, ref[...], state)
    top, acc = absorb(q, other_ref, va_ref, state[:, 1:2], state)
    out = acc / acc[:, :1]
    packed = jnp.where(low_half(ROWS // 2), swap(out[: ROWS // 2]), out[ROWS // 2 :])
    o_ref[...] = packed.astype(BF16).reshape(o_ref.shape)


def picks_kernel(mine_ref, picks_ref, me_ref, *rest):
    o_ref, va_ref = rest[-2:]
    fill_values(mine_ref, va_ref)
    step = pl.program_id(0)
    own = mine_ref[:, TOK : TOK + CHUNK, :]
    q = unpack_queries(jnp.where(step == 0, own, picks_ref[...]))
    top, acc = absorb(q, mine_ref, va_ref, None, None)
    sums = acc[:, :1]
    mean = acc / sums
    level = top + jnp.log2(sums)
    part0 = level.astype(BF16).astype(F32)
    part1 = (level - part0).astype(BF16).astype(F32)
    part2 = level - part0 - part1
    lane = lax.broadcasted_iota(jnp.int32, acc.shape, 1)
    low = jnp.where(lane == 0, part0, jnp.where(lane == 1, part1, part2))
    out = jnp.where(lane < HDIM, low, mean).astype(BF16).reshape(2, GROUP, CHUNK, LANES)
    side = me_ref[0] & 1
    side = jnp.where(step == 0, side, 1 - side)
    for half in range(2):
        o_ref[:, side, half * CHUNK : (half + 1) * CHUNK] = out[half]


VMEM = pl.BlockSpec(memory_space=pltpu.VMEM)
SMEM = pl.BlockSpec(memory_space=pltpu.SMEM)


def attend_settings(chunks):
    pairs = chunks * ROWS * GROUP * TOK
    return dict(
        grid=(chunks,),
        scratch_shapes=[pltpu.VMEM((GROUP, TOK, LANES), BF16)],
        compiler_params=pltpu.CompilerParams(vmem_limit_bytes=36 << 20),
        cost_estimate=pl.CostEstimate(
            flops=2 * pairs * LANES * 4, bytes_accessed=1 << 20, transcendentals=pairs
        ),
    )


ANY = pl.BlockSpec(memory_space=pl.ANY)


def attend_own(mine, first, last, after=()):
    return pl.pallas_call(
        functools.partial(own_kernel, first),
        in_specs=[VMEM] + [ANY] * len(after),
        out_specs=pl.BlockSpec((ROWS, LANES), lambda i: (i, 0)),
        out_shape=jax.ShapeDtypeStruct(((last - first) * ROWS, LANES), F32),
        name=f"attend_own_{first}",
        **attend_settings(last - first),
    )(mine, *after)


def attend_picks(mine, picks, me, after):
    return pl.pallas_call(
        picks_kernel,
        in_specs=[VMEM, VMEM, SMEM] + [ANY] * len(after),
        out_specs=VMEM,
        out_shape=jax.ShapeDtypeStruct((GROUP, 2, QMAX, LANES), BF16),
        name="attend_picks",
        **attend_settings(2),
    )(mine, picks, me, *after)


def attend_other(mine, other, states, after=()):
    counts = [state.shape[0] // ROWS for state in states]
    chunks = sum(counts)
    starts = [CHUNKS - sum(counts[i:]) for i in range(len(counts))]

    def state_spec(start, count):
        shift = start - starts[0]
        return pl.BlockSpec((ROWS, LANES), lambda i: (jnp.clip(i - shift, 0, count - 1), 0))

    return pl.pallas_call(
        functools.partial(other_kernel, starts),
        in_specs=[VMEM, VMEM]
        + [state_spec(*pair) for pair in zip(starts, counts, strict=True)]
        + [ANY] * len(after),
        out_specs=pl.BlockSpec((GROUP, CHUNK, LANES), lambda i: (0, i, 0)),
        out_shape=jax.ShapeDtypeStruct((GROUP, chunks * CHUNK, LANES), BF16),
        name="attend_other",
        **attend_settings(chunks),
    )(mine, other, *states, *after)


def join_heads(even_odd):
    top, bottom = [], []
    for even, odd in even_odd:
        low = low_half(even.shape[0])
        top.append(jnp.where(low, even, swap(odd)).astype(BF16))
        bottom.append(jnp.where(low, swap(even), odd).astype(BF16))
    return jnp.concatenate(top, axis=1), jnp.concatenate(bottom, axis=1)


def level_of(part):
    return part[:, 0:1] + part[:, 1:2] + part[:, 2:3]


def rows_kernel(part_ref, x_ref, w_ref, place_ref, slots_ref, counts_ref, owner_ref, me_ref, *rest):
    send_ref, att_ref = rest[-2:]
    heads = []
    for h in range(HEADS):
        a, b = part_ref[2 * h].astype(F32), part_ref[2 * h + 1].astype(F32)
        la, lb = level_of(a), level_of(b)
        most = jnp.maximum(la, lb)
        wa, wb = jnp.exp2(la - most), jnp.exp2(lb - most)
        heads.append((a * wa + b * wb) / (wa + wb))
    att = jnp.concatenate(
        [
            jnp.where(low_half(QMAX), swap(heads[2 * i]), heads[2 * i + 1]).astype(BF16)
            for i in range(HEADS // 2)
        ],
        axis=1,
    )
    att_ref[...] = att
    gap = jnp.zeros((TOK // 2 - CHUNK, D), BF16)
    placed = jnp.concatenate([att[:CHUNK], gap, att[CHUNK:], gap], axis=0)
    token_slot = jnp.where(slot_of_token(slots_ref[...]), 1.0, 0.0).astype(BF16)
    where = lax.dot_general(token_slot, place_ref[...], TN, preferred_element_type=F32).astype(BF16)
    chosen = jnp.dot(where, placed, preferred_element_type=F32).astype(BF16)
    x = lax.dot_general(token_slot, x_ref[...], TN, preferred_element_type=F32)
    rows = (x + jnp.dot(chosen, w_ref[...], preferred_element_type=F32)).astype(BF16)
    me = me_ref[0]
    slot = lax.broadcasted_iota(jnp.int32, rows.shape, 0)
    send_ref[...] = jnp.zeros_like(send_ref)
    send_ref[owner_ref[me]] = jnp.where(slot < counts_ref[me], rows, jnp.zeros_like(rows))


def track_rows(parts, x, w_out, place, slots, counts, owner, me, after):
    return pl.pallas_call(
        rows_kernel,
        in_specs=[VMEM] * 5 + [SMEM] * 3 + [ANY] * len(after),
        out_specs=[VMEM, VMEM],
        out_shape=[
            jax.ShapeDtypeStruct((FRAMES, QMAX, D), BF16),
            jax.ShapeDtypeStruct((QMAX, D), BF16),
        ],
        compiler_params=pltpu.CompilerParams(vmem_limit_bytes=20 << 20),
        cost_estimate=pl.CostEstimate(flops=2 << 30, bytes_accessed=4 << 20, transcendentals=0),
        name="track_rows",
    )(parts, x, w_out, place, slots, counts, owner, me, *after)


def mix_kernel(att1_ref, at2_ref, x_ref, w_ref, place_ref, mixed_ref):
    pairs = [(at2_ref[2 * i].astype(F32), at2_ref[2 * i + 1].astype(F32)) for i in range(HEADS // 2)]
    top, bottom = join_heads(pairs)
    placed = jnp.concatenate([att1_ref[:CHUNK], top, att1_ref[CHUNK:], bottom], axis=0)
    att = jnp.dot(place_ref[...], placed, preferred_element_type=F32).astype(BF16)
    mixed_ref[...] = (
        x_ref[...].astype(F32) + jnp.dot(att, w_ref[...], preferred_element_type=F32)
    ).astype(BF16)


def mix(att1, att2, x, w_out, place):
    return pl.pallas_call(
        mix_kernel,
        in_specs=[VMEM] * 5,
        out_specs=VMEM,
        out_shape=jax.ShapeDtypeStruct((TOK, D), BF16),
        compiler_params=pltpu.CompilerParams(vmem_limit_bytes=20 << 20),
        name="mix",
    )(att1, att2, x, w_out, place)


def correlate_kernel(rows_ref, mixed_ref, o_ref):
    step = o_ref.shape[1]
    start = pl.program_id(0) * step
    rows = rows_ref[pl.ds(start, step)].reshape(-1, D)
    corr = lax.dot_general(rows, mixed_ref[...], NT, preferred_element_type=F32)
    o_ref[...] = (corr * (1.0 / D**0.5)).reshape(o_ref.shape)


def correlate(arrived, mixed):
    step = 8
    return pl.pallas_call(
        correlate_kernel,
        grid=(FRAMES // step,),
        in_specs=[VMEM, VMEM],
        out_specs=pl.BlockSpec((1, step, QMAX, TOK), lambda i: (0, i, 0, 0)),
        out_shape=jax.ShapeDtypeStruct((1, FRAMES, QMAX, TOK), F32),
        compiler_params=pltpu.CompilerParams(vmem_limit_bytes=20 << 20),
        name="correlate",
    )(arrived, mixed)


def per_device(features, norm_gain, w_qkv, w_out, counts, query_index, owner):
    groups = [[2 * i + side for i in range(GROUP)] for side in range(2)]
    swap_sides = [(d, d ^ 1) for d in range(FRAMES)]
    me = lax.axis_index("frame").astype(jnp.int32).reshape(1)
    packed, place = project(features, norm_gain, query_index, w_qkv)
    mine = lax.all_to_all(packed, "frame", 0, 0, tiled=True, axis_index_groups=groups)
    picks = lax.ppermute(mine[:, TOK : TOK + CHUNK], "frame", swap_sides)
    other = lax.ppermute(mine[:, :TOK], "frame", swap_sides)
    state1 = attend_own(mine, 1, 3)
    parts = attend_picks(mine, picks, me, [state1])
    parts_here = lax.all_to_all(
        parts.reshape(FRAMES, QMAX, LANES), "frame", 0, 0, tiled=True
    )
    state2 = attend_own(mine, 3, SPLIT, [parts])
    send, att1 = track_rows(
        parts_here, features, w_out, place, query_index, counts, owner, me, [state2]
    )
    arrived = lax.all_to_all(send, "frame", 0, 0, tiled=True)
    state3 = attend_own(mine, SPLIT, CHUNKS, [att1])
    rest = attend_other(mine, other, [state1, state2, state3])
    rest, arrived = lax.optimization_barrier((rest, arrived))
    att2 = lax.all_to_all(rest, "frame", 0, 0, tiled=True, axis_index_groups=groups)
    mixed = mix(att1, att2, features, w_out, place)
    return mixed, correlate(arrived, mixed)


def solution(mesh):
    rows = P(("scene", "frame"), None)
    in_specs = (rows, P(), P(), P(), P("scene"), rows, P("scene"))
    out_specs = (rows, P(("scene", "frame"), None, None, None))
    return jax.shard_map(
        per_device, mesh=mesh, in_specs=in_specs, out_specs=out_specs, check_vma=False
    )
```

time: 144 us -> 141 us (0.979)
  blocking collectives: 63.8 us -> 16.6 us
  starting transfers between devices: 6.95 us -> 26.3 us
  waiting for transfers between devices: 10.1 us -> 25.6 us
  local copies, waits for them, and re-layouts: 1.08 us -> 10.1 us
    all_to_all x2 -> x1, blocking collectives: 63.8 us -> 16.6 us  [per_device(): lax.all_to_all(rest, 'frame', 0, 0, tiled=True, axis_index_groups=groups)]
    all_to_all x1 -> x3, starting transfers between devices: 3.85 us -> 22.7 us  [the longest x1 8.13 us: per_device(): lax.all_to_all(packed, 'frame', 0, 0, tiled=True, axis_index_groups=groups)]
    all_to_all x1 -> x3, waiting for transfers between devices: 10.1 us -> 25.6 us  [the longest x1 23.8 us: per_device(): lax.all_to_all(packed, 'frame', 0, 0, tiled=True, axis_index_groups=groups)]
    unnamed x14 -> x32, local copies, waits for them, and re-layouts: 0.99 us -> 9.02 us
    pallas_call x4 -> x8, Pallas kernels: 54.7 us -> 53.5 us  [the longest x1 22.6 us: attend_other(): pl.pallas_call(functools.partial(other_kernel, starts), in_specs=[VMEM, V...]
    ppermute x1 -> x2, starting transfers between devices: 3.1 us -> 3.61 us  [the longest x1 3.1 us: per_device(): picks = lax.ppermute(mine[:, TOK:TOK + CHUNK], 'frame', swap_sides)]
  transfers between devices with their start and end apart: 2 -> 5, of which waited for: 1 -> 2; matrix products, arithmetic and copies ran while one was open for 0% -> 1% of each run, Pallas kernels for 16% -> 35%
where the time goes in v3:
time: 141 us; the launch traced here: 140 us
  Pallas kernels  60.5 us (43%)
  starting transfers between devices  26.3 us (19%)
  waiting for transfers between devices  25.6 us (18%)
  blocking collectives  16.6 us (12%)
  local copies, waits for them, and re-layouts  10.1 us (7%)
    all_to_all x1, waiting for transfers between devices, per_device(): lax.all_to_all(packed, 'frame', 0, 0, tiled=True, axis_index_groups=groups)  23.8 us
    pallas_call x1, Pallas kernels, attend_other(): pl.pallas_call(functools.partial(other_kernel, starts), in_specs=[VMEM, V...  22.6 us
    pallas_call x3, Pallas kernels, attend_own(): pl.pallas_call(functools.partial(own_kernel, first), in_specs=[VMEM] + [A...  18.7 us
    all_to_all x1, blocking collectives, per_device(): lax.all_to_all(rest, 'frame', 0, 0, tiled=True, axis_index_groups=groups)  16.6 us
    unnamed x32, local copies, waits for them, and re-layouts  9.02 us
    all_to_all x1, starting transfers between devices, per_device(): lax.all_to_all(packed, 'frame', 0, 0, tiled=True, axis_index_groups=groups)  8.13 us
    all_to_all x1, starting transfers between devices, per_device(): arrived = lax.all_to_all(send, 'frame', 0, 0, tiled=True)  7.8 us
    pallas_call x1, Pallas kernels, project(): pl.pallas_call(project_kernel, grid=(steps,), in_specs=[pl.BlockSpec((TOK...  7 us
  transfers between devices with their start and end apart: 5, of which 2 were waited for; matrix products, arithmetic and copies ran while one was open for 1% of the time, Pallas kernels for 35%

profile of v3, /device:TPU:0, one launch (start us, length us, event | category | flops | bytes accessed | tf_op | source)
XLA Modules:
  0.0 140.1 jit_solution(12744311509455361840)
XLA Ops:
  0.6 7.0 %project.1 = (bf16[16,384,128]{2,1,0:T(8,128)(2,1)}, bf16[256,256]{1,0:T(8,128)(2,1)}) custom-call(bf16[256,1024]{1,0:T(8,128)(2,1)} %x_ref.5, f32[1,1024]{1,0:T(1,128)} %bitcast.3, s32[1,32]{1,0:T(1,128)} %slots_ref.3, bf16[1024,3072]{1,0:T(8,128)(2,1)} %wv_ref.1, bf16[1024,3072]{1,0:T(8,128)(2,1)} %wv_ref.1, bf16[1024,3072]{1,0:T(8,128)(2,1)} %wv_ref.1), custom_call_target="tpu_custom_call" | custom-call | tf_op jit(solution)/shard_map/project/pallas_call | solution.py:84
  7.6 8.1 %all-to-all-start = ((bf16[16,384,128]{2,1,0:T(8,128)(2,1)}), bf16[16,384,128]{2,1,0:T(8,128)(2,1)S(1)}, u32[]{:S(2)}, u32[]{:S(2)}) async-start(bf16[16,384,128]{2,1,0:T(8,128)(2,1)} %get-tuple-element.8), calls=%async_computation | async-start | bytes 3145728 | tf_op jit(solution)/shard_map/all_to_all | solution.py:373
  15.8 23.8 %all-to-all-done.mine_ref = bf16[16,384,128]{2,1,0:T(8,128)(2,1)S(1)} async-done(((bf16[16,384,128]{2,1,0:T(8,128)(2,1)}), bf16[16,384,128]{2,1,0:T(8,128)(2,1)S(1)}, u32[]{:S(2)}, u32[]{:S(2)}) %all-to-all-start) | async-done | bytes 1572896 | tf_op jit(solution)/shard_map/all_to_all | solution.py:373
  39.6 3.1 %collective-permute-start = (bf16[16,16,128]{2,1,0:T(8,128)(2,1)S(1)}, bf16[16,16,128]{2,1,0:T(8,128)(2,1)S(1)}, u32[]{:S(2)}, u32[]{:S(2)}) collective-permute-start(bf16[16,16,128]{2,1,0:T(8,128)(2,1)S(1)} %slice.8), channel_id=1, source_target_pairs={{0,1},{1,0},{2,3},{3,2},{4,5},{5,4},{6,7},{7,6},{8,9},{9,8},{10,11... | collective-permute-start | bytes 196616 | tf_op jit(solution)/shard_map/ppermute | solution.py:374
  42.7 1.0 slice.9
  44.2 5.4 %attend_own_1.1.rest_0_ = f32[1024,128]{1,0:T(8,128)S(1)} custom-call(bf16[16,384,128]{2,1,0:T(8,128)(2,1)S(1)} %all-to-all-done.mine_ref), custom_call_target="tpu_custom_call" | custom-call | flops 4294967296 | bytes 1048576 | tf_op jit(solution)/shard_map/attend_own_1/pallas_call | solution.py:226
  49.6 6.4 %attend_picks.1.rest_0_ = bf16[16,2,32,128]{3,2,1,0:T(8,128)(2,1)} custom-call(bf16[16,384,128]{2,1,0:T(8,128)(2,1)S(1)} %all-to-all-done.mine_ref, bf16[16,16,128]{2,1,0:T(8,128)(2,1)S(1)} %collective-permute-done.picks_ref, s32[1]{0:T(128)} %bitcast.1.me_ref, f32[1024,128]{1,0:T(8,128)S(1)} %attend_own_1.1.rest_0_), custom_call_target="tpu_custom_call" | custom-call | flops 4294967296 | bytes 1048576 | tf_op jit(solution)/shard_map/attend_picks/pallas_call | solution.py:237
  56.0 6.8 %all-to-all-start.1 = ((bf16[32,32,128]{2,1,0:T(8,128)(2,1)}), bf16[32,32,128]{2,1,0:T(8,128)(2,1)S(1)}, u32[]{:S(2)}, u32[]{:S(2)}) async-start(bf16[32,32,128]{2,1,0:T(8,128)(2,1)} %bitcast.2), calls=%async_computation.1 | async-start | bytes 524288 | tf_op jit(solution)/shard_map/all_to_all | solution.py:378
  62.9 8.0 %attend_own_3.1.rest_0_.rest_1_ = f32[1536,128]{1,0:T(8,128)S(1)} custom-call(bf16[16,384,128]{2,1,0:T(8,128)(2,1)S(1)} %all-to-all-done.mine_ref, bf16[16,2,32,128]{3,2,1,0:T(8,128)(2,1)} %attend_picks.1.rest_0_), custom_call_target="tpu_custom_call" | custom-call | flops 6442450944 | bytes 1048576 | tf_op jit(solution)/shard_map/attend_own_3/pallas_call | solution.py:226
  70.9 0.9 copy-done.11
  71.7 1.8 %all-to-all-done.1.part_ref = bf16[32,32,128]{2,1,0:T(8,128)(2,1)S(1)} async-done(((bf16[32,32,128]{2,1,0:T(8,128)(2,1)}), bf16[32,32,128]{2,1,0:T(8,128)(2,1)S(1)}, u32[]{:S(2)}, u32[]{:S(2)}) %all-to-all-start.1) | async-done | bytes 262176 | tf_op jit(solution)/shard_map/all_to_all | solution.py:378
  73.6 1.6 %copy-done.2 = bf16[1024,1024]{1,0:T(8,128)(2,1)S(1)} copy-done((bf16[1024,1024]{1,0:T(8,128)(2,1)S(1)}, bf16[1024,1024]{1,0:T(8,128)(2,1)}, u32[]{:S(2)}) %copy-start.2) | copy-done | bytes 2097176
  75.2 1.1 copy-done.12
  76.3 1.7 %track_rows.1 = (bf16[32,32,1024]{2,1,0:T(8,128)(2,1)S(1)}, bf16[32,1024]{1,0:T(8,128)(2,1)S(1)}) custom-call(bf16[32,32,128]{2,1,0:T(8,128)(2,1)S(1)} %all-to-all-done.1.part_ref, bf16[256,1024]{1,0:T(8,128)(2,1)S(1)} %copy-done.5, bf16[1024,1024]{1,0:T(8,128)(2,1)S(1)} %copy-done.2, bf16[256,256]{1,0:T(8,128)(2,1)S(1)} %copy-done.7, ...), custom_call_target="tpu_custom_call" | custom-call | flops 2147483648 | bytes 4194304 | tf_op jit(solution)/shard_map/track_rows/pallas_call | solution.py:312
  78.1 1.3 copy-done.4
  79.4 7.8 %all-to-all-start.2 = ((bf16[32,32,1024]{2,1,0:T(8,128)(2,1)}), bf16[32,32,1024]{2,1,0:T(8,128)(2,1)S(1)}, u32[]{:S(2)}, u32[]{:S(2)}) async-start(bf16[32,32,1024]{2,1,0:T(8,128)(2,1)} %copy-done.4), calls=%async_computation.2 | async-start | bytes 4194304 | tf_op jit(solution)/shard_map/all_to_all | solution.py:385
  87.2 1.4 copy-done.1
  88.6 5.4 %attend_own_6.1.rest_2_ = f32[1024,128]{1,0:T(8,128)S(1)} custom-call(bf16[16,384,128]{2,1,0:T(8,128)(2,1)S(1)} %copy-done.1, bf16[32,1024]{1,0:T(8,128)(2,1)S(1)} %get-tuple-element.10.rest_0_.att1_ref), custom_call_target="tpu_custom_call" | custom-call | flops 4294967296 | bytes 1048576 | tf_op jit(solution)/shard_map/attend_own_6/pallas_call | solution.py:226
  94.0 22.6 %attend_other.1 = bf16[16,112,128]{2,1,0:T(8,128)(2,1)S(1)} custom-call(bf16[16,384,128]{2,1,0:T(8,128)(2,1)S(1)} %copy-done.1, bf16[16,256,128]{2,1,0:T(8,128)(2,1)} %collective-permute-done.1.other_ref, f32[1024,128]{1,0:T(8,128)S(1)} %copy-done.15, f32[1536,128]{1,0:T(8,128)S(1)} %copy-done.13, f32[1024,128]{1,0:T(8,128)S(1)} %attend_own_6.1.rest_2_), custom_call_target="tpu_custom_call" | custom-call | flops 15032385536 | bytes 1048576 | tf_op jit(solution)/shard_map/attend_other/pallas_call | solution.py:256
  116.6 16.6 %all_to_all.20.at2_ref = bf16[16,112,128]{2,1,0:T(8,128)(2,1)S(1)} all-to-all(bf16[16,112,128]{2,1,0:T(8,128)(2,1)S(1)} %attend_other.1), channel_id=1, replica_groups={{0,2,4,6,8,10,12,14,16,18,20,22,24,26,28,30},{1,3,5,7,9,11,13,15,17,19,..., dimensions={0} | all-to-all | bytes 917504 | tf_op jit(solution)/shard_map/all_to_all | solution.py:389
  133.2 1.6 %copy-done.3 = bf16[1024,1024]{1,0:T(8,128)(2,1)S(1)} copy-done((bf16[1024,1024]{1,0:T(8,128)(2,1)S(1)}, bf16[1024,1024]{1,0:T(8,128)(2,1)}, u32[]{:S(2)}) %copy-start.3) | copy-done | bytes 2097176
  134.8 1.8 %mix.1.mixed_ref = bf16[256,1024]{1,0:T(8,128)(2,1)} custom-call(bf16[32,1024]{1,0:T(8,128)(2,1)S(1)} %get-tuple-element.10.rest_0_.att1_ref, bf16[16,112,128]{2,1,0:T(8,128)(2,1)S(1)} %all_to_all.20.at2_ref, bf16[256,1024]{1,0:T(8,128)(2,1)S(1)} %copy-done.5, bf16[1024,1024]{1,0:T(8,128)(2,1)S(1)} %copy-done.3, bf16[256,256]{1,0:T(8,128)(2,1)S(1)} %copy-done.7), custom_call_target="tpu_custom_call" | custom-call | tf_op jit(solution)/shard_map/mix/pallas_call | solution.py:337
  136.6 1.0 copy-done.6
  137.6 2.4 %correlate.1 = f32[1,32,32,256]{3,2,1,0:T(8,128)} custom-call(bf16[32,32,1024]{2,1,0:T(8,128)(2,1)S(1)} %all-to-all-done.2.rows_ref, bf16[256,1024]{1,0:T(8,128)(2,1)S(1)} %copy-done.6), custom_call_target="tpu_custom_call" | custom-call | tf_op jit(solution)/shard_map/correlate/pallas_call | solution.py:357
  (30 shorter events, 0.6 us)
Async XLA Ops:
  7.6 31.9 %all-to-all-start = ((bf16[16,384,128]{2,1,0:T(8,128)(2,1)}), bf16[16,384,128]{2,1,0:T(8,128)(2,1)S(1)}, u32[]{:S(2)}, u32[]{:S(2)}) async-start(bf16[16,384,128]{2,1,0:T(8,128)(2,1)} %get-tuple-element.8), calls=%async_computation | async-start | bytes 3145728 | tf_op jit(solution)/shard_map/all_to_all | solution.py:373
  39.5 23.3 %copy-start = (bf16[16,384,128]{2,1,0:T(8,128)(2,1)}, bf16[16,384,128]{2,1,0:T(8,128)(2,1)S(1)}, u32[]{:S(2)}) copy-start(bf16[16,384,128]{2,1,0:T(8,128)(2,1)S(1)} %all-to-all-done.mine_ref) | copy-start | bytes 4718596
  39.6 10.0 %collective-permute-start = (bf16[16,16,128]{2,1,0:T(8,128)(2,1)S(1)}, bf16[16,16,128]{2,1,0:T(8,128)(2,1)S(1)}, u32[]{:S(2)}, u32[]{:S(2)}) collective-permute-start(bf16[16,16,128]{2,1,0:T(8,128)(2,1)S(1)} %slice.8), channel_id=1, source_target_pairs={{0,1},{1,0},{2,3},{3,2},{4,5},{5,4},{6,7},{7,6},{8,9},{9,8},{10,11... | collective-permute-start | bytes 196616 | tf_op jit(solution)/shard_map/ppermute | solution.py:374
  43.7 50.3 %collective-permute-start.1 = (bf16[16,256,128]{2,1,0:T(8,128)(2,1)}, bf16[16,256,128]{2,1,0:T(8,128)(2,1)}, u32[]{:S(2)}, u32[]{:S(2)}) collective-permute-start(bf16[16,256,128]{2,1,0:T(8,128)(2,1)} %slice.9), channel_id=1, source_target_pairs={{0,1},{1,0},{2,3},{3,2},{4,5},{5,4},{6,7},{7,6},{8,9},{9,8},{10,11... | collective-permute-start | bytes 3145736 | tf_op jit(solution)/shard_map/ppermute | solution.py:375
  49.6 6.4 %copy-start.14 = (f32[1024,128]{1,0:T(8,128)}, f32[1024,128]{1,0:T(8,128)S(1)}, u32[]{:S(2)}) copy-start(f32[1024,128]{1,0:T(8,128)S(1)} %attend_own_1.1.rest_0_) | copy-start | bytes 1572868
  56.0 17.6 %all-to-all-start.1 = ((bf16[32,32,128]{2,1,0:T(8,128)(2,1)}), bf16[32,32,128]{2,1,0:T(8,128)(2,1)S(1)}, u32[]{:S(2)}, u32[]{:S(2)}) async-start(bf16[32,32,128]{2,1,0:T(8,128)(2,1)} %bitcast.2), calls=%async_computation.1 | async-start | bytes 524288 | tf_op jit(solution)/shard_map/all_to_all | solution.py:378
  62.8 10.8 %copy-start.5 = (bf16[256,1024]{1,0:T(8,128)(2,1)S(1)}, bf16[256,1024]{1,0:T(8,128)(2,1)}, u32[]{:S(2)}) copy-start(bf16[256,1024]{1,0:T(8,128)(2,1)} %x_ref.5) | copy-start | bytes 1572868
  62.8 10.7 %copy-start.7 = (bf16[256,256]{1,0:T(8,128)(2,1)S(1)}, bf16[256,256]{1,0:T(8,128)(2,1)}, u32[]{:S(2)}) copy-start(bf16[256,256]{1,0:T(8,128)(2,1)} %get-tuple-element.9.place_ref) | copy-start | bytes 393220
  62.8 10.7 %copy-start.8 = (s32[1,32]{1,0:T(1,128)S(1)}, s32[1,32]{1,0:T(1,128)}, u32[]{:S(2)}) copy-start(s32[1,32]{1,0:T(1,128)} %slots_ref.3) | copy-start | bytes 388
  62.9 10.7 %copy-start.9 = (s32[32]{0:T(128)S(1)}, s32[32]{0:T(128)}, u32[]{:S(2)}) copy-start(s32[32]{0:T(128)} %counts_ref.1) | copy-start | bytes 388
  62.9 10.7 %copy-start.10 = (s32[32]{0:T(128)S(1)}, s32[32]{0:T(128)}, u32[]{:S(2)}) copy-start(s32[32]{0:T(128)} %owner_ref.1) | copy-start | bytes 388
  70.8 0.9 copy-start.11
  73.6 1.6 %copy-start.2 = (bf16[1024,1024]{1,0:T(8,128)(2,1)S(1)}, bf16[1024,1024]{1,0:T(8,128)(2,1)}, u32[]{:S(2)}) copy-start(bf16[1024,1024]{1,0:T(8,128)(2,1)} %w_ref.3) | copy-start | bytes 6291460
  75.2 1.1 copy-start.12
  78.0 1.3 copy-start.4
  79.4 37.2 %all-to-all-start.2 = ((bf16[32,32,1024]{2,1,0:T(8,128)(2,1)}), bf16[32,32,1024]{2,1,0:T(8,128)(2,1)S(1)}, u32[]{:S(2)}, u32[]{:S(2)}) async-start(bf16[32,32,1024]{2,1,0:T(8,128)(2,1)} %copy-done.4), calls=%async_computation.2 | async-start | bytes 4194304 | tf_op jit(solution)/shard_map/all_to_all | solution.py:385
  87.2 1.4 %copy-start.1 = (bf16[16,384,128]{2,1,0:T(8,128)(2,1)S(1)}, bf16[16,384,128]{2,1,0:T(8,128)(2,1)}, u32[]{:S(2)}) copy-start(bf16[16,384,128]{2,1,0:T(8,128)(2,1)} %copy-done) | copy-start | bytes 4718596
  88.6 5.4 %copy-start.13 = (f32[1536,128]{1,0:T(8,128)S(1)}, f32[1536,128]{1,0:T(8,128)}, u32[]{:S(2)}) copy-start(f32[1536,128]{1,0:T(8,128)} %copy-done.11) | copy-start | bytes 2359300
  88.6 5.4 %copy-start.15 = (f32[1024,128]{1,0:T(8,128)S(1)}, f32[1024,128]{1,0:T(8,128)}, u32[]{:S(2)}) copy-start(f32[1024,128]{1,0:T(8,128)} %copy-done.14) | copy-start | bytes 1572868
  133.2 1.6 %copy-start.3 = (bf16[1024,1024]{1,0:T(8,128)(2,1)S(1)}, bf16[1024,1024]{1,0:T(8,128)(2,1)}, u32[]{:S(2)}) copy-start(bf16[1024,1024]{1,0:T(8,128)(2,1)} %w_ref.3) | copy-start | bytes 6291460
  136.6 1.0 copy-start.6

commit v4 on v3

v4 whole, which is shorter than its diff:
```python
import functools

import jax
import jax.numpy as jnp
from jax import lax
from jax.experimental import pallas as pl
from jax.experimental.pallas import tpu as pltpu
from jax.sharding import PartitionSpec as P

D = 1024
HEADS = 16
HDIM = 64
TOK = 256
FRAMES = 32
QMAX = 32
LANES = 128
LOG2E = 1.4426950408889634
NT = (((1,), (1,)), ((), ()))
TN = (((0,), (0,)), ((), ()))
CHUNK = 16
F32 = jnp.float32
BF16 = jnp.bfloat16


def low_half(rows):
    return lax.broadcasted_iota(jnp.int32, (rows, LANES), 1) < HDIM


def swap(x):
    return pltpu.roll(x, HDIM, 1)


def slot_of_token(slots):
    return lax.broadcasted_iota(jnp.int32, (TOK, QMAX), 0) == slots


def arrange(slots):
    picked = jnp.max(jnp.where(slot_of_token(slots), 1.0, 0.0), axis=1, keepdims=True)
    row = lax.broadcasted_iota(jnp.int32, (TOK, TOK), 0)
    col = lax.broadcasted_iota(jnp.int32, (TOK, TOK), 1)
    wide = jnp.broadcast_to(picked, (TOK, LANES)).astype(BF16)
    before = jnp.dot(jnp.where(col < row, 1.0, 0.0).astype(BF16), wide, preferred_element_type=F32)
    before = before[:, :1].astype(jnp.int32)
    total = jnp.sum(picked).astype(jnp.int32)
    token = lax.broadcasted_iota(jnp.int32, (TOK, 1), 0)
    rank = jnp.where(picked > 0.5, before, total + token - before)
    within = rank & 31
    place = (rank >> 5) * CHUNK + (within & 15) + jnp.where(within >= CHUNK, TOK // 2, 0)
    return jnp.where(place == col, 1.0, 0.0).astype(BF16)


STEPS = 4
WIDTH = D // STEPS


def project_kernel(x_ref, g_ref, slots_ref, w_hbm, o_ref, place_ref, n_ref, w_ref, sems):
    def load(step, part):
        cols = pl.ds(pl.multiple_of(part * D + step * WIDTH, WIDTH), WIDTH)
        return pltpu.make_async_copy(w_hbm.at[:, cols], w_ref.at[step, part], sems.at[step, part])

    step = pl.program_id(0)

    @pl.when(step == 0)
    def _():
        for i in range(STEPS):
            for part in range(3):
                load(i, part).start()
        place = arrange(slots_ref[...])
        place_ref[...] = place
        xf = x_ref[...].astype(F32)
        mean = jnp.mean(xf, axis=-1, keepdims=True)
        cen = xf - mean
        var = jnp.mean(cen * cen, axis=-1, keepdims=True)
        normed = (cen * lax.rsqrt(var + 1e-05) * g_ref[...]).astype(BF16)
        n_ref[...] = lax.dot_general(place, normed, TN, preferred_element_type=F32).astype(BF16)

    n = n_ref[...]

    def product(part):
        load(step, part).wait()
        return jnp.dot(n, w_ref[step, part], preferred_element_type=F32)

    q = product(0) * (1.0 / HDIM**0.5)
    k = product(1)
    v = product(2)
    half = TOK // 2
    low = low_half(TOK)
    lowh = low_half(half)
    for c in range(WIDTH // LANES):
        cols = slice(c * LANES, (c + 1) * LANES)
        kp, vp = k[:, cols], v[:, cols]
        qa, qb = q[:half, cols], q[half:, cols]
        o_ref[2 * c, :TOK] = jnp.where(low, kp, swap(vp)).astype(BF16)
        o_ref[2 * c + 1, :TOK] = jnp.where(low, swap(kp), vp).astype(BF16)
        o_ref[2 * c, TOK:] = jnp.where(lowh, qa, swap(qb)).astype(BF16)
        o_ref[2 * c + 1, TOK:] = jnp.where(lowh, swap(qa), qb).astype(BF16)


def project(x, gain, slots, w_qkv):
    rows = TOK + TOK // 2
    return pl.pallas_call(
        project_kernel,
        grid=(STEPS,),
        in_specs=[
            pl.BlockSpec((TOK, D), lambda i: (0, 0)),
            pl.BlockSpec((1, D), lambda i: (0, 0)),
            pl.BlockSpec((1, QMAX), lambda i: (0, 0)),
            pl.BlockSpec(memory_space=pl.ANY),
        ],
        out_specs=[
            pl.BlockSpec((HEADS // STEPS, rows, LANES), lambda i: (i, 0, 0)),
            pl.BlockSpec((TOK, TOK), lambda i: (0, 0)),
        ],
        out_shape=[
            jax.ShapeDtypeStruct((HEADS, rows, LANES), BF16),
            jax.ShapeDtypeStruct((TOK, TOK), BF16),
        ],
        scratch_shapes=[
            pltpu.VMEM((TOK, D), BF16),
            pltpu.VMEM((STEPS, 3, D, WIDTH), BF16),
            pltpu.SemaphoreType.DMA((STEPS, 3)),
        ],
        compiler_params=pltpu.CompilerParams(vmem_limit_bytes=60 << 20),
        name="project",
    )(x, gain.reshape(1, D), slots, w_qkv)


BLOCK_FRAMES = 4
GROUP = FRAMES // 2
CHUNKS = TOK // (2 * CHUNK)
ROWS = GROUP * 2 * CHUNK
SPLIT = 6


def unpack_queries(packed):
    packed = packed.reshape(GROUP * CHUNK, LANES).astype(F32)
    low = low_half(packed.shape[0])
    zero = jnp.zeros_like(packed)
    both = [jnp.where(low, packed, zero), jnp.where(low, swap(packed), zero)]
    return jnp.concatenate(both, axis=0).astype(BF16)


class Source:
    def __init__(self, kv_hbm, q_hbm, first, count, kv_ref, va_ref, q_ref, sems):
        self.kv_ref, self.va_ref, self.q_ref = kv_ref, va_ref, q_ref
        self.copies, self.waited = {}, set()
        rows = pl.ds(TOK + first * CHUNK, count * CHUNK)
        self.start("q", q_hbm.at[:, rows], q_ref, sems.at[0])
        for j in range(BLOCKS):
            frames = pl.ds(j * BLOCK_FRAMES, BLOCK_FRAMES)
            self.start(j, kv_hbm.at[frames, pl.ds(0, TOK)], kv_ref.at[frames], sems.at[1 + j])

    def start(self, name, source, target, sem):
        self.copies[name] = pltpu.make_async_copy(source, target, sem)
        self.copies[name].start()

    def wait(self, name):
        if name not in self.waited:
            self.waited.add(name)
            self.copies[name].wait()

    def keys(self, j):
        if j not in self.waited:
            self.wait(j)
            for f in range(j * BLOCK_FRAMES, (j + 1) * BLOCK_FRAMES):
                kv = self.kv_ref[f]
                self.va_ref[f] = jnp.where(low_half(TOK), jnp.ones_like(kv), kv)
        return self.block(self.kv_ref, j)

    def values(self, j):
        return self.block(self.va_ref, j)

    def block(self, ref, j):
        return ref[j * BLOCK_FRAMES : (j + 1) * BLOCK_FRAMES].reshape(BLOCK_FRAMES * TOK, LANES)

    def queries(self, i):
        self.wait("q")
        return unpack_queries(self.q_ref[:, i * CHUNK : (i + 1) * CHUNK])


BLOCKS = GROUP // BLOCK_FRAMES


def attend(items, source):
    steps = [(i, j) for i in range(len(items)) for j in range(BLOCKS)]
    queries = {}

    def scores(i, j):
        if i not in queries:
            queries[i] = items[i][0]()
        return lax.dot_general(queries[i], source.keys(j), NT, preferred_element_type=F32)

    s = scores(0, 0)
    top = acc = None
    for n, (i, j) in enumerate(steps):
        ahead = scores(*steps[n + 1]) if n + 1 < len(steps) else None
        if j == 0:
            acc = None if items[i][1] is None else items[i][1]()
            top = None if acc is None else acc[:, 1:2]
        newtop = jnp.max(s, axis=-1, keepdims=True) * LOG2E
        if top is not None:
            newtop = jnp.maximum(top, newtop)
        p = jnp.exp2(s * LOG2E - newtop).astype(BF16)
        pv = jnp.dot(p, source.values(j), preferred_element_type=F32)
        acc = pv if top is None else acc * jnp.exp2(top - newtop) + pv
        top, s = newtop, ahead
        if j == BLOCKS - 1:
            items[i][2](top, acc)


def own_kernel(first, count, mine_hbm, *rest):
    state_ref, tick_ref, kv_ref, va_ref, q_ref, sems = rest[-6:]
    tick_ref[...] = jnp.zeros_like(tick_ref)
    source = Source(mine_hbm, mine_hbm, first, count, kv_ref, va_ref, q_ref, sems)

    def item(i):
        def finish(top, acc):
            lane = lax.broadcasted_iota(jnp.int32, acc.shape, 1)
            state_ref[i * ROWS : (i + 1) * ROWS] = jnp.where(lane == 1, top, acc)

        return lambda: source.queries(i), None, finish

    attend([item(i) for i in range(count)], source)


def other_kernel(counts, mine_hbm, other_hbm, *rest):
    o_ref, kv_ref, va_ref, q_ref, sems, state_ref, state_sems = rest[-7:]
    chunks = sum(counts)
    source = Source(other_hbm, mine_hbm, CHUNKS - chunks, chunks, kv_ref, va_ref, q_ref, sems)
    places = [(n, k) for n, count in enumerate(counts) for k in range(count)]
    for n, count in enumerate(counts):
        target = state_ref.at[pl.ds(sum(counts[:n]) * ROWS, count * ROWS)]
        source.start(("state", n), rest[n], target, state_sems.at[n])

    def item(i):
        def state():
            source.wait(("state", places[i][0]))
            return state_ref[i * ROWS : (i + 1) * ROWS]

        def finish(top, acc):
            out = acc / acc[:, :1]
            packed = jnp.where(low_half(ROWS // 2), swap(out[: ROWS // 2]), out[ROWS // 2 :])
            packed = packed.astype(BF16).reshape(GROUP, CHUNK, LANES)
            o_ref[:, i * CHUNK : (i + 1) * CHUNK] = packed

        return lambda: source.queries(i), state, finish

    attend([item(i) for i in range(chunks)], source)


def picks_kernel(mine_hbm, picks_ref, me_ref, *rest):
    o_ref, tick_ref, kv_ref, va_ref, q_ref, sems = rest[-6:]
    tick_ref[...] = jnp.zeros_like(tick_ref)
    source = Source(mine_hbm, mine_hbm, 0, 1, kv_ref, va_ref, q_ref, sems)
    mine_side = me_ref[0] & 1

    def item(side, queries):
        def finish(top, acc):
            sums = acc[:, :1]
            mean = acc / sums
            level = top + jnp.log2(sums)
            part0 = level.astype(BF16).astype(F32)
            part1 = (level - part0).astype(BF16).astype(F32)
            part2 = level - part0 - part1
            lane = lax.broadcasted_iota(jnp.int32, acc.shape, 1)
            low = jnp.where(lane == 0, part0, jnp.where(lane == 1, part1, part2))
            out = jnp.where(lane < HDIM, low, mean).astype(BF16).reshape(2, GROUP, CHUNK, LANES)
            for half in range(2):
                o_ref[:, side, half * CHUNK : (half + 1) * CHUNK] = out[half]

        return queries, None, finish

    items = [
        item(mine_side, lambda: source.queries(0)),
        item(1 - mine_side, lambda: unpack_queries(picks_ref[...])),
    ]
    attend(items, source)


SMEM = pl.BlockSpec(memory_space=pltpu.SMEM)
ANY = pl.BlockSpec(memory_space=pl.ANY)
WHOLE = pl.BlockSpec()
TICK = jax.ShapeDtypeStruct((8, LANES), F32)
PARAMS = pltpu.CompilerParams(vmem_limit_bytes=60 << 20)


def attend_settings(chunks, work):
    pairs = work * ROWS * GROUP * TOK
    return dict(
        scratch_shapes=[
            pltpu.VMEM((GROUP, TOK, LANES), BF16),
            pltpu.VMEM((GROUP, TOK, LANES), BF16),
            pltpu.VMEM((GROUP, chunks * CHUNK, LANES), BF16),
            pltpu.SemaphoreType.DMA((1 + BLOCKS,)),
        ],
        compiler_params=PARAMS,
        cost_estimate=pl.CostEstimate(
            flops=2 * pairs * LANES * 4, bytes_accessed=1 << 20, transcendentals=pairs
        ),
    )


def attend_own(mine, first, last, after=()):
    count = last - first
    return pl.pallas_call(
        functools.partial(own_kernel, first, count),
        in_specs=[ANY] + [WHOLE] * len(after),
        out_specs=[WHOLE, WHOLE],
        out_shape=[jax.ShapeDtypeStruct((count * ROWS, LANES), F32), TICK],
        name=f"attend_own_{first}",
        **attend_settings(count, count),
    )(mine, *after)


def attend_picks(mine, picks, me, after):
    return pl.pallas_call(
        picks_kernel,
        in_specs=[ANY, WHOLE, SMEM] + [WHOLE] * len(after),
        out_specs=[WHOLE, WHOLE],
        out_shape=[jax.ShapeDtypeStruct((GROUP, 2, QMAX, LANES), BF16), TICK],
        name="attend_picks",
        **attend_settings(1, 2),
    )(mine, picks, me, *after)


def attend_other(mine, other, states):
    counts = [state.shape[0] // ROWS for state in states]
    chunks = sum(counts)
    settings = attend_settings(chunks, chunks)
    settings["scratch_shapes"] += [
        pltpu.VMEM((chunks * ROWS, LANES), F32),
        pltpu.SemaphoreType.DMA((len(states),)),
    ]
    return pl.pallas_call(
        functools.partial(other_kernel, counts),
        in_specs=[ANY] * (2 + len(states)),
        out_specs=WHOLE,
        out_shape=jax.ShapeDtypeStruct((GROUP, chunks * CHUNK, LANES), BF16),
        name="attend_other",
        **settings,
    )(mine, other, *states)


def join_heads(even_odd):
    top, bottom = [], []
    for even, odd in even_odd:
        low = low_half(even.shape[0])
        top.append(jnp.where(low, even, swap(odd)).astype(BF16))
        bottom.append(jnp.where(low, swap(even), odd).astype(BF16))
    return jnp.concatenate(top, axis=1), jnp.concatenate(bottom, axis=1)


def level_of(part):
    return part[:, 0:1] + part[:, 1:2] + part[:, 2:3]


def rows_kernel(part_ref, x_hbm, w_hbm, place_ref, slots_ref, counts_ref, owner_ref, me_ref, *rest):
    send_hbm, att_ref, x_ref, w_ref, zero_ref, rows_ref, sems = rest[-7:]
    load_w = pltpu.make_async_copy(w_hbm, w_ref, sems.at[0])
    load_x = pltpu.make_async_copy(x_hbm, x_ref, sems.at[1])
    load_w.start()
    load_x.start()
    zero_ref[...] = jnp.zeros_like(zero_ref)
    count = zero_ref.shape[0]
    clears = [
        pltpu.make_async_copy(zero_ref, send_hbm.at[pl.ds(i * count, count)], sems.at[2 + i])
        for i in range(FRAMES // count)
    ]
    for clear in clears:
        clear.start()
    heads = []
    for h in range(HEADS):
        a, b = part_ref[2 * h].astype(F32), part_ref[2 * h + 1].astype(F32)
        la, lb = level_of(a), level_of(b)
        most = jnp.maximum(la, lb)
        wa, wb = jnp.exp2(la - most), jnp.exp2(lb - most)
        heads.append((a * wa + b * wb) / (wa + wb))
    att = jnp.concatenate(
        [
            jnp.where(low_half(QMAX), swap(heads[2 * i]), heads[2 * i + 1]).astype(BF16)
            for i in range(HEADS // 2)
        ],
        axis=1,
    )
    att_ref[...] = att
    gap = jnp.zeros((TOK // 2 - CHUNK, D), BF16)
    placed = jnp.concatenate([att[:CHUNK], gap, att[CHUNK:], gap], axis=0)
    token_slot = jnp.where(slot_of_token(slots_ref[...]), 1.0, 0.0).astype(BF16)
    where = lax.dot_general(token_slot, place_ref[...], TN, preferred_element_type=F32).astype(BF16)
    chosen = jnp.dot(where, placed, preferred_element_type=F32).astype(BF16)
    load_x.wait()
    x = lax.dot_general(token_slot, x_ref[...], TN, preferred_element_type=F32)
    load_w.wait()
    rows = (x + jnp.dot(chosen, w_ref[...], preferred_element_type=F32)).astype(BF16)
    me = me_ref[0]
    slot = lax.broadcasted_iota(jnp.int32, rows.shape, 0)
    rows_ref[...] = jnp.where(slot < counts_ref[me], rows, jnp.zeros_like(rows))
    for clear in clears:
        clear.wait()
    put = pltpu.make_async_copy(rows_ref, send_hbm.at[owner_ref[me]], sems.at[0])
    put.start()
    put.wait()


def track_rows(parts, x, w_out, place, slots, counts, owner, me, after):
    return pl.pallas_call(
        rows_kernel,
        in_specs=[WHOLE, ANY, ANY, WHOLE, WHOLE] + [SMEM] * 3 + [WHOLE] * len(after),
        out_specs=[ANY, WHOLE],
        scratch_shapes=[
            pltpu.VMEM((TOK, D), BF16),
            pltpu.VMEM((D, D), BF16),
            pltpu.VMEM((8, QMAX, D), BF16),
            pltpu.VMEM((QMAX, D), BF16),
            pltpu.SemaphoreType.DMA((2 + FRAMES // 8,)),
        ],
        out_shape=[
            jax.ShapeDtypeStruct((FRAMES, QMAX, D), BF16),
            jax.ShapeDtypeStruct((QMAX, D), BF16),
        ],
        compiler_params=PARAMS,
        cost_estimate=pl.CostEstimate(flops=2 << 30, bytes_accessed=4 << 20, transcendentals=0),
        name="track_rows",
    )(parts, x, w_out, place, slots, counts, owner, me, *after)


def finish_kernel(att1_ref, at2_ref, place_ref, rows_hbm, x_hbm, w_hbm, mixed_ref, corr_ref, x_ref, w_ref, rows_ref, sems):
    load_rows = pltpu.make_async_copy(rows_hbm, rows_ref, sems.at[2])

    @pl.when(pl.program_id(0) == 0)
    def _():
        load_w = pltpu.make_async_copy(w_hbm, w_ref, sems.at[0])
        load_x = pltpu.make_async_copy(x_hbm, x_ref, sems.at[1])
        load_w.start()
        load_x.start()
        load_rows.start()
        pairs = [
            (at2_ref[2 * i].astype(F32), at2_ref[2 * i + 1].astype(F32)) for i in range(HEADS // 2)
        ]
        top, bottom = join_heads(pairs)
        placed = jnp.concatenate([att1_ref[:CHUNK], top, att1_ref[CHUNK:], bottom], axis=0)
        att = jnp.dot(place_ref[...], placed, preferred_element_type=F32).astype(BF16)
        load_x.wait()
        load_w.wait()
        mixed_ref[...] = (
            x_ref[...].astype(F32) + jnp.dot(att, w_ref[...], preferred_element_type=F32)
        ).astype(BF16)
        load_rows.wait()

    step = corr_ref.shape[1]
    rows = rows_ref[pl.ds(pl.program_id(0) * step, step)].reshape(-1, D)
    corr = lax.dot_general(rows, mixed_ref[...], NT, preferred_element_type=F32)
    corr_ref[...] = (corr * (1.0 / D**0.5)).reshape(corr_ref.shape)


def finish(att1, att2, x, w_out, place, arrived):
    step = 8
    return pl.pallas_call(
        finish_kernel,
        grid=(FRAMES // step,),
        in_specs=[
            pl.BlockSpec(att1.shape, lambda i: (0, 0)),
            pl.BlockSpec(att2.shape, lambda i: (0, 0, 0)),
            pl.BlockSpec(place.shape, lambda i: (0, 0)),
        ]
        + [ANY] * 3,
        out_specs=[
            pl.BlockSpec((TOK, D), lambda i: (0, 0)),
            pl.BlockSpec((1, step, QMAX, TOK), lambda i: (0, i, 0, 0)),
        ],
        out_shape=[
            jax.ShapeDtypeStruct((TOK, D), BF16),
            jax.ShapeDtypeStruct((1, FRAMES, QMAX, TOK), F32),
        ],
        scratch_shapes=[
            pltpu.VMEM((TOK, D), BF16),
            pltpu.VMEM((D, D), BF16),
            pltpu.VMEM((FRAMES, QMAX, D), BF16),
            pltpu.SemaphoreType.DMA((3,)),
        ],
        compiler_params=PARAMS,
        name="finish",
    )(att1, att2, place, arrived, x, w_out)


def per_device(features, norm_gain, w_qkv, w_out, counts, query_index, owner):
    groups = [[2 * i + side for i in range(GROUP)] for side in range(2)]
    swap_sides = [(d, d ^ 1) for d in range(FRAMES)]
    me = lax.axis_index("frame").astype(jnp.int32).reshape(1)
    packed, place = project(features, norm_gain, query_index, w_qkv)
    mine = lax.all_to_all(packed, "frame", 0, 0, tiled=True, axis_index_groups=groups)
    picks = lax.ppermute(mine[:, TOK : TOK + CHUNK], "frame", swap_sides)
    other = lax.ppermute(mine[:, :TOK], "frame", swap_sides)
    state1, tick = attend_own(mine, 1, 3)
    parts, tick = attend_picks(mine, picks, me, [tick])
    parts_here = lax.all_to_all(
        parts.reshape(FRAMES, QMAX, LANES), "frame", 0, 0, tiled=True
    )
    state2, tick = attend_own(mine, 3, SPLIT, [tick])
    send, att1 = track_rows(
        parts_here, features, w_out, place, query_index, counts, owner, me, [tick]
    )
    arrived = lax.all_to_all(send, "frame", 0, 0, tiled=True)
    state3, _ = attend_own(mine, SPLIT, CHUNKS, [att1])
    rest = attend_other(mine, other, [state1, state2, state3])
    rest, arrived = lax.optimization_barrier((rest, arrived))
    att2 = lax.all_to_all(rest, "frame", 0, 0, tiled=True, axis_index_groups=groups)
    return tuple(finish(att1, att2, features, w_out, place, arrived))


def solution(mesh):
    rows = P(("scene", "frame"), None)
    in_specs = (rows, P(), P(), P(), P("scene"), rows, P("scene"))
    out_specs = (rows, P(("scene", "frame"), None, None, None))
    return jax.shard_map(
        per_device, mesh=mesh, in_specs=in_specs, out_specs=out_specs, check_vma=False
    )
```

time: 141 us -> 154 us (1.092); the launches traced: 140 us -> 151 us
  Pallas kernels: 60.5 us -> 79.1 us
  local copies, waits for them, and re-layouts: 10.1 us -> 1.43 us
  starting transfers between devices: 26.3 us -> 29 us
  waiting for transfers between devices: 25.6 us -> 23.8 us
    pallas_call x9 -> x8, Pallas kernels: 60.5 us -> 79.1 us  [the longest x3 27.7 us: attend_own(): pl.pallas_call(functools.partial(own_kernel, first, count), in_specs=[ANY...]
    unnamed x32 -> x8, local copies, waits for them, and re-layouts: 9.02 us -> 1.33 us
    all_to_all x1, starting transfers between devices: 7.8 us -> 10 us  [per_device(): arrived = lax.all_to_all(send, 'frame', 0, 0, tiled=True)]
    all_to_all x1, waiting for transfers between devices: 1.84 us -> 0.01 us  [per_device(): lax.all_to_all(parts.reshape(FRAMES, QMAX, LANES), 'frame', 0, 0, tiled=T...]
  transfers between devices with their start and end apart: 5 -> 5, of which waited for: 2 -> 1; matrix products, arithmetic and copies ran while one was open for 1% -> 0% of each run, Pallas kernels for 35% -> 43%
where the time goes in v4:
time: 154 us; the launch traced here: 151 us
  Pallas kernels  79.1 us (51%)
  starting transfers between devices  29 us (19%)
  waiting for transfers between devices  23.8 us (15%)
  blocking collectives  17 us (11%)
    pallas_call x3, Pallas kernels, attend_own(): pl.pallas_call(functools.partial(own_kernel, first, count), in_specs=[ANY...  27.7 us
    all_to_all x1, waiting for transfers between devices, per_device(): lax.all_to_all(packed, 'frame', 0, 0, tiled=True, axis_index_groups=groups)  23.8 us
    pallas_call x1, Pallas kernels, attend_other(): pl.pallas_call(functools.partial(other_kernel, counts), in_specs=[ANY] *...  22.9 us
    all_to_all x1, blocking collectives, per_device(): lax.all_to_all(rest, 'frame', 0, 0, tiled=True, axis_index_groups=groups)  17 us
    all_to_all x1, starting transfers between devices, per_device(): arrived = lax.all_to_all(send, 'frame', 0, 0, tiled=True)  10 us
    pallas_call x1, Pallas kernels, attend_picks(): pl.pallas_call(picks_kernel, in_specs=[ANY, WHOLE, SMEM] + [WHOLE] * len(...  9.06 us
    all_to_all x1, starting transfers between devices, per_device(): lax.all_to_all(packed, 'frame', 0, 0, tiled=True, axis_index_groups=groups)  8.14 us
    pallas_call x1, Pallas kernels, project(): pl.pallas_call(project_kernel, grid=(STEPS,), in_specs=[pl.BlockSpec((TOK...  8.08 us
  transfers between devices with their start and end apart: 5, of which 1 were waited for; matrix products, arithmetic and copies ran while one was open for 0% of the time, Pallas kernels for 43%

profile of v4, /device:TPU:0, one launch (start us, length us, event | category | flops | bytes accessed | tf_op | source)
XLA Modules:
  0.0 151.3 jit_solution(11326144576232163255)
XLA Ops:
  0.6 8.1 %project.1 = (bf16[16,384,128]{2,1,0:T(8,128)(2,1)}, bf16[256,256]{1,0:T(8,128)(2,1)}) custom-call(bf16[256,1024]{1,0:T(8,128)(2,1)} %x_hbm.3, f32[1,1024]{1,0:T(1,128)} %bitcast.4, s32[1,32]{1,0:T(1,128)} %slots_ref.3, bf16[1024,3072]{1,0:T(8,128)(2,1)} %w_hbm.3), custom_call_target="tpu_custom_call" | custom-call | tf_op jit(solution)/shard_map/project/pallas_call | solution.py:101
  8.7 8.1 %all-to-all-start = ((bf16[16,384,128]{2,1,0:T(8,128)(2,1)}), bf16[16,384,128]{2,1,0:T(8,128)(2,1)S(1)}, u32[]{:S(2)}, u32[]{:S(2)}) async-start(bf16[16,384,128]{2,1,0:T(8,128)(2,1)} %get-tuple-element.15), calls=%async_computation | async-start | bytes 3145728 | tf_op jit(solution)/shard_map/all_to_all | solution.py:491
  16.9 23.8 %all-to-all-done.mine_hbm = bf16[16,384,128]{2,1,0:T(8,128)(2,1)S(1)} async-done(((bf16[16,384,128]{2,1,0:T(8,128)(2,1)}), bf16[16,384,128]{2,1,0:T(8,128)(2,1)S(1)}, u32[]{:S(2)}, u32[]{:S(2)}) %all-to-all-start) | async-done | bytes 1572896 | tf_op jit(solution)/shard_map/all_to_all | solution.py:491
  40.7 3.1 %collective-permute-start = (bf16[16,16,128]{2,1,0:T(8,128)(2,1)S(1)}, bf16[16,16,128]{2,1,0:T(8,128)(2,1)S(1)}, u32[]{:S(2)}, u32[]{:S(2)}) collective-permute-start(bf16[16,16,128]{2,1,0:T(8,128)(2,1)S(1)} %slice.8), channel_id=1, source_target_pairs={{0,1},{1,0},{2,3},{3,2},{4,5},{5,4},{6,7},{7,6},{8,9},{9,8},{10,11... | collective-permute-start | bytes 196616 | tf_op jit(solution)/shard_map/ppermute | solution.py:492
  43.8 0.1 slice.9
  43.9 1.1 collective-permute-start.1
  45.0 0.0 copy-done.1
  45.0 7.9 %attend_own_1.1 = (f32[1024,128]{1,0:T(8,128)}, f32[8,128]{1,0:T(8,128)}) custom-call(bf16[16,384,128]{2,1,0:T(8,128)(2,1)} %copy-done.1), custom_call_target="tpu_custom_call" | custom-call | flops 4294967296 | bytes 1048576 | tf_op jit(solution)/shard_map/attend_own_1/pallas_call | solution.py:305
  52.9 0.0 collective-permute-done.picks_ref
  52.9 0.0 copy-start.3
  52.9 0.6 copy-done.3
  53.5 9.1 %attend_picks.1 = (bf16[16,2,32,128]{3,2,1,0:T(8,128)(2,1)}, f32[8,128]{1,0:T(8,128)}) custom-call(bf16[16,384,128]{2,1,0:T(8,128)(2,1)} %copy-done.1, bf16[16,16,128]{2,1,0:T(8,128)(2,1)} %copy-done.3, s32[1]{0:T(128)} %bitcast.1.me_ref, f32[8,128]{1,0:T(8,128)} %get-tuple-element.16.rest_0_), custom_call_target="tpu_custom_call" | custom-call | flops 4294967296 | bytes 1048576 | tf_op jit(solution)/shard_map/attend_picks/pallas_call | solution.py:316
  62.6 6.6 %all-to-all-start.1 = ((bf16[32,32,128]{2,1,0:T(8,128)(2,1)}), bf16[32,32,128]{2,1,0:T(8,128)(2,1)S(1)}, u32[]{:S(2)}, u32[]{:S(2)}) async-start(bf16[32,32,128]{2,1,0:T(8,128)(2,1)} %bitcast.3), calls=%async_computation.1 | async-start | bytes 524288 | tf_op jit(solution)/shard_map/all_to_all | solution.py:496
  69.3 11.1 %attend_own_3.1 = (f32[1536,128]{1,0:T(8,128)}, f32[8,128]{1,0:T(8,128)}) custom-call(bf16[16,384,128]{2,1,0:T(8,128)(2,1)} %copy-done.1, f32[8,128]{1,0:T(8,128)} %get-tuple-element.19.rest_0_), custom_call_target="tpu_custom_call" | custom-call | flops 6442450944 | bytes 1048576 | tf_op jit(solution)/shard_map/attend_own_3/pallas_call | solution.py:305
  80.3 0.0 all-to-all-done.1.part_ref
  80.4 0.7 copy-done.2
  81.1 5.3 %track_rows.1 = (bf16[32,32,1024]{2,1,0:T(8,128)(2,1)}, bf16[32,1024]{1,0:T(8,128)(2,1)}) custom-call(bf16[32,32,128]{2,1,0:T(8,128)(2,1)} %copy-done.2, bf16[256,1024]{1,0:T(8,128)(2,1)} %x_hbm.3, bf16[1024,1024]{1,0:T(8,128)(2,1)} %w_hbm.5, bf16[256,256]{1,0:T(8,128)(2,1)} %get-tuple-element.18.place_ref, s32[1,32]{1,0:T(1,128)} %slots_ref.3, ...), custom_call_target="tpu_custom_call" | custom-call | flops 2147483648 | bytes 4194304 | tf_op jit(solution)/shard_map/track_rows/pallas_call | solution.py:406
  86.4 10.0 %all-to-all-start.2 = ((bf16[32,32,1024]{2,1,0:T(8,128)(2,1)}), bf16[32,32,1024]{2,1,0:T(8,128)(2,1)S(1)}, u32[]{:S(2)}, u32[]{:S(2)}) async-start(bf16[32,32,1024]{2,1,0:T(8,128)(2,1)} %get-tuple-element.25), calls=%async_computation.2 | async-start | bytes 4194304 | tf_op jit(solution)/shard_map/all_to_all | solution.py:503
  96.4 8.8 %attend_own_6.1 = (f32[1024,128]{1,0:T(8,128)}, f32[8,128]{1,0:T(8,128)}) custom-call(bf16[16,384,128]{2,1,0:T(8,128)(2,1)} %copy-done.1, bf16[32,1024]{1,0:T(8,128)(2,1)} %get-tuple-element.21.rest_0_.att1_ref), custom_call_target="tpu_custom_call" | custom-call | flops 4294967296 | bytes 1048576 | tf_op jit(solution)/shard_map/attend_own_6/pallas_call | solution.py:305
  105.2 0.0 collective-permute-done.1.other_hbm
  105.2 22.9 %attend_other.1 = bf16[16,112,128]{2,1,0:T(8,128)(2,1)} custom-call(bf16[16,384,128]{2,1,0:T(8,128)(2,1)} %copy-done.1, bf16[16,256,128]{2,1,0:T(8,128)(2,1)} %collective-permute-done.1.other_hbm, f32[1024,128]{1,0:T(8,128)} %get-tuple-element.22.rest_0_, f32[1536,128]{1,0:T(8,128)} %get-tuple-element.23.rest_1_, f32[1024,128]{1,0:T(8,128)} %get-tuple-element.24.rest_2_), custom_call_target="tpu_custom_call" | custom-call | flops 15032385536 | bytes 1048576 | tf_op jit(solution)/shard_map/attend_other/pallas_call | solution.py:334
  128.1 0.0 all-to-all-done.2.rows_hbm
  128.2 17.0 %all_to_all.20.at2_ref = bf16[16,112,128]{2,1,0:T(8,128)(2,1)} all-to-all(bf16[16,112,128]{2,1,0:T(8,128)(2,1)} %attend_other.1), channel_id=1, replica_groups={{0,2,4,6,8,10,12,14,16,18,20,22,24,26,28,30},{1,3,5,7,9,11,13,15,17,19,..., dimensions={0} | all-to-all | bytes 917504 | tf_op jit(solution)/shard_map/all_to_all | solution.py:507
  145.1 5.9 %finish.1 = (bf16[256,1024]{1,0:T(8,128)(2,1)}, f32[1,32,32,256]{3,2,1,0:T(8,128)}) custom-call(bf16[32,1024]{1,0:T(8,128)(2,1)} %get-tuple-element.21.rest_0_.att1_ref, bf16[16,112,128]{2,1,0:T(8,128)(2,1)} %all_to_all.20.at2_ref, bf16[256,256]{1,0:T(8,128)(2,1)} %get-tuple-element.18.place_ref, bf16[32,32,1024]{2,1,0:T(8,128)(2,1)} %copy-done, ...), custom_call_target="tpu_custom_call" | custom-call | tf_op jit(solution)/shard_map/finish/pallas_call | solution.py:458
  (5 shorter events, 0.0 us)
Async XLA Ops:
  8.7 31.9 %all-to-all-start = ((bf16[16,384,128]{2,1,0:T(8,128)(2,1)}), bf16[16,384,128]{2,1,0:T(8,128)(2,1)S(1)}, u32[]{:S(2)}, u32[]{:S(2)}) async-start(bf16[16,384,128]{2,1,0:T(8,128)(2,1)} %get-tuple-element.15), calls=%async_computation | async-start | bytes 3145728 | tf_op jit(solution)/shard_map/all_to_all | solution.py:491
  40.6 4.3 %copy-start.1 = (bf16[16,384,128]{2,1,0:T(8,128)(2,1)}, bf16[16,384,128]{2,1,0:T(8,128)(2,1)S(1)}, u32[]{:S(2)}) copy-start(bf16[16,384,128]{2,1,0:T(8,128)(2,1)S(1)} %all-to-all-done.mine_hbm) | copy-start | bytes 4718596
  40.7 12.2 %collective-permute-start = (bf16[16,16,128]{2,1,0:T(8,128)(2,1)S(1)}, bf16[16,16,128]{2,1,0:T(8,128)(2,1)S(1)}, u32[]{:S(2)}, u32[]{:S(2)}) collective-permute-start(bf16[16,16,128]{2,1,0:T(8,128)(2,1)S(1)} %slice.8), channel_id=1, source_target_pairs={{0,1},{1,0},{2,3},{3,2},{4,5},{5,4},{6,7},{7,6},{8,9},{9,8},{10,11... | collective-permute-start | bytes 196616 | tf_op jit(solution)/shard_map/ppermute | solution.py:492
  43.9 61.4 %collective-permute-start.1 = (bf16[16,256,128]{2,1,0:T(8,128)(2,1)S(1)}, bf16[16,256,128]{2,1,0:T(8,128)(2,1)}, u32[]{:S(2)}, u32[]{:S(2)}) collective-permute-start(bf16[16,256,128]{2,1,0:T(8,128)(2,1)S(1)} %slice.9), channel_id=1, source_target_pairs={{0,1},{1,0},{2,3},{3,2},{4,5},{5,4},{6,7},{7,6},{8,9},{9,8},{10,11... | collective-permute-start | bytes 3145736 | tf_op jit(solution)/shard_map/ppermute | solution.py:493
  52.9 0.6 copy-start.3
  62.6 17.7 %all-to-all-start.1 = ((bf16[32,32,128]{2,1,0:T(8,128)(2,1)}), bf16[32,32,128]{2,1,0:T(8,128)(2,1)S(1)}, u32[]{:S(2)}, u32[]{:S(2)}) async-start(bf16[32,32,128]{2,1,0:T(8,128)(2,1)} %bitcast.3), calls=%async_computation.1 | async-start | bytes 524288 | tf_op jit(solution)/shard_map/all_to_all | solution.py:496
  80.4 0.7 copy-start.2
  86.4 41.7 %all-to-all-start.2 = ((bf16[32,32,1024]{2,1,0:T(8,128)(2,1)}), bf16[32,32,1024]{2,1,0:T(8,128)(2,1)S(1)}, u32[]{:S(2)}, u32[]{:S(2)}) async-start(bf16[32,32,1024]{2,1,0:T(8,128)(2,1)} %get-tuple-element.25), calls=%async_computation.2 | async-start | bytes 4194304 | tf_op jit(solution)/shard_map/all_to_all | solution.py:503
  128.1 17.0 %copy-start = (bf16[32,32,1024]{2,1,0:T(8,128)(2,1)}, bf16[32,32,1024]{2,1,0:T(8,128)(2,1)S(1)}, u32[]{:S(2)}) copy-start(bf16[32,32,1024]{2,1,0:T(8,128)(2,1)S(1)} %all-to-all-done.2.rows_hbm) | copy-start | bytes 6291460

commit v5 on v3

--- a/solution.py
+++ b/solution.py
@@ -158,7 +158,8 @@
 
 
 def own_kernel(first, mine_ref, *rest):
-    state_ref, va_ref = rest[-2:]
+    state_ref, tick_ref, va_ref = rest[-3:]
+    tick_ref[...] = jnp.zeros_like(tick_ref)
     fill_values(mine_ref, va_ref)
     q = load_queries(mine_ref, pl.program_id(0) + first)
     top, acc = absorb(q, mine_ref, va_ref, None, None)
@@ -182,7 +183,8 @@
 
 
 def picks_kernel(mine_ref, picks_ref, me_ref, *rest):
-    o_ref, va_ref = rest[-2:]
+    o_ref, tick_ref, va_ref = rest[-3:]
+    tick_ref[...] = jnp.zeros_like(tick_ref)
     fill_values(mine_ref, va_ref)
     step = pl.program_id(0)
     own = mine_ref[:, TOK : TOK + CHUNK, :]
@@ -212,22 +214,23 @@
     return dict(
         grid=(chunks,),
         scratch_shapes=[pltpu.VMEM((GROUP, TOK, LANES), BF16)],
-        compiler_params=pltpu.CompilerParams(vmem_limit_bytes=36 << 20),
+        compiler_params=pltpu.CompilerParams(vmem_limit_bytes=20 << 20),
         cost_estimate=pl.CostEstimate(
             flops=2 * pairs * LANES * 4, bytes_accessed=1 << 20, transcendentals=pairs
         ),
     )
 
 
-ANY = pl.BlockSpec(memory_space=pl.ANY)
+HBM = pl.BlockSpec(memory_space=pltpu.HBM)
+TICK = jax.ShapeDtypeStruct((8, LANES), F32)
 
 
 def attend_own(mine, first, last, after=()):
     return pl.pallas_call(
         functools.partial(own_kernel, first),
-        in_specs=[VMEM] + [ANY] * len(after),
-        out_specs=pl.BlockSpec((ROWS, LANES), lambda i: (i, 0)),
-        out_shape=jax.ShapeDtypeStruct(((last - first) * ROWS, LANES), F32),
+        in_specs=[VMEM] + [VMEM if tick.ndim == 2 else HBM for tick in after],
+        out_specs=[pl.BlockSpec((ROWS, LANES), lambda i: (i, 0)), VMEM],
+        out_shape=[jax.ShapeDtypeStruct(((last - first) * ROWS, LANES), F32), TICK],
         name=f"attend_own_{first}",
         **attend_settings(last - first),
     )(mine, *after)
@@ -236,9 +239,9 @@
 def attend_picks(mine, picks, me, after):
     return pl.pallas_call(
         picks_kernel,
-        in_specs=[VMEM, VMEM, SMEM] + [ANY] * len(after),
-        out_specs=VMEM,
-        out_shape=jax.ShapeDtypeStruct((GROUP, 2, QMAX, LANES), BF16),
+        in_specs=[VMEM, VMEM, SMEM] + [VMEM] * len(after),
+        out_specs=[pl.BlockSpec((GROUP, 2, QMAX, LANES), lambda i: (0, 0, 0, 0)), VMEM],
+        out_shape=[jax.ShapeDtypeStruct((GROUP, 2, QMAX, LANES), BF16), TICK],
         name="attend_picks",
         **attend_settings(2),
     )(mine, picks, me, *after)
@@ -257,7 +260,7 @@
         functools.partial(other_kernel, starts),
         in_specs=[VMEM, VMEM]
         + [state_spec(*pair) for pair in zip(starts, counts, strict=True)]
-        + [ANY] * len(after),
+        + [VMEM] * len(after),
         out_specs=pl.BlockSpec((GROUP, CHUNK, LANES), lambda i: (0, i, 0)),
         out_shape=jax.ShapeDtypeStruct((GROUP, chunks * CHUNK, LANES), BF16),
         name="attend_other",
@@ -278,8 +281,10 @@
     return part[:, 0:1] + part[:, 1:2] + part[:, 2:3]
 
 
-def rows_kernel(part_ref, x_ref, w_ref, place_ref, slots_ref, counts_ref, owner_ref, me_ref, *rest):
-    send_ref, att_ref = rest[-2:]
+def rows_kernel(part_ref, w_hbm, zeros_hbm, x_ref, place_ref, slots_ref, counts_ref, owner_ref, me_ref, *rest):
+    send_hbm, att_ref, w_ref, rows_ref, sems = rest[-5:]
+    load_w = pltpu.make_async_copy(w_hbm, w_ref, sems.at[0])
+    load_w.start()
     heads = []
     for h in range(HEADS):
         a, b = part_ref[2 * h].astype(F32), part_ref[2 * h + 1].astype(F32)
@@ -301,68 +306,81 @@
     where = lax.dot_general(token_slot, place_ref[...], TN, preferred_element_type=F32).astype(BF16)
     chosen = jnp.dot(where, placed, preferred_element_type=F32).astype(BF16)
     x = lax.dot_general(token_slot, x_ref[...], TN, preferred_element_type=F32)
+    load_w.wait()
     rows = (x + jnp.dot(chosen, w_ref[...], preferred_element_type=F32)).astype(BF16)
     me = me_ref[0]
     slot = lax.broadcasted_iota(jnp.int32, rows.shape, 0)
-    send_ref[...] = jnp.zeros_like(send_ref)
-    send_ref[owner_ref[me]] = jnp.where(slot < counts_ref[me], rows, jnp.zeros_like(rows))
-
-
-def track_rows(parts, x, w_out, place, slots, counts, owner, me, after):
+    rows_ref[...] = jnp.where(slot < counts_ref[me], rows, jnp.zeros_like(rows))
+    put = pltpu.make_async_copy(rows_ref, send_hbm.at[owner_ref[me]], sems.at[1])
+    put.start()
+    put.wait()
+
+
+def track_rows(parts, w_out, zeros, x, place, slots, counts, owner, me, after):
     return pl.pallas_call(
         rows_kernel,
-        in_specs=[VMEM] * 5 + [SMEM] * 3 + [ANY] * len(after),
-        out_specs=[VMEM, VMEM],
+        in_specs=[VMEM, HBM, HBM] + [VMEM] * 3 + [SMEM] * 3 + [VMEM] * len(after),
+        out_specs=[HBM, VMEM],
+        input_output_aliases={2: 0},
+        scratch_shapes=[
+            pltpu.VMEM((D, D), BF16),
+            pltpu.VMEM((QMAX, D), BF16),
+            pltpu.SemaphoreType.DMA((2,)),
+        ],
         out_shape=[
             jax.ShapeDtypeStruct((FRAMES, QMAX, D), BF16),
             jax.ShapeDtypeStruct((QMAX, D), BF16),
         ],
-        compiler_params=pltpu.CompilerParams(vmem_limit_bytes=20 << 20),
+        compiler_params=pltpu.CompilerParams(vmem_limit_bytes=58 << 20),
         cost_estimate=pl.CostEstimate(flops=2 << 30, bytes_accessed=4 << 20, transcendentals=0),
         name="track_rows",
-    )(parts, x, w_out, place, slots, counts, owner, me, *after)
-
-
-def mix_kernel(att1_ref, at2_ref, x_ref, w_ref, place_ref, mixed_ref):
-    pairs = [(at2_ref[2 * i].astype(F32), at2_ref[2 * i + 1].astype(F32)) for i in range(HEADS // 2)]
-    top, bottom = join_heads(pairs)
-    placed = jnp.concatenate([att1_ref[:CHUNK], top, att1_ref[CHUNK:], bottom], axis=0)
-    att = jnp.dot(place_ref[...], placed, preferred_element_type=F32).astype(BF16)
-    mixed_ref[...] = (
-        x_ref[...].astype(F32) + jnp.dot(att, w_ref[...], preferred_element_type=F32)
-    ).astype(BF16)
-
-
-def mix(att1, att2, x, w_out, place):
-    return pl.pallas_call(
-        mix_kernel,
-        in_specs=[VMEM] * 5,
-        out_specs=VMEM,
-        out_shape=jax.ShapeDtypeStruct((TOK, D), BF16),
-        compiler_params=pltpu.CompilerParams(vmem_limit_bytes=20 << 20),
-        name="mix",
-    )(att1, att2, x, w_out, place)
-
-
-def correlate_kernel(rows_ref, mixed_ref, o_ref):
-    step = o_ref.shape[1]
-    start = pl.program_id(0) * step
-    rows = rows_ref[pl.ds(start, step)].reshape(-1, D)
+    )(parts, w_out, zeros, x, place, slots, counts, owner, me, *after)
+
+
+def finish_kernel(att1_ref, at2_ref, place_ref, rows_ref, x_ref, w_hbm, mixed_ref, corr_ref, w_ref, sems):
+
+    @pl.when(pl.program_id(0) == 0)
+    def _():
+        load_w = pltpu.make_async_copy(w_hbm, w_ref, sems)
+        load_w.start()
+        pairs = [
+            (at2_ref[2 * i].astype(F32), at2_ref[2 * i + 1].astype(F32)) for i in range(HEADS // 2)
+        ]
+        top, bottom = join_heads(pairs)
+        placed = jnp.concatenate([att1_ref[:CHUNK], top, att1_ref[CHUNK:], bottom], axis=0)
+        att = jnp.dot(place_ref[...], placed, preferred_element_type=F32).astype(BF16)
+        load_w.wait()
+        mixed_ref[...] = (
+            x_ref[...].astype(F32) + jnp.dot(att, w_ref[...], preferred_element_type=F32)
+        ).astype(BF16)
+
+    step = corr_ref.shape[1]
+    rows = rows_ref[pl.ds(pl.program_id(0) * step, step)].reshape(-1, D)
     corr = lax.dot_general(rows, mixed_ref[...], NT, preferred_element_type=F32)
-    o_ref[...] = (corr * (1.0 / D**0.5)).reshape(o_ref.shape)
-
-
-def correlate(arrived, mixed):
+    corr_ref[...] = (corr * (1.0 / D**0.5)).reshape(corr_ref.shape)
+
+
+def finish(att1, att2, x, w_out, place, arrived):
     step = 8
     return pl.pallas_call(
-        correlate_kernel,
+        finish_kernel,
         grid=(FRAMES // step,),
-        in_specs=[VMEM, VMEM],
-        out_specs=pl.BlockSpec((1, step, QMAX, TOK), lambda i: (0, i, 0, 0)),
-        out_shape=jax.ShapeDtypeStruct((1, FRAMES, QMAX, TOK), F32),
-        compiler_params=pltpu.CompilerParams(vmem_limit_bytes=20 << 20),
-        name="correlate",
-    )(arrived, mixed)
+        in_specs=[VMEM] * 5 + [HBM],
+        out_specs=[
+            pl.BlockSpec((TOK, D), lambda i: (0, 0)),
+            pl.BlockSpec((1, step, QMAX, TOK), lambda i: (0, i, 0, 0)),
+        ],
+        out_shape=[
+            jax.ShapeDtypeStruct((TOK, D), BF16),
+            jax.ShapeDtypeStruct((1, FRAMES, QMAX, TOK), F32),
+        ],
+        scratch_shapes=[
+            pltpu.VMEM((D, D), BF16),
+            pltpu.SemaphoreType.DMA,
+        ],
+        compiler_params=pltpu.CompilerParams(vmem_limit_bytes=58 << 20),
+        name="finish",
+    )(att1, att2, place, arrived, x, w_out)
 
 
 def per_device(features, norm_gain, w_qkv, w_out, counts, query_index, owner):
@@ -373,22 +391,22 @@
     mine = lax.all_to_all(packed, "frame", 0, 0, tiled=True, axis_index_groups=groups)
     picks = lax.ppermute(mine[:, TOK : TOK + CHUNK], "frame", swap_sides)
     other = lax.ppermute(mine[:, :TOK], "frame", swap_sides)
-    state1 = attend_own(mine, 1, 3)
-    parts = attend_picks(mine, picks, me, [state1])
+    zeros = jnp.zeros((FRAMES, QMAX, D), BF16)
+    state1, tick = attend_own(mine, 1, 3, [zeros])
+    parts, tick = attend_picks(mine, picks, me, [tick])
     parts_here = lax.all_to_all(
         parts.reshape(FRAMES, QMAX, LANES), "frame", 0, 0, tiled=True
     )
-    state2 = attend_own(mine, 3, SPLIT, [parts])
+    state2, tick = attend_own(mine, 3, SPLIT, [tick])
     send, att1 = track_rows(
-        parts_here, features, w_out, place, query_index, counts, owner, me, [state2]
+        parts_here, w_out, zeros, features, place, query_index, counts, owner, me, [tick]
     )
     arrived = lax.all_to_all(send, "frame", 0, 0, tiled=True)
-    state3 = attend_own(mine, SPLIT, CHUNKS, [att1])
+    state3, _ = attend_own(mine, SPLIT, CHUNKS, [att1])
     rest = attend_other(mine, other, [state1, state2, state3])
     rest, arrived = lax.optimization_barrier((rest, arrived))
     att2 = lax.all_to_all(rest, "frame", 0, 0, tiled=True, axis_index_groups=groups)
-    mixed = mix(att1, att2, features, w_out, place)
-    return mixed, correlate(arrived, mixed)
+    return tuple(finish(att1, att2, features, w_out, place, arrived))
 
 
 def solution(mesh):

time: 141 us -> 140 us (level)
  local copies, waits for them, and re-layouts: 10.1 us -> 4.64 us
  Pallas kernels: 60.5 us -> 64.7 us
    unnamed x32 -> x22, local copies, waits for them, and re-layouts: 9.02 us -> 3.34 us
    pallas_call x7 -> x6, Pallas kernels: 31 us -> 36.3 us  [the longest x3 18.7 us: attend_own(): pl.pallas_call(functools.partial(own_kernel, first), in_specs=[VMEM] + [V...]
  transfers between devices with their start and end apart: 5 -> 5, of which waited for: 2 -> 3; matrix products, arithmetic and copies ran while one was open for 1% -> 1% of each run, Pallas kernels for 35% -> 37%
where the time goes in v5:
time: 140 us; the launch traced here: 139 us
  Pallas kernels  64.7 us (46%)
  starting transfers between devices  27.1 us (19%)
  waiting for transfers between devices  25.9 us (18%)
  blocking collectives  15.9 us (11%)
  local copies, waits for them, and re-layouts  4.64 us (3%)
    all_to_all x1, waiting for transfers between devices, per_device(): lax.all_to_all(packed, 'frame', 0, 0, tiled=True, axis_index_groups=groups)  23.8 us
    pallas_call x1, Pallas kernels, attend_other(): pl.pallas_call(functools.partial(other_kernel, starts), in_specs=[VMEM, V...  21.5 us
    pallas_call x3, Pallas kernels, attend_own(): pl.pallas_call(functools.partial(own_kernel, first), in_specs=[VMEM] + [V...  18.7 us
    all_to_all x1, blocking collectives, per_device(): lax.all_to_all(rest, 'frame', 0, 0, tiled=True, axis_index_groups=groups)  15.9 us
    all_to_all x1, starting transfers between devices, per_device(): arrived = lax.all_to_all(send, 'frame', 0, 0, tiled=True)  8.59 us
    all_to_all x1, starting transfers between devices, per_device(): lax.all_to_all(packed, 'frame', 0, 0, tiled=True, axis_index_groups=groups)  8.13 us
    pallas_call x1, Pallas kernels, project(): pl.pallas_call(project_kernel, grid=(steps,), in_specs=[pl.BlockSpec((TOK...  6.99 us
    all_to_all x1, starting transfers between devices, per_device(): lax.all_to_all(parts.reshape(FRAMES, QMAX, LANES), 'frame', 0, 0, tiled=T...  6.81 us
  transfers between devices with their start and end apart: 5, of which 3 were waited for; matrix products, arithmetic and copies ran while one was open for 1% of the time, Pallas kernels for 37%

profile of v5, /device:TPU:0, one launch (start us, length us, event | category | flops | bytes accessed | tf_op | source)
XLA Modules:
  0.0 139.3 jit_solution(15407983427762558278)
XLA Ops:
  0.6 7.0 %project.1 = (bf16[16,384,128]{2,1,0:T(8,128)(2,1)}, bf16[256,256]{1,0:T(8,128)(2,1)}) custom-call(bf16[256,1024]{1,0:T(8,128)(2,1)} %x_ref.5, f32[1,1024]{1,0:T(1,128)} %bitcast.3, s32[1,32]{1,0:T(1,128)} %slots_ref.3, bf16[1024,3072]{1,0:T(8,128)(2,1)} %wv_ref.1, bf16[1024,3072]{1,0:T(8,128)(2,1)} %wv_ref.1, bf16[1024,3072]{1,0:T(8,128)(2,1)} %wv_ref.1), custom_call_target="tpu_custom_call" | custom-call | tf_op jit(solution)/shard_map/project/pallas_call | solution.py:84
  7.6 8.1 %all-to-all-start = ((bf16[16,384,128]{2,1,0:T(8,128)(2,1)}), bf16[16,384,128]{2,1,0:T(8,128)(2,1)S(1)}, u32[]{:S(2)}, u32[]{:S(2)}) async-start(bf16[16,384,128]{2,1,0:T(8,128)(2,1)} %get-tuple-element.15), calls=%async_computation | async-start | bytes 3145728 | tf_op jit(solution)/shard_map/all_to_all | solution.py:391
  15.8 23.8 %all-to-all-done.mine_ref = bf16[16,384,128]{2,1,0:T(8,128)(2,1)S(1)} async-done(((bf16[16,384,128]{2,1,0:T(8,128)(2,1)}), bf16[16,384,128]{2,1,0:T(8,128)(2,1)S(1)}, u32[]{:S(2)}, u32[]{:S(2)}) %all-to-all-start) | async-done | bytes 1572896 | tf_op jit(solution)/shard_map/all_to_all | solution.py:391
  39.6 3.1 %collective-permute-start = (bf16[16,16,128]{2,1,0:T(8,128)(2,1)S(1)}, bf16[16,16,128]{2,1,0:T(8,128)(2,1)S(1)}, u32[]{:S(2)}, u32[]{:S(2)}) collective-permute-start(bf16[16,16,128]{2,1,0:T(8,128)(2,1)S(1)} %slice.8), channel_id=1, source_target_pairs={{0,1},{1,0},{2,3},{3,2},{4,5},{5,4},{6,7},{7,6},{8,9},{9,8},{10,11... | collective-permute-start | bytes 196616 | tf_op jit(solution)/shard_map/ppermute | solution.py:392
  42.7 1.0 slice.9
  43.7 0.5 collective-permute-start.1
  44.2 0.3 broadcast_in_dim.3.rest_0_.zeros_hbm
  44.5 1.1 copy-done.2
  45.6 5.4 %attend_own_1.1 = (f32[1024,128]{1,0:T(8,128)S(1)}, f32[8,128]{1,0:T(8,128)S(1)}) custom-call(bf16[16,384,128]{2,1,0:T(8,128)(2,1)S(1)} %copy-done.2, bf16[32,32,1024]{2,1,0:T(8,128)(2,1)S(1)} %broadcast_in_dim.3.rest_0_.zeros_hbm), custom_call_target="tpu_custom_call" | custom-call | flops 4294967296 | bytes 1048576 | tf_op jit(solution)/shard_map/attend_own_1/pallas_call | solution.py:229
  51.0 0.0 copy-start.5
  51.0 6.4 %attend_picks.1 = (bf16[16,2,32,128]{3,2,1,0:T(8,128)(2,1)}, f32[8,128]{1,0:T(8,128)S(1)}) custom-call(bf16[16,384,128]{2,1,0:T(8,128)(2,1)S(1)} %copy-done.2, bf16[16,16,128]{2,1,0:T(8,128)(2,1)S(1)} %collective-permute-done.picks_ref, s32[1]{0:T(128)} %bitcast.1.me_ref, f32[8,128]{1,0:T(8,128)S(1)} %get-tuple-element.16.rest_0_), custom_call_target="tpu_custom_call" | custom-call | flops 4294967296 | bytes 1048576 | tf_op jit(solution)/shard_map/attend_picks/pallas_call | solution.py:240
  57.4 6.8 %all-to-all-start.1 = ((bf16[32,32,128]{2,1,0:T(8,128)(2,1)}), bf16[32,32,128]{2,1,0:T(8,128)(2,1)S(1)}, u32[]{:S(2)}, u32[]{:S(2)}) async-start(bf16[32,32,128]{2,1,0:T(8,128)(2,1)} %bitcast.2), calls=%async_computation.1 | async-start | bytes 524288 | tf_op jit(solution)/shard_map/all_to_all | solution.py:397
  64.2 8.0 %attend_own_3.1 = (f32[1536,128]{1,0:T(8,128)S(1)}, f32[8,128]{1,0:T(8,128)S(1)}) custom-call(bf16[16,384,128]{2,1,0:T(8,128)(2,1)S(1)} %copy-done.3, f32[8,128]{1,0:T(8,128)S(1)} %get-tuple-element.19.rest_0_), custom_call_target="tpu_custom_call" | custom-call | flops 6442450944 | bytes 1048576 | tf_op jit(solution)/shard_map/attend_own_3/pallas_call | solution.py:229
  72.2 0.9 copy-done.7
  73.1 0.6 copy-done.9
  73.7 1.3 all-to-all-done.1.part_ref
  75.0 0.7 copy-done.10
  75.7 4.6 %track_rows.1 = (bf16[32,32,1024]{2,1,0:T(8,128)(2,1)}, bf16[32,1024]{1,0:T(8,128)(2,1)}) custom-call(bf16[32,32,128]{2,1,0:T(8,128)(2,1)} %copy-done.10, bf16[1024,1024]{1,0:T(8,128)(2,1)} %w_hbm.3, bf16[32,32,1024]{2,1,0:T(8,128)(2,1)} %copy-done, bf16[256,1024]{1,0:T(8,128)(2,1)} %x_ref.5, ...), custom_call_target="tpu_custom_call", output_to_operand_aliasing={{0}: (2, {})} | custom-call | flops 2147483648 | bytes 4194304 | tf_op jit(solution)/shard_map/track_rows/pallas_call | solution.py:320
  80.3 8.6 %all-to-all-start.2 = ((bf16[32,32,1024]{2,1,0:T(8,128)(2,1)}), bf16[32,32,1024]{2,1,0:T(8,128)(2,1)}, u32[]{:S(2)}, u32[]{:S(2)}) async-start(bf16[32,32,1024]{2,1,0:T(8,128)(2,1)} %get-tuple-element.25), calls=%async_computation.2 | async-start | bytes 4194304 | tf_op jit(solution)/shard_map/all_to_all | solution.py:404
  88.9 5.4 %attend_own_6.1 = (f32[1024,128]{1,0:T(8,128)S(1)}, f32[8,128]{1,0:T(8,128)}) custom-call(bf16[16,384,128]{2,1,0:T(8,128)(2,1)S(1)} %copy-done.3, bf16[32,1024]{1,0:T(8,128)(2,1)S(1)} %copy-done.4), custom_call_target="tpu_custom_call" | custom-call | flops 4294967296 | bytes 1048576 | tf_op jit(solution)/shard_map/attend_own_6/pallas_call | solution.py:229
  94.3 21.5 %attend_other.1 = bf16[16,112,128]{2,1,0:T(8,128)(2,1)S(1)} custom-call(bf16[16,384,128]{2,1,0:T(8,128)(2,1)S(1)} %copy-done.3, bf16[16,256,128]{2,1,0:T(8,128)(2,1)S(1)} %collective-permute-done.1.other_ref, f32[1024,128]{1,0:T(8,128)S(1)} %copy-done.6, f32[1536,128]{1,0:T(8,128)S(1)} %copy-done.8, f32[1024,128]{1,0:T(8,128)S(1)} %get-tuple-element.24.rest_2_), custom_call_target="tpu_custom_call" | custom-call | flops 15032385536 | bytes 1048576 | tf_op jit(solution)/shard_map/attend_other/pallas_call | solution.py:259
  115.8 0.8 all-to-all-done.2.rows_ref
  116.6 15.9 %all_to_all.20.at2_ref = bf16[16,112,128]{2,1,0:T(8,128)(2,1)} all-to-all(bf16[16,112,128]{2,1,0:T(8,128)(2,1)S(1)} %attend_other.1), channel_id=1, replica_groups={{0,2,4,6,8,10,12,14,16,18,20,22,24,26,28,30},{1,3,5,7,9,11,13,15,17,19,..., dimensions={0} | all-to-all | bytes 917504 | tf_op jit(solution)/shard_map/all_to_all | solution.py:408
  132.5 6.6 %finish.1 = (bf16[256,1024]{1,0:T(8,128)(2,1)}, f32[1,32,32,256]{3,2,1,0:T(8,128)}) custom-call(bf16[32,1024]{1,0:T(8,128)(2,1)} %get-tuple-element.21.rest_0_.att1_ref, bf16[16,112,128]{2,1,0:T(8,128)(2,1)} %all_to_all.20.at2_ref, bf16[256,256]{1,0:T(8,128)(2,1)} %get-tuple-element.18.place_ref, bf16[32,32,1024]{2,1,0:T(8,128)(2,1)} %all-to-all-done.2.rows_ref, ...), custom_call_target="tpu_custom_call" | custom-call | tf_op jit(solution)/shard_map/finish/pallas_call | solution.py:365
  (20 shorter events, 0.0 us)
Async XLA Ops:
  7.6 31.9 %all-to-all-start = ((bf16[16,384,128]{2,1,0:T(8,128)(2,1)}), bf16[16,384,128]{2,1,0:T(8,128)(2,1)S(1)}, u32[]{:S(2)}, u32[]{:S(2)}) async-start(bf16[16,384,128]{2,1,0:T(8,128)(2,1)} %get-tuple-element.15), calls=%async_computation | async-start | bytes 3145728 | tf_op jit(solution)/shard_map/all_to_all | solution.py:391
  39.5 4.2 %copy-start.1 = (bf16[16,384,128]{2,1,0:T(8,128)(2,1)}, bf16[16,384,128]{2,1,0:T(8,128)(2,1)S(1)}, u32[]{:S(2)}) copy-start(bf16[16,384,128]{2,1,0:T(8,128)(2,1)S(1)} %all-to-all-done.mine_ref) | copy-start | bytes 4718596
  39.6 11.5 %collective-permute-start = (bf16[16,16,128]{2,1,0:T(8,128)(2,1)S(1)}, bf16[16,16,128]{2,1,0:T(8,128)(2,1)S(1)}, u32[]{:S(2)}, u32[]{:S(2)}) collective-permute-start(bf16[16,16,128]{2,1,0:T(8,128)(2,1)S(1)} %slice.8), channel_id=1, source_target_pairs={{0,1},{1,0},{2,3},{3,2},{4,5},{5,4},{6,7},{7,6},{8,9},{9,8},{10,11... | collective-permute-start | bytes 196616 | tf_op jit(solution)/shard_map/ppermute | solution.py:392
  43.7 50.6 %collective-permute-start.1 = (bf16[16,256,128]{2,1,0:T(8,128)(2,1)}, bf16[16,256,128]{2,1,0:T(8,128)(2,1)S(1)}, u32[]{:S(2)}, u32[]{:S(2)}) collective-permute-start(bf16[16,256,128]{2,1,0:T(8,128)(2,1)} %slice.9), channel_id=1, source_target_pairs={{0,1},{1,0},{2,3},{3,2},{4,5},{5,4},{6,7},{7,6},{8,9},{9,8},{10,11... | collective-permute-start | bytes 3145736 | tf_op jit(solution)/shard_map/ppermute | solution.py:393
  44.2 1.4 %copy-start.2 = (bf16[16,384,128]{2,1,0:T(8,128)(2,1)S(1)}, bf16[16,384,128]{2,1,0:T(8,128)(2,1)}, u32[]{:S(2)}) copy-start(bf16[16,384,128]{2,1,0:T(8,128)(2,1)} %copy-done.1) | copy-start | bytes 4718596
  45.6 5.4 %copy-start = (bf16[32,32,1024]{2,1,0:T(8,128)(2,1)}, bf16[32,32,1024]{2,1,0:T(8,128)(2,1)S(1)}, u32[]{:S(2)}) copy-start(bf16[32,32,1024]{2,1,0:T(8,128)(2,1)S(1)} %broadcast_in_dim.3.rest_0_.zeros_hbm) | copy-start | bytes 6291460
  51.0 6.4 %copy-start.5 = (f32[1024,128]{1,0:T(8,128)}, f32[1024,128]{1,0:T(8,128)S(1)}, u32[]{:S(2)}) copy-start(f32[1024,128]{1,0:T(8,128)S(1)} %get-tuple-element.22.rest_0_) | copy-start | bytes 1572868
  51.0 13.2 %copy-start.3 = (bf16[16,384,128]{2,1,0:T(8,128)(2,1)S(1)}, bf16[16,384,128]{2,1,0:T(8,128)(2,1)}, u32[]{:S(2)}) copy-start(bf16[16,384,128]{2,1,0:T(8,128)(2,1)} %copy-done.1) | copy-start | bytes 4718596
  57.4 17.6 %all-to-all-start.1 = ((bf16[32,32,128]{2,1,0:T(8,128)(2,1)}), bf16[32,32,128]{2,1,0:T(8,128)(2,1)S(1)}, u32[]{:S(2)}, u32[]{:S(2)}) async-start(bf16[32,32,128]{2,1,0:T(8,128)(2,1)} %bitcast.2), calls=%async_computation.1 | async-start | bytes 524288 | tf_op jit(solution)/shard_map/all_to_all | solution.py:397
  72.2 0.9 copy-start.7
  73.1 0.6 copy-start.9
  75.0 0.7 copy-start.10
  80.3 8.6 %copy-start.4 = (bf16[32,1024]{1,0:T(8,128)(2,1)S(1)}, bf16[32,1024]{1,0:T(8,128)(2,1)}, u32[]{:S(2)}) copy-start(bf16[32,1024]{1,0:T(8,128)(2,1)} %get-tuple-element.21.rest_0_.att1_ref) | copy-start | bytes 196612
  80.3 36.3 %all-to-all-start.2 = ((bf16[32,32,1024]{2,1,0:T(8,128)(2,1)}), bf16[32,32,1024]{2,1,0:T(8,128)(2,1)}, u32[]{:S(2)}, u32[]{:S(2)}) async-start(bf16[32,32,1024]{2,1,0:T(8,128)(2,1)} %get-tuple-element.25), calls=%async_computation.2 | async-start | bytes 4194304 | tf_op jit(solution)/shard_map/all_to_all | solution.py:404
  88.9 5.4 %copy-start.6 = (f32[1024,128]{1,0:T(8,128)S(1)}, f32[1024,128]{1,0:T(8,128)}, u32[]{:S(2)}) copy-start(f32[1024,128]{1,0:T(8,128)} %copy-done.5) | copy-start | bytes 1572868
  88.9 5.4 %copy-start.8 = (f32[1536,128]{1,0:T(8,128)S(1)}, f32[1536,128]{1,0:T(8,128)}, u32[]{:S(2)}) copy-start(f32[1536,128]{1,0:T(8,128)} %copy-done.7) | copy-start | bytes 2359300

commit v6 on v5

--- a/solution.py
+++ b/solution.py
@@ -49,9 +49,20 @@
     return jnp.where(place == col, 1.0, 0.0).astype(BF16)
 
 
-def project_kernel(x_ref, g_ref, slots_ref, wq_ref, wk_ref, wv_ref, o_ref, place_ref, n_ref):
-    @pl.when(pl.program_id(0) == 0)
+STEPS = 4
+WIDTH = D // STEPS
+
+
+def project_kernel(x_ref, g_ref, slots_ref, w_hbm, o_ref, place_ref, n_ref, w_ref, sems):
+    step = pl.program_id(0)
+
+    @pl.when(step == 0)
     def _():
+        loads = []
+        for i in range(STEPS):
+            rows = pl.ds(i * WIDTH, WIDTH)
+            loads.append(pltpu.make_async_copy(w_hbm.at[rows], w_ref.at[rows], sems.at[i]))
+            loads[i].start()
         place = arrange(slots_ref[...])
         place_ref[...] = place
         xf = x_ref[...].astype(F32)
@@ -60,15 +71,22 @@
         var = jnp.mean(cen * cen, axis=-1, keepdims=True)
         normed = (cen * lax.rsqrt(var + 1e-05) * g_ref[...]).astype(BF16)
         n_ref[...] = lax.dot_general(place, normed, TN, preferred_element_type=F32).astype(BF16)
+        for load in loads:
+            load.wait()
 
     n = n_ref[...]
-    q = jnp.dot(n, wq_ref[...], preferred_element_type=F32) * (1.0 / HDIM**0.5)
-    k = jnp.dot(n, wk_ref[...], preferred_element_type=F32)
-    v = jnp.dot(n, wv_ref[...], preferred_element_type=F32)
+
+    def product(part):
+        cols = pl.ds(pl.multiple_of(part * D + step * WIDTH, WIDTH), WIDTH)
+        return jnp.dot(n, w_ref[:, cols], preferred_element_type=F32)
+
+    q = product(0) * (1.0 / HDIM**0.5)
+    k = product(1)
+    v = product(2)
     half = TOK // 2
     low = low_half(TOK)
     lowh = low_half(half)
-    for c in range(wq_ref.shape[1] // LANES):
+    for c in range(WIDTH // LANES):
         cols = slice(c * LANES, (c + 1) * LANES)
         kp, vp = k[:, cols], v[:, cols]
         qa, qb = q[:half, cols], q[half:, cols]
@@ -79,31 +97,32 @@
 
 
 def project(x, gain, slots, w_qkv):
-    steps = 4
-    width = D // steps
+    rows = TOK + TOK // 2
     return pl.pallas_call(
         project_kernel,
-        grid=(steps,),
+        grid=(STEPS,),
         in_specs=[
             pl.BlockSpec((TOK, D), lambda i: (0, 0)),
             pl.BlockSpec((1, D), lambda i: (0, 0)),
             pl.BlockSpec((1, QMAX), lambda i: (0, 0)),
-            pl.BlockSpec((D, width), lambda i: (0, i)),
-            pl.BlockSpec((D, width), lambda i: (0, i + steps)),
-            pl.BlockSpec((D, width), lambda i: (0, i + 2 * steps)),
+            pl.BlockSpec(memory_space=pl.ANY),
         ],
         out_specs=[
-            pl.BlockSpec((HEADS // steps, TOK + TOK // 2, LANES), lambda i: (i, 0, 0)),
+            pl.BlockSpec((HEADS // STEPS, rows, LANES), lambda i: (i, 0, 0)),
             pl.BlockSpec((TOK, TOK), lambda i: (0, 0)),
         ],
         out_shape=[
-            jax.ShapeDtypeStruct((HEADS, TOK + TOK // 2, LANES), BF16),
+            jax.ShapeDtypeStruct((HEADS, rows, LANES), BF16),
             jax.ShapeDtypeStruct((TOK, TOK), BF16),
         ],
-        scratch_shapes=[pltpu.VMEM((TOK, D), BF16)],
+        scratch_shapes=[
+            pltpu.VMEM((TOK, D), BF16),
+            pltpu.VMEM((D, 3 * D), BF16),
+            pltpu.SemaphoreType.DMA((STEPS,)),
+        ],
         compiler_params=pltpu.CompilerParams(vmem_limit_bytes=60 << 20),
         name="project",
-    )(x, gain.reshape(1, D), slots, w_qkv, w_qkv, w_qkv)
+    )(x, gain.reshape(1, D), slots, w_qkv)
 
 
 BLOCK_FRAMES = 4
@@ -228,7 +247,7 @@
 def attend_own(mine, first, last, after=()):
     return pl.pallas_call(
         functools.partial(own_kernel, first),
-        in_specs=[VMEM] + [VMEM if tick.ndim == 2 else HBM for tick in after],
+        in_specs=[VMEM] * (1 + len(after)),
         out_specs=[pl.BlockSpec((ROWS, LANES), lambda i: (i, 0)), VMEM],
         out_shape=[jax.ShapeDtypeStruct(((last - first) * ROWS, LANES), F32), TICK],
         name=f"attend_own_{first}",
@@ -281,7 +300,7 @@
     return part[:, 0:1] + part[:, 1:2] + part[:, 2:3]
 
 
-def rows_kernel(part_ref, w_hbm, zeros_hbm, x_ref, place_ref, slots_ref, counts_ref, owner_ref, me_ref, *rest):
+def rows_kernel(part_ref, w_hbm, x_ref, place_ref, slots_ref, counts_ref, owner_ref, me_ref, *rest):
     send_hbm, att_ref, w_ref, rows_ref, sems = rest[-5:]
     load_w = pltpu.make_async_copy(w_hbm, w_ref, sems.at[0])
     load_w.start()
@@ -316,12 +335,11 @@
     put.wait()
 
 
-def track_rows(parts, w_out, zeros, x, place, slots, counts, owner, me, after):
+def track_rows(parts, w_out, x, place, slots, counts, owner, me, after):
     return pl.pallas_call(
         rows_kernel,
-        in_specs=[VMEM, HBM, HBM] + [VMEM] * 3 + [SMEM] * 3 + [VMEM] * len(after),
+        in_specs=[VMEM, HBM] + [VMEM] * 3 + [SMEM] * 3 + [HBM] * len(after),
         out_specs=[HBM, VMEM],
-        input_output_aliases={2: 0},
         scratch_shapes=[
             pltpu.VMEM((D, D), BF16),
             pltpu.VMEM((QMAX, D), BF16),
@@ -334,38 +352,56 @@
         compiler_params=pltpu.CompilerParams(vmem_limit_bytes=58 << 20),
         cost_estimate=pl.CostEstimate(flops=2 << 30, bytes_accessed=4 << 20, transcendentals=0),
         name="track_rows",
-    )(parts, w_out, zeros, x, place, slots, counts, owner, me, *after)
-
-
-def finish_kernel(att1_ref, at2_ref, place_ref, rows_ref, x_ref, w_hbm, mixed_ref, corr_ref, w_ref, sems):
+    )(parts, w_out, x, place, slots, counts, owner, me, *after)
+
+
+def finish_kernel(
+    att1_ref, at2_ref, place_ref, owner_ref, me_ref, rows_hbm, x_hbm, w_hbm, mixed_ref, corr_ref, x_ref, w_ref, rows_ref, sems
+):
+    load_rows = pltpu.make_async_copy(rows_hbm, rows_ref, sems.at[2])
 
     @pl.when(pl.program_id(0) == 0)
     def _():
-        load_w = pltpu.make_async_copy(w_hbm, w_ref, sems)
+        load_w = pltpu.make_async_copy(w_hbm, w_ref, sems.at[0])
+        load_x = pltpu.make_async_copy(x_hbm, x_ref, sems.at[1])
         load_w.start()
+        load_x.start()
+        load_rows.start()
         pairs = [
             (at2_ref[2 * i].astype(F32), at2_ref[2 * i + 1].astype(F32)) for i in range(HEADS // 2)
         ]
         top, bottom = join_heads(pairs)
         placed = jnp.concatenate([att1_ref[:CHUNK], top, att1_ref[CHUNK:], bottom], axis=0)
         att = jnp.dot(place_ref[...], placed, preferred_element_type=F32).astype(BF16)
+        load_x.wait()
         load_w.wait()
         mixed_ref[...] = (
             x_ref[...].astype(F32) + jnp.dot(att, w_ref[...], preferred_element_type=F32)
         ).astype(BF16)
+        load_rows.wait()
 
     step = corr_ref.shape[1]
-    rows = rows_ref[pl.ds(pl.program_id(0) * step, step)].reshape(-1, D)
+    first = pl.program_id(0) * step
+    rows = rows_ref[pl.ds(first, step)].reshape(-1, D)
     corr = lax.dot_general(rows, mixed_ref[...], NT, preferred_element_type=F32)
-    corr_ref[...] = (corr * (1.0 / D**0.5)).reshape(corr_ref.shape)
-
-
-def finish(att1, att2, x, w_out, place, arrived):
+    corr = (corr * (1.0 / D**0.5)).reshape(step, QMAX, TOK)
+    for i in range(step):
+        owned = owner_ref[first + i] == me_ref[0]
+        corr_ref[0, i] = jnp.where(owned, corr[i], jnp.zeros_like(corr[i]))
+
+
+def finish(att1, att2, x, w_out, place, owner, me, arrived):
     step = 8
     return pl.pallas_call(
         finish_kernel,
         grid=(FRAMES // step,),
-        in_specs=[VMEM] * 5 + [HBM],
+        in_specs=[
+            pl.BlockSpec(att1.shape, lambda i: (0, 0)),
+            pl.BlockSpec(att2.shape, lambda i: (0, 0, 0)),
+            pl.BlockSpec(place.shape, lambda i: (0, 0)),
+        ]
+        + [SMEM] * 2
+        + [HBM] * 3,
         out_specs=[
             pl.BlockSpec((TOK, D), lambda i: (0, 0)),
             pl.BlockSpec((1, step, QMAX, TOK), lambda i: (0, i, 0, 0)),
@@ -375,12 +411,14 @@
             jax.ShapeDtypeStruct((1, FRAMES, QMAX, TOK), F32),
         ],
         scratch_shapes=[
+            pltpu.VMEM((TOK, D), BF16),
             pltpu.VMEM((D, D), BF16),
-            pltpu.SemaphoreType.DMA,
+            pltpu.VMEM((FRAMES, QMAX, D), BF16),
+            pltpu.SemaphoreType.DMA((3,)),
         ],
         compiler_params=pltpu.CompilerParams(vmem_limit_bytes=58 << 20),
         name="finish",
-    )(att1, att2, place, arrived, x, w_out)
+    )(att1, att2, place, owner, me, arrived, x, w_out)
 
 
 def per_device(features, norm_gain, w_qkv, w_out, counts, query_index, owner):
@@ -391,22 +429,21 @@
     mine = lax.all_to_all(packed, "frame", 0, 0, tiled=True, axis_index_groups=groups)
     picks = lax.ppermute(mine[:, TOK : TOK + CHUNK], "frame", swap_sides)
     other = lax.ppermute(mine[:, :TOK], "frame", swap_sides)
-    zeros = jnp.zeros((FRAMES, QMAX, D), BF16)
-    state1, tick = attend_own(mine, 1, 3, [zeros])
+    state1, tick = attend_own(mine, 1, 3)
     parts, tick = attend_picks(mine, picks, me, [tick])
     parts_here = lax.all_to_all(
         parts.reshape(FRAMES, QMAX, LANES), "frame", 0, 0, tiled=True
     )
-    state2, tick = attend_own(mine, 3, SPLIT, [tick])
+    state2, _ = attend_own(mine, 3, SPLIT, [tick])
     send, att1 = track_rows(
-        parts_here, w_out, zeros, features, place, query_index, counts, owner, me, [tick]
+        parts_here, w_out, features, place, query_index, counts, owner, me, [state2]
     )
     arrived = lax.all_to_all(send, "frame", 0, 0, tiled=True)
     state3, _ = attend_own(mine, SPLIT, CHUNKS, [att1])
     rest = attend_other(mine, other, [state1, state2, state3])
     rest, arrived = lax.optimization_barrier((rest, arrived))
     att2 = lax.all_to_all(rest, "frame", 0, 0, tiled=True, axis_index_groups=groups)
-    return tuple(finish(att1, att2, features, w_out, place, arrived))
+    return tuple(finish(att1, att2, features, w_out, place, owner, me, arrived))
 
 
 def solution(mesh):

time: 140 us -> 138 us (0.986)
  local copies, waits for them, and re-layouts: 4.64 us -> 2.65 us
    unnamed x22 -> x12, local copies, waits for them, and re-layouts: 3.34 us -> 1.6 us
where the time goes in v6:
time: 138 us; the launch traced here: 137 us
  Pallas kernels  64.6 us (47%)
  starting transfers between devices  26.6 us (19%)
  waiting for transfers between devices  26.5 us (19%)
  blocking collectives  15.9 us (12%)
  local copies, waits for them, and re-layouts  2.65 us (2%)
    all_to_all x1, waiting for transfers between devices, per_device(): lax.all_to_all(packed, 'frame', 0, 0, tiled=True, axis_index_groups=groups)  23.8 us
    pallas_call x1, Pallas kernels, attend_other(): pl.pallas_call(functools.partial(other_kernel, starts), in_specs=[VMEM, V...  21.5 us
    pallas_call x3, Pallas kernels, attend_own(): pl.pallas_call(functools.partial(own_kernel, first), in_specs=[VMEM] * (1...  18.7 us
    all_to_all x1, blocking collectives, per_device(): lax.all_to_all(rest, 'frame', 0, 0, tiled=True, axis_index_groups=groups)  15.9 us
    all_to_all x1, starting transfers between devices, per_device(): lax.all_to_all(packed, 'frame', 0, 0, tiled=True, axis_index_groups=groups)  8.15 us
    all_to_all x1, starting transfers between devices, per_device(): arrived = lax.all_to_all(send, 'frame', 0, 0, tiled=True)  8 us
    pallas_call x1, Pallas kernels, project(): pl.pallas_call(project_kernel, grid=(STEPS,), in_specs=[pl.BlockSpec((TOK...  7.58 us
    all_to_all x1, starting transfers between devices, per_device(): lax.all_to_all(parts.reshape(FRAMES, QMAX, LANES), 'frame', 0, 0, tiled=T...  6.81 us
  transfers between devices with their start and end apart: 5, of which 3 were waited for; matrix products, arithmetic and copies ran while one was open for 1% of the time, Pallas kernels for 37%

profile of v6, /device:TPU:0, one launch (start us, length us, event | category | flops | bytes accessed | tf_op | source)
XLA Modules:
  0.0 137.1 jit_solution(10123217308503693170)
XLA Ops:
  0.6 7.6 %project.1 = (bf16[16,384,128]{2,1,0:T(8,128)(2,1)}, bf16[256,256]{1,0:T(8,128)(2,1)}) custom-call(bf16[256,1024]{1,0:T(8,128)(2,1)} %x_hbm.1, f32[1,1024]{1,0:T(1,128)} %bitcast.3, s32[1,32]{1,0:T(1,128)} %slots_ref.3, bf16[1024,3072]{1,0:T(8,128)(2,1)} %w_hbm.3), custom_call_target="tpu_custom_call" | custom-call | tf_op jit(solution)/shard_map/project/pallas_call | solution.py:101
  8.2 8.1 %all-to-all-start = ((bf16[16,384,128]{2,1,0:T(8,128)(2,1)}), bf16[16,384,128]{2,1,0:T(8,128)(2,1)S(1)}, u32[]{:S(2)}, u32[]{:S(2)}) async-start(bf16[16,384,128]{2,1,0:T(8,128)(2,1)} %get-tuple-element.14), calls=%async_computation | async-start | bytes 3145728 | tf_op jit(solution)/shard_map/all_to_all | solution.py:429
  16.4 23.8 %all-to-all-done.mine_ref = bf16[16,384,128]{2,1,0:T(8,128)(2,1)S(1)} async-done(((bf16[16,384,128]{2,1,0:T(8,128)(2,1)}), bf16[16,384,128]{2,1,0:T(8,128)(2,1)S(1)}, u32[]{:S(2)}, u32[]{:S(2)}) %all-to-all-start) | async-done | bytes 1572896 | tf_op jit(solution)/shard_map/all_to_all | solution.py:429
  40.2 3.1 %collective-permute-start = (bf16[16,16,128]{2,1,0:T(8,128)(2,1)S(1)}, bf16[16,16,128]{2,1,0:T(8,128)(2,1)S(1)}, u32[]{:S(2)}, u32[]{:S(2)}) collective-permute-start(bf16[16,16,128]{2,1,0:T(8,128)(2,1)S(1)} %slice.8), channel_id=1, source_target_pairs={{0,1},{1,0},{2,3},{3,2},{4,5},{5,4},{6,7},{7,6},{8,9},{9,8},{10,11... | collective-permute-start | bytes 196616 | tf_op jit(solution)/shard_map/ppermute | solution.py:430
  43.3 1.0 slice.9
  44.3 0.5 collective-permute-start.1
  44.8 5.4 %attend_own_1.1 = (f32[1024,128]{1,0:T(8,128)S(1)}, f32[8,128]{1,0:T(8,128)S(1)}) custom-call(bf16[16,384,128]{2,1,0:T(8,128)(2,1)S(1)} %all-to-all-done.mine_ref), custom_call_target="tpu_custom_call" | custom-call | flops 4294967296 | bytes 1048576 | tf_op jit(solution)/shard_map/attend_own_1/pallas_call | solution.py:248
  50.2 0.0 copy-start.3
  50.2 0.0 collective-permute-done.picks_ref
  50.2 6.4 %attend_picks.1 = (bf16[16,2,32,128]{3,2,1,0:T(8,128)(2,1)}, f32[8,128]{1,0:T(8,128)S(1)}) custom-call(bf16[16,384,128]{2,1,0:T(8,128)(2,1)S(1)} %all-to-all-done.mine_ref, bf16[16,16,128]{2,1,0:T(8,128)(2,1)S(1)} %collective-permute-done.picks_ref, s32[1]{0:T(128)} %bitcast.1.me_ref, f32[8,128]{1,0:T(8,128)S(1)} %get-tuple-element.15.rest_0_), custom_call_target="tpu_custom_call" | custom-call | flops 4294967296 | bytes 1048576 | tf_op jit(solution)/shard_map/attend_picks/pallas_call | solution.py:259
  56.6 6.8 %all-to-all-start.1 = ((bf16[32,32,128]{2,1,0:T(8,128)(2,1)}), bf16[32,32,128]{2,1,0:T(8,128)(2,1)S(1)}, u32[]{:S(2)}, u32[]{:S(2)}) async-start(bf16[32,32,128]{2,1,0:T(8,128)(2,1)} %bitcast.2), calls=%async_computation.1 | async-start | bytes 524288 | tf_op jit(solution)/shard_map/all_to_all | solution.py:434
  63.4 8.0 %attend_own_3.1 = (f32[1536,128]{1,0:T(8,128)S(1)}, f32[8,128]{1,0:T(8,128)}) custom-call(bf16[16,384,128]{2,1,0:T(8,128)(2,1)S(1)} %all-to-all-done.mine_ref, f32[8,128]{1,0:T(8,128)S(1)} %get-tuple-element.18.rest_0_), custom_call_target="tpu_custom_call" | custom-call | flops 6442450944 | bytes 1048576 | tf_op jit(solution)/shard_map/attend_own_3/pallas_call | solution.py:248
  71.4 0.9 copy-done.1
  72.3 1.9 %all-to-all-done.1.part_ref = bf16[32,32,128]{2,1,0:T(8,128)(2,1)S(1)} async-done(((bf16[32,32,128]{2,1,0:T(8,128)(2,1)}), bf16[32,32,128]{2,1,0:T(8,128)(2,1)S(1)}, u32[]{:S(2)}, u32[]{:S(2)}) %all-to-all-start.1) | async-done | bytes 262176 | tf_op jit(solution)/shard_map/all_to_all | solution.py:434
  74.2 0.7 copy-done.5
  74.9 4.6 %track_rows.1 = (bf16[32,32,1024]{2,1,0:T(8,128)(2,1)}, bf16[32,1024]{1,0:T(8,128)(2,1)}) custom-call(bf16[32,32,128]{2,1,0:T(8,128)(2,1)} %copy-done.5, bf16[1024,1024]{1,0:T(8,128)(2,1)} %w_hbm.5, bf16[256,1024]{1,0:T(8,128)(2,1)} %x_hbm.1, bf16[256,256]{1,0:T(8,128)(2,1)} %get-tuple-element.17.place_ref, s32[1,32]{1,0:T(1,128)} %slots_ref.3, ...), custom_call_target="tpu_custom_call" | custom-call | flops 2147483648 | bytes 4194304 | tf_op jit(solution)/shard_map/track_rows/pallas_call | solution.py:339
  79.4 8.0 %all-to-all-start.2 = ((bf16[32,32,1024]{2,1,0:T(8,128)(2,1)}), bf16[32,32,1024]{2,1,0:T(8,128)(2,1)}, u32[]{:S(2)}, u32[]{:S(2)}) async-start(bf16[32,32,1024]{2,1,0:T(8,128)(2,1)} %get-tuple-element.23), calls=%async_computation.2 | async-start | bytes 4194304 | tf_op jit(solution)/shard_map/all_to_all | solution.py:441
  87.5 0.0 copy-start.4
  87.5 5.4 %attend_own_6.1 = (f32[1024,128]{1,0:T(8,128)S(1)}, f32[8,128]{1,0:T(8,128)}) custom-call(bf16[16,384,128]{2,1,0:T(8,128)(2,1)S(1)} %all-to-all-done.mine_ref, bf16[32,1024]{1,0:T(8,128)(2,1)S(1)} %copy-done), custom_call_target="tpu_custom_call" | custom-call | flops 4294967296 | bytes 1048576 | tf_op jit(solution)/shard_map/attend_own_6/pallas_call | solution.py:248
  92.9 0.0 collective-permute-done.1.other_ref
  92.9 21.5 %attend_other.1 = bf16[16,112,128]{2,1,0:T(8,128)(2,1)S(1)} custom-call(bf16[16,384,128]{2,1,0:T(8,128)(2,1)S(1)} %all-to-all-done.mine_ref, bf16[16,256,128]{2,1,0:T(8,128)(2,1)S(1)} %collective-permute-done.1.other_ref, f32[1024,128]{1,0:T(8,128)S(1)} %copy-done.4, f32[1536,128]{1,0:T(8,128)S(1)} %copy-done.2, f32[1024,128]{1,0:T(8,128)S(1)} %get-tuple-element.22.rest_2_), custom_call_target="tpu_custom_call" | custom-call | flops 15032385536 | bytes 1048576 | tf_op jit(solution)/shard_map/attend_other/pallas_call | solution.py:278
  114.4 0.8 all-to-all-done.2.rows_hbm
  115.2 15.9 %all_to_all.20.at2_ref = bf16[16,112,128]{2,1,0:T(8,128)(2,1)} all-to-all(bf16[16,112,128]{2,1,0:T(8,128)(2,1)S(1)} %attend_other.1), channel_id=1, replica_groups={{0,2,4,6,8,10,12,14,16,18,20,22,24,26,28,30},{1,3,5,7,9,11,13,15,17,19,..., dimensions={0} | all-to-all | bytes 917504 | tf_op jit(solution)/shard_map/all_to_all | solution.py:445
  131.0 6.0 %finish.1 = (bf16[256,1024]{1,0:T(8,128)(2,1)}, f32[1,32,32,256]{3,2,1,0:T(8,128)}) custom-call(bf16[32,1024]{1,0:T(8,128)(2,1)} %get-tuple-element.20.rest_0_.att1_ref, bf16[16,112,128]{2,1,0:T(8,128)(2,1)} %all_to_all.20.at2_ref, bf16[256,256]{1,0:T(8,128)(2,1)} %get-tuple-element.17.place_ref, s32[32]{0:T(128)} %owner_ref.3, s32[1]{0:T(128)} %bitcast.1.me_ref, ...), custom_call_target="tpu_custom_call" | custom-call | tf_op jit(solution)/shard_map/finish/pallas_call | solution.py:395
  (9 shorter events, 0.0 us)
Async XLA Ops:
  8.2 31.9 %all-to-all-start = ((bf16[16,384,128]{2,1,0:T(8,128)(2,1)}), bf16[16,384,128]{2,1,0:T(8,128)(2,1)S(1)}, u32[]{:S(2)}, u32[]{:S(2)}) async-start(bf16[16,384,128]{2,1,0:T(8,128)(2,1)} %get-tuple-element.14), calls=%async_computation | async-start | bytes 3145728 | tf_op jit(solution)/shard_map/all_to_all | solution.py:429
  40.2 10.0 %collective-permute-start = (bf16[16,16,128]{2,1,0:T(8,128)(2,1)S(1)}, bf16[16,16,128]{2,1,0:T(8,128)(2,1)S(1)}, u32[]{:S(2)}, u32[]{:S(2)}) collective-permute-start(bf16[16,16,128]{2,1,0:T(8,128)(2,1)S(1)} %slice.8), channel_id=1, source_target_pairs={{0,1},{1,0},{2,3},{3,2},{4,5},{5,4},{6,7},{7,6},{8,9},{9,8},{10,11... | collective-permute-start | bytes 196616 | tf_op jit(solution)/shard_map/ppermute | solution.py:430
  44.3 48.6 %collective-permute-start.1 = (bf16[16,256,128]{2,1,0:T(8,128)(2,1)}, bf16[16,256,128]{2,1,0:T(8,128)(2,1)S(1)}, u32[]{:S(2)}, u32[]{:S(2)}) collective-permute-start(bf16[16,256,128]{2,1,0:T(8,128)(2,1)} %slice.9), channel_id=1, source_target_pairs={{0,1},{1,0},{2,3},{3,2},{4,5},{5,4},{6,7},{7,6},{8,9},{9,8},{10,11... | collective-permute-start | bytes 3145736 | tf_op jit(solution)/shard_map/ppermute | solution.py:431
  50.2 6.4 %copy-start.3 = (f32[1024,128]{1,0:T(8,128)}, f32[1024,128]{1,0:T(8,128)S(1)}, u32[]{:S(2)}) copy-start(f32[1024,128]{1,0:T(8,128)S(1)} %get-tuple-element.21.rest_0_) | copy-start | bytes 1572868
  56.6 17.6 %all-to-all-start.1 = ((bf16[32,32,128]{2,1,0:T(8,128)(2,1)}), bf16[32,32,128]{2,1,0:T(8,128)(2,1)S(1)}, u32[]{:S(2)}, u32[]{:S(2)}) async-start(bf16[32,32,128]{2,1,0:T(8,128)(2,1)} %bitcast.2), calls=%async_computation.1 | async-start | bytes 524288 | tf_op jit(solution)/shard_map/all_to_all | solution.py:434
  71.4 0.9 copy-start.1
  74.2 0.7 copy-start.5
  79.4 8.0 %copy-start = (bf16[32,1024]{1,0:T(8,128)(2,1)S(1)}, bf16[32,1024]{1,0:T(8,128)(2,1)}, u32[]{:S(2)}) copy-start(bf16[32,1024]{1,0:T(8,128)(2,1)} %get-tuple-element.20.rest_0_.att1_ref) | copy-start | bytes 196612
  79.4 35.7 %all-to-all-start.2 = ((bf16[32,32,1024]{2,1,0:T(8,128)(2,1)}), bf16[32,32,1024]{2,1,0:T(8,128)(2,1)}, u32[]{:S(2)}, u32[]{:S(2)}) async-start(bf16[32,32,1024]{2,1,0:T(8,128)(2,1)} %get-tuple-element.23), calls=%async_computation.2 | async-start | bytes 4194304 | tf_op jit(solution)/shard_map/all_to_all | solution.py:441
  87.4 5.4 %copy-start.2 = (f32[1536,128]{1,0:T(8,128)S(1)}, f32[1536,128]{1,0:T(8,128)}, u32[]{:S(2)}) copy-start(f32[1536,128]{1,0:T(8,128)} %copy-done.1) | copy-start | bytes 2359300
  87.5 5.4 %copy-start.4 = (f32[1024,128]{1,0:T(8,128)S(1)}, f32[1024,128]{1,0:T(8,128)}, u32[]{:S(2)}) copy-start(f32[1024,128]{1,0:T(8,128)} %copy-done.3) | copy-start | bytes 1572868

commit v7 on v6

--- a/solution.py
+++ b/solution.py
@@ -49,20 +49,9 @@
     return jnp.where(place == col, 1.0, 0.0).astype(BF16)
 
 
-STEPS = 4
-WIDTH = D // STEPS
-
-
-def project_kernel(x_ref, g_ref, slots_ref, w_hbm, o_ref, place_ref, n_ref, w_ref, sems):
-    step = pl.program_id(0)
-
-    @pl.when(step == 0)
+def project_kernel(x_ref, g_ref, slots_ref, wq_ref, wk_ref, wv_ref, o_ref, place_ref, n_ref):
+    @pl.when(pl.program_id(0) == 0)
     def _():
-        loads = []
-        for i in range(STEPS):
-            rows = pl.ds(i * WIDTH, WIDTH)
-            loads.append(pltpu.make_async_copy(w_hbm.at[rows], w_ref.at[rows], sems.at[i]))
-            loads[i].start()
         place = arrange(slots_ref[...])
         place_ref[...] = place
         xf = x_ref[...].astype(F32)
@@ -71,22 +60,15 @@
         var = jnp.mean(cen * cen, axis=-1, keepdims=True)
         normed = (cen * lax.rsqrt(var + 1e-05) * g_ref[...]).astype(BF16)
         n_ref[...] = lax.dot_general(place, normed, TN, preferred_element_type=F32).astype(BF16)
-        for load in loads:
-            load.wait()
 
     n = n_ref[...]
-
-    def product(part):
-        cols = pl.ds(pl.multiple_of(part * D + step * WIDTH, WIDTH), WIDTH)
-        return jnp.dot(n, w_ref[:, cols], preferred_element_type=F32)
-
-    q = product(0) * (1.0 / HDIM**0.5)
-    k = product(1)
-    v = product(2)
+    q = jnp.dot(n, wq_ref[...], preferred_element_type=F32) * (1.0 / HDIM**0.5)
+    k = jnp.dot(n, wk_ref[...], preferred_element_type=F32)
+    v = jnp.dot(n, wv_ref[...], preferred_element_type=F32)
     half = TOK // 2
     low = low_half(TOK)
     lowh = low_half(half)
-    for c in range(WIDTH // LANES):
+    for c in range(wq_ref.shape[1] // LANES):
         cols = slice(c * LANES, (c + 1) * LANES)
         kp, vp = k[:, cols], v[:, cols]
         qa, qb = q[:half, cols], q[half:, cols]
@@ -97,32 +79,31 @@
 
 
 def project(x, gain, slots, w_qkv):
-    rows = TOK + TOK // 2
+    steps = 4
+    width = D // steps
     return pl.pallas_call(
         project_kernel,
-        grid=(STEPS,),
+        grid=(steps,),
         in_specs=[
             pl.BlockSpec((TOK, D), lambda i: (0, 0)),
             pl.BlockSpec((1, D), lambda i: (0, 0)),
             pl.BlockSpec((1, QMAX), lambda i: (0, 0)),
-            pl.BlockSpec(memory_space=pl.ANY),
+            pl.BlockSpec((D, width), lambda i: (0, i)),
+            pl.BlockSpec((D, width), lambda i: (0, i + steps)),
+            pl.BlockSpec((D, width), lambda i: (0, i + 2 * steps)),
         ],
         out_specs=[
-            pl.BlockSpec((HEADS // STEPS, rows, LANES), lambda i: (i, 0, 0)),
+            pl.BlockSpec((HEADS // steps, TOK + TOK // 2, LANES), lambda i: (i, 0, 0)),
             pl.BlockSpec((TOK, TOK), lambda i: (0, 0)),
         ],
         out_shape=[
-            jax.ShapeDtypeStruct((HEADS, rows, LANES), BF16),
+            jax.ShapeDtypeStruct((HEADS, TOK + TOK // 2, LANES), BF16),
             jax.ShapeDtypeStruct((TOK, TOK), BF16),
         ],
-        scratch_shapes=[
-            pltpu.VMEM((TOK, D), BF16),
-            pltpu.VMEM((D, 3 * D), BF16),
-            pltpu.SemaphoreType.DMA((STEPS,)),
-        ],
+        scratch_shapes=[pltpu.VMEM((TOK, D), BF16)],
         compiler_params=pltpu.CompilerParams(vmem_limit_bytes=60 << 20),
         name="project",
-    )(x, gain.reshape(1, D), slots, w_qkv)
+    )(x, gain.reshape(1, D), slots, w_qkv, w_qkv, w_qkv)
 
 
 BLOCK_FRAMES = 4
@@ -349,7 +330,7 @@
             jax.ShapeDtypeStruct((FRAMES, QMAX, D), BF16),
             jax.ShapeDtypeStruct((QMAX, D), BF16),
         ],
-        compiler_params=pltpu.CompilerParams(vmem_limit_bytes=58 << 20),
+        compiler_params=pltpu.CompilerParams(vmem_limit_bytes=52 << 20),
         cost_estimate=pl.CostEstimate(flops=2 << 30, bytes_accessed=4 << 20, transcendentals=0),
         name="track_rows",
     )(parts, w_out, x, place, slots, counts, owner, me, *after)
@@ -429,12 +410,12 @@
     mine = lax.all_to_all(packed, "frame", 0, 0, tiled=True, axis_index_groups=groups)
     picks = lax.ppermute(mine[:, TOK : TOK + CHUNK], "frame", swap_sides)
     other = lax.ppermute(mine[:, :TOK], "frame", swap_sides)
-    state1, tick = attend_own(mine, 1, 3)
+    state1, tick = attend_own(mine, 1, 2)
     parts, tick = attend_picks(mine, picks, me, [tick])
     parts_here = lax.all_to_all(
         parts.reshape(FRAMES, QMAX, LANES), "frame", 0, 0, tiled=True
     )
-    state2, _ = attend_own(mine, 3, SPLIT, [tick])
+    state2, _ = attend_own(mine, 2, SPLIT, [tick])
     send, att1 = track_rows(
         parts_here, w_out, features, place, query_index, counts, owner, me, [state2]
     )

time: 138 us -> 136 us (0.986)
  waiting for transfers between devices: 26.5 us -> 23.8 us
  starting transfers between devices: 26.6 us -> 28.3 us
    all_to_all x1, waiting for transfers between devices: 1.89 us -> 0.02 us  [per_device(): lax.all_to_all(parts.reshape(FRAMES, QMAX, LANES), 'frame', 0, 0, tiled=T...]
    all_to_all x1, starting transfers between devices: 8 us -> 9.75 us  [per_device(): arrived = lax.all_to_all(send, 'frame', 0, 0, tiled=True)]
  transfers between devices with their start and end apart: 5 -> 5, of which waited for: 3 -> 1; matrix products, arithmetic and copies ran while one was open for 1% -> 1% of each run, Pallas kernels for 37% -> 38%
where the time goes in v7:
time: 136 us
  Pallas kernels  63.9 us (47%)
  starting transfers between devices  28.3 us (21%)
  waiting for transfers between devices  23.8 us (18%)
  blocking collectives  16.7 us (12%)
  local copies, waits for them, and re-layouts  2.06 us (2%)
    all_to_all x1, waiting for transfers between devices, per_device(): lax.all_to_all(packed, 'frame', 0, 0, tiled=True, axis_index_groups=groups)  23.8 us
    pallas_call x1, Pallas kernels, attend_other(): pl.pallas_call(functools.partial(other_kernel, starts), in_specs=[VMEM, V...  22.5 us
    pallas_call x3, Pallas kernels, attend_own(): pl.pallas_call(functools.partial(own_kernel, first), in_specs=[VMEM] * (1...  18.7 us
    all_to_all x1, blocking collectives, per_device(): lax.all_to_all(rest, 'frame', 0, 0, tiled=True, axis_index_groups=groups)  16.7 us
    all_to_all x1, starting transfers between devices, per_device(): arrived = lax.all_to_all(send, 'frame', 0, 0, tiled=True)  9.75 us
    all_to_all x1, starting transfers between devices, per_device(): lax.all_to_all(packed, 'frame', 0, 0, tiled=True, axis_index_groups=groups)  8.13 us
    pallas_call x1, Pallas kernels, project(): pl.pallas_call(project_kernel, grid=(steps,), in_specs=[pl.BlockSpec((TOK...  6.99 us
    all_to_all x1, starting transfers between devices, per_device(): lax.all_to_all(parts.reshape(FRAMES, QMAX, LANES), 'frame', 0, 0, tiled=T...  6.81 us
  transfers between devices with their start and end apart: 5, of which 1 were waited for; matrix products, arithmetic and copies ran while one was open for 1% of the time, Pallas kernels for 38%

profile of v7, /device:TPU:0, one launch (start us, length us, event | category | flops | bytes accessed | tf_op | source)
XLA Modules:
  0.0 135.8 jit_solution(1229156567662205319)
XLA Ops:
  0.6 7.0 %project.1 = (bf16[16,384,128]{2,1,0:T(8,128)(2,1)}, bf16[256,256]{1,0:T(8,128)(2,1)}) custom-call(bf16[256,1024]{1,0:T(8,128)(2,1)} %x_hbm.1, f32[1,1024]{1,0:T(1,128)} %bitcast.3, s32[1,32]{1,0:T(1,128)} %slots_ref.3, bf16[1024,3072]{1,0:T(8,128)(2,1)} %wv_ref.1, bf16[1024,3072]{1,0:T(8,128)(2,1)} %wv_ref.1, bf16[1024,3072]{1,0:T(8,128)(2,1)} %wv_ref.1), custom_call_target="tpu_custom_call" | custom-call | tf_op jit(solution)/shard_map/project/pallas_call | solution.py:84
  7.6 8.1 %all-to-all-start = ((bf16[16,384,128]{2,1,0:T(8,128)(2,1)}), bf16[16,384,128]{2,1,0:T(8,128)(2,1)S(1)}, u32[]{:S(2)}, u32[]{:S(2)}) async-start(bf16[16,384,128]{2,1,0:T(8,128)(2,1)} %get-tuple-element.14), calls=%async_computation | async-start | bytes 3145728 | tf_op jit(solution)/shard_map/all_to_all | solution.py:410
  15.8 23.8 %all-to-all-done.mine_ref = bf16[16,384,128]{2,1,0:T(8,128)(2,1)S(1)} async-done(((bf16[16,384,128]{2,1,0:T(8,128)(2,1)}), bf16[16,384,128]{2,1,0:T(8,128)(2,1)S(1)}, u32[]{:S(2)}, u32[]{:S(2)}) %all-to-all-start) | async-done | bytes 1572896 | tf_op jit(solution)/shard_map/all_to_all | solution.py:410
  39.5 3.1 %collective-permute-start = (bf16[16,16,128]{2,1,0:T(8,128)(2,1)S(1)}, bf16[16,16,128]{2,1,0:T(8,128)(2,1)S(1)}, u32[]{:S(2)}, u32[]{:S(2)}) collective-permute-start(bf16[16,16,128]{2,1,0:T(8,128)(2,1)S(1)} %slice.8), channel_id=1, source_target_pairs={{0,1},{1,0},{2,3},{3,2},{4,5},{5,4},{6,7},{7,6},{8,9},{9,8},{10,11... | collective-permute-start | bytes 196616 | tf_op jit(solution)/shard_map/ppermute | solution.py:411
  42.7 1.0 slice.9
  43.7 0.5 collective-permute-start.1
  44.2 2.8 %attend_own_1.1 = (f32[512,128]{1,0:T(8,128)S(1)}, f32[8,128]{1,0:T(8,128)S(1)}) custom-call(bf16[16,384,128]{2,1,0:T(8,128)(2,1)S(1)} %all-to-all-done.mine_ref), custom_call_target="tpu_custom_call" | custom-call | flops 2147483648 | bytes 1048576 | tf_op jit(solution)/shard_map/attend_own_1/pallas_call | solution.py:229
  47.0 6.4 %attend_picks.1 = (bf16[16,2,32,128]{3,2,1,0:T(8,128)(2,1)}, f32[8,128]{1,0:T(8,128)S(1)}) custom-call(bf16[16,384,128]{2,1,0:T(8,128)(2,1)S(1)} %all-to-all-done.mine_ref, bf16[16,16,128]{2,1,0:T(8,128)(2,1)S(1)} %collective-permute-done.picks_ref, s32[1]{0:T(128)} %bitcast.1.me_ref, f32[8,128]{1,0:T(8,128)S(1)} %get-tuple-element.15.rest_0_), custom_call_target="tpu_custom_call" | custom-call | flops 4294967296 | bytes 1048576 | tf_op jit(solution)/shard_map/attend_picks/pallas_call | solution.py:240
  53.4 6.8 %all-to-all-start.1 = ((bf16[32,32,128]{2,1,0:T(8,128)(2,1)}), bf16[32,32,128]{2,1,0:T(8,128)(2,1)S(1)}, u32[]{:S(2)}, u32[]{:S(2)}) async-start(bf16[32,32,128]{2,1,0:T(8,128)(2,1)} %bitcast.2), calls=%async_computation.1 | async-start | bytes 524288 | tf_op jit(solution)/shard_map/all_to_all | solution.py:415
  60.2 0.0 copy-start
  60.2 0.0 copy-start.3
  60.3 0.0 copy-start.4
  60.3 0.0 copy-start.5
  60.3 10.6 %attend_own_2.1 = (f32[2048,128]{1,0:T(8,128)S(1)}, f32[8,128]{1,0:T(8,128)}) custom-call(bf16[16,384,128]{2,1,0:T(8,128)(2,1)S(1)} %all-to-all-done.mine_ref, f32[8,128]{1,0:T(8,128)S(1)} %get-tuple-element.18.rest_0_), custom_call_target="tpu_custom_call" | custom-call | flops 8589934592 | bytes 1048576 | tf_op jit(solution)/shard_map/attend_own_2/pallas_call | solution.py:229
  70.9 0.0 copy-start.6
  70.9 1.0 copy-done.6
  71.8 0.0 all-to-all-done.1.part_ref
  71.9 3.3 %track_rows.1 = (bf16[32,32,1024]{2,1,0:T(8,128)(2,1)}, bf16[32,1024]{1,0:T(8,128)(2,1)S(1)}) custom-call(bf16[32,32,128]{2,1,0:T(8,128)(2,1)S(1)} %all-to-all-done.1.part_ref, bf16[1024,1024]{1,0:T(8,128)(2,1)} %w_hbm.3, bf16[256,1024]{1,0:T(8,128)(2,1)S(1)} %copy-done, bf16[256,256]{1,0:T(8,128)(2,1)S(1)} %copy-done.1, s32[1,32]{1,0:T(1,128)S(1)} %copy-done.3, ...), custom_call_target="tpu_custom_call" | custom-call | flops 2147483648 | bytes 4194304 | tf_op jit(solution)/shard_map/track_rows/pallas_call | solution.py:320
  75.2 9.7 %all-to-all-start.2 = ((bf16[32,32,1024]{2,1,0:T(8,128)(2,1)}), bf16[32,32,1024]{2,1,0:T(8,128)(2,1)}, u32[]{:S(2)}, u32[]{:S(2)}) async-start(bf16[32,32,1024]{2,1,0:T(8,128)(2,1)} %get-tuple-element.23), calls=%async_computation.2 | async-start | bytes 4194304 | tf_op jit(solution)/shard_map/all_to_all | solution.py:422
  85.0 0.0 copy-start.7
  85.0 5.4 %attend_own_6.1 = (f32[1024,128]{1,0:T(8,128)S(1)}, f32[8,128]{1,0:T(8,128)}) custom-call(bf16[16,384,128]{2,1,0:T(8,128)(2,1)S(1)} %all-to-all-done.mine_ref, bf16[32,1024]{1,0:T(8,128)(2,1)S(1)} %get-tuple-element.20.rest_0_.att1_ref), custom_call_target="tpu_custom_call" | custom-call | flops 4294967296 | bytes 1048576 | tf_op jit(solution)/shard_map/attend_own_6/pallas_call | solution.py:229
  90.4 22.5 %attend_other.1 = bf16[16,112,128]{2,1,0:T(8,128)(2,1)S(1)} custom-call(bf16[16,384,128]{2,1,0:T(8,128)(2,1)S(1)} %all-to-all-done.mine_ref, bf16[16,256,128]{2,1,0:T(8,128)(2,1)} %collective-permute-done.1.other_ref, f32[512,128]{1,0:T(8,128)S(1)} %get-tuple-element.21.rest_0_, f32[2048,128]{1,0:T(8,128)S(1)} %copy-done.7, ...), custom_call_target="tpu_custom_call" | custom-call | flops 15032385536 | bytes 1048576 | tf_op jit(solution)/shard_map/attend_other/pallas_call | solution.py:259
  113.0 16.7 %all_to_all.20.at2_ref = bf16[16,112,128]{2,1,0:T(8,128)(2,1)} all-to-all(bf16[16,112,128]{2,1,0:T(8,128)(2,1)S(1)} %attend_other.1), channel_id=1, replica_groups={{0,2,4,6,8,10,12,14,16,18,20,22,24,26,28,30},{1,3,5,7,9,11,13,15,17,19,..., dimensions={0} | all-to-all | bytes 917504 | tf_op jit(solution)/shard_map/all_to_all | solution.py:426
  129.6 6.0 %finish.1 = (bf16[256,1024]{1,0:T(8,128)(2,1)}, f32[1,32,32,256]{3,2,1,0:T(8,128)}) custom-call(bf16[32,1024]{1,0:T(8,128)(2,1)} %copy-done.2, bf16[16,112,128]{2,1,0:T(8,128)(2,1)} %all_to_all.20.at2_ref, bf16[256,256]{1,0:T(8,128)(2,1)} %get-tuple-element.17.place_ref, s32[32]{0:T(128)} %owner_ref.3, s32[1]{0:T(128)} %bitcast.1.me_ref, ...), custom_call_target="tpu_custom_call" | custom-call | tf_op jit(solution)/shard_map/finish/pallas_call | solution.py:376
  (13 shorter events, 0.0 us)
Async XLA Ops:
  7.6 31.9 %all-to-all-start = ((bf16[16,384,128]{2,1,0:T(8,128)(2,1)}), bf16[16,384,128]{2,1,0:T(8,128)(2,1)S(1)}, u32[]{:S(2)}, u32[]{:S(2)}) async-start(bf16[16,384,128]{2,1,0:T(8,128)(2,1)} %get-tuple-element.14), calls=%async_computation | async-start | bytes 3145728 | tf_op jit(solution)/shard_map/all_to_all | solution.py:410
  39.5 7.4 %collective-permute-start = (bf16[16,16,128]{2,1,0:T(8,128)(2,1)S(1)}, bf16[16,16,128]{2,1,0:T(8,128)(2,1)S(1)}, u32[]{:S(2)}, u32[]{:S(2)}) collective-permute-start(bf16[16,16,128]{2,1,0:T(8,128)(2,1)S(1)} %slice.8), channel_id=1, source_target_pairs={{0,1},{1,0},{2,3},{3,2},{4,5},{5,4},{6,7},{7,6},{8,9},{9,8},{10,11... | collective-permute-start | bytes 196616 | tf_op jit(solution)/shard_map/ppermute | solution.py:411
  43.7 46.7 %collective-permute-start.1 = (bf16[16,256,128]{2,1,0:T(8,128)(2,1)}, bf16[16,256,128]{2,1,0:T(8,128)(2,1)}, u32[]{:S(2)}, u32[]{:S(2)}) collective-permute-start(bf16[16,256,128]{2,1,0:T(8,128)(2,1)} %slice.9), channel_id=1, source_target_pairs={{0,1},{1,0},{2,3},{3,2},{4,5},{5,4},{6,7},{7,6},{8,9},{9,8},{10,11... | collective-permute-start | bytes 3145736 | tf_op jit(solution)/shard_map/ppermute | solution.py:412
  53.4 18.4 %all-to-all-start.1 = ((bf16[32,32,128]{2,1,0:T(8,128)(2,1)}), bf16[32,32,128]{2,1,0:T(8,128)(2,1)S(1)}, u32[]{:S(2)}, u32[]{:S(2)}) async-start(bf16[32,32,128]{2,1,0:T(8,128)(2,1)} %bitcast.2), calls=%async_computation.1 | async-start | bytes 524288 | tf_op jit(solution)/shard_map/all_to_all | solution.py:415
  60.2 11.6 %copy-start = (bf16[256,1024]{1,0:T(8,128)(2,1)S(1)}, bf16[256,1024]{1,0:T(8,128)(2,1)}, u32[]{:S(2)}) copy-start(bf16[256,1024]{1,0:T(8,128)(2,1)} %x_hbm.1) | copy-start | bytes 1572868
  60.2 11.6 %copy-start.1 = (bf16[256,256]{1,0:T(8,128)(2,1)S(1)}, bf16[256,256]{1,0:T(8,128)(2,1)}, u32[]{:S(2)}) copy-start(bf16[256,256]{1,0:T(8,128)(2,1)} %get-tuple-element.17.place_ref) | copy-start | bytes 393220
  60.2 11.6 %copy-start.3 = (s32[1,32]{1,0:T(1,128)S(1)}, s32[1,32]{1,0:T(1,128)}, u32[]{:S(2)}) copy-start(s32[1,32]{1,0:T(1,128)} %slots_ref.3) | copy-start | bytes 388
  60.3 11.6 %copy-start.4 = (s32[32]{0:T(128)S(1)}, s32[32]{0:T(128)}, u32[]{:S(2)}) copy-start(s32[32]{0:T(128)} %owner_ref.3) | copy-start | bytes 388
  60.3 11.6 %copy-start.5 = (s32[32]{0:T(128)S(1)}, s32[32]{0:T(128)}, u32[]{:S(2)}) copy-start(s32[32]{0:T(128)} %counts_ref.1) | copy-start | bytes 388
  70.9 1.0 copy-start.6
  75.2 9.8 %copy-start.2 = (bf16[32,1024]{1,0:T(8,128)(2,1)}, bf16[32,1024]{1,0:T(8,128)(2,1)S(1)}, u32[]{:S(2)}) copy-start(bf16[32,1024]{1,0:T(8,128)(2,1)S(1)} %get-tuple-element.20.rest_0_.att1_ref) | copy-start | bytes 196612
  75.2 37.7 %all-to-all-start.2 = ((bf16[32,32,1024]{2,1,0:T(8,128)(2,1)}), bf16[32,32,1024]{2,1,0:T(8,128)(2,1)}, u32[]{:S(2)}, u32[]{:S(2)}) async-start(bf16[32,32,1024]{2,1,0:T(8,128)(2,1)} %get-tuple-element.23), calls=%async_computation.2 | async-start | bytes 4194304 | tf_op jit(solution)/shard_map/all_to_all | solution.py:422
  85.0 5.4 %copy-start.7 = (f32[2048,128]{1,0:T(8,128)S(1)}, f32[2048,128]{1,0:T(8,128)}, u32[]{:S(2)}) copy-start(f32[2048,128]{1,0:T(8,128)} %copy-done.6) | copy-start | bytes 3145732

commit v8 on v7

--- a/solution.py
+++ b/solution.py
@@ -337,29 +337,35 @@
 
 
 def finish_kernel(
-    att1_ref, at2_ref, place_ref, owner_ref, me_ref, rows_hbm, x_hbm, w_hbm, mixed_ref, corr_ref, x_ref, w_ref, rows_ref, sems
+    owner_ref, me_ref, att1_hbm, at2_hbm, place_hbm, w_hbm, x_hbm, rows_hbm, mixed_ref, corr_ref, *scratch
 ):
-    load_rows = pltpu.make_async_copy(rows_hbm, rows_ref, sems.at[2])
+    att1_ref, at2_ref, place_ref, w_ref, x_ref, rows_ref, sems = scratch
 
     @pl.when(pl.program_id(0) == 0)
     def _():
-        load_w = pltpu.make_async_copy(w_hbm, w_ref, sems.at[0])
-        load_x = pltpu.make_async_copy(x_hbm, x_ref, sems.at[1])
-        load_w.start()
-        load_x.start()
-        load_rows.start()
+        sources = (at2_hbm, att1_hbm, place_hbm, w_hbm, x_hbm, rows_hbm)
+        targets = (at2_ref, att1_ref, place_ref, w_ref, x_ref, rows_ref)
+        loads = [
+            pltpu.make_async_copy(source, target, sems.at[n])
+            for n, (source, target) in enumerate(zip(sources, targets, strict=True))
+        ]
+        for load in loads:
+            load.start()
+        loads[0].wait()
         pairs = [
             (at2_ref[2 * i].astype(F32), at2_ref[2 * i + 1].astype(F32)) for i in range(HEADS // 2)
         ]
         top, bottom = join_heads(pairs)
+        loads[1].wait()
+        loads[2].wait()
         placed = jnp.concatenate([att1_ref[:CHUNK], top, att1_ref[CHUNK:], bottom], axis=0)
         att = jnp.dot(place_ref[...], placed, preferred_element_type=F32).astype(BF16)
-        load_x.wait()
-        load_w.wait()
+        loads[3].wait()
+        loads[4].wait()
         mixed_ref[...] = (
             x_ref[...].astype(F32) + jnp.dot(att, w_ref[...], preferred_element_type=F32)
         ).astype(BF16)
-        load_rows.wait()
+        loads[5].wait()
 
     step = corr_ref.shape[1]
     first = pl.program_id(0) * step
@@ -372,17 +378,11 @@
 
 
 def finish(att1, att2, x, w_out, place, owner, me, arrived):
-    step = 8
+    step = 16
     return pl.pallas_call(
         finish_kernel,
         grid=(FRAMES // step,),
-        in_specs=[
-            pl.BlockSpec(att1.shape, lambda i: (0, 0)),
-            pl.BlockSpec(att2.shape, lambda i: (0, 0, 0)),
-            pl.BlockSpec(place.shape, lambda i: (0, 0)),
-        ]
-        + [SMEM] * 2
-        + [HBM] * 3,
+        in_specs=[SMEM] * 2 + [HBM] * 6,
         out_specs=[
             pl.BlockSpec((TOK, D), lambda i: (0, 0)),
             pl.BlockSpec((1, step, QMAX, TOK), lambda i: (0, i, 0, 0)),
@@ -392,14 +392,12 @@
             jax.ShapeDtypeStruct((1, FRAMES, QMAX, TOK), F32),
         ],
         scratch_shapes=[
-            pltpu.VMEM((TOK, D), BF16),
-            pltpu.VMEM((D, D), BF16),
-            pltpu.VMEM((FRAMES, QMAX, D), BF16),
-            pltpu.SemaphoreType.DMA((3,)),
-        ],
+            pltpu.VMEM(array.shape, array.dtype) for array in (att1, att2, place, w_out, x, arrived)
+        ]
+        + [pltpu.SemaphoreType.DMA((6,))],
         compiler_params=pltpu.CompilerParams(vmem_limit_bytes=58 << 20),
         name="finish",
-    )(att1, att2, place, owner, me, arrived, x, w_out)
+    )(owner, me, att1, att2, place, w_out, x, arrived)
 
 
 def per_device(features, norm_gain, w_qkv, w_out, counts, query_index, owner):

time: 136 us -> 136 us (level)
  no operation moved by 1% of the time
where the time goes in v8:
time: 136 us; the launch traced here: 135 us
  Pallas kernels  63.2 us (46%)
  starting transfers between devices  28.3 us (21%)
  waiting for transfers between devices  23.8 us (18%)
  blocking collectives  16.7 us (12%)
  local copies, waits for them, and re-layouts  2.06 us (2%)
    all_to_all x1, waiting for transfers between devices, per_device(): lax.all_to_all(packed, 'frame', 0, 0, tiled=True, axis_index_groups=groups)  23.8 us
    pallas_call x1, Pallas kernels, attend_other(): pl.pallas_call(functools.partial(other_kernel, starts), in_specs=[VMEM, V...  22.5 us
    pallas_call x3, Pallas kernels, attend_own(): pl.pallas_call(functools.partial(own_kernel, first), in_specs=[VMEM] * (1...  18.7 us
    all_to_all x1, blocking collectives, per_device(): lax.all_to_all(rest, 'frame', 0, 0, tiled=True, axis_index_groups=groups)  16.7 us
    all_to_all x1, starting transfers between devices, per_device(): arrived = lax.all_to_all(send, 'frame', 0, 0, tiled=True)  9.75 us
    all_to_all x1, starting transfers between devices, per_device(): lax.all_to_all(packed, 'frame', 0, 0, tiled=True, axis_index_groups=groups)  8.13 us
    pallas_call x1, Pallas kernels, project(): pl.pallas_call(project_kernel, grid=(steps,), in_specs=[pl.BlockSpec((TOK...  6.99 us
    all_to_all x1, starting transfers between devices, per_device(): lax.all_to_all(parts.reshape(FRAMES, QMAX, LANES), 'frame', 0, 0, tiled=T...  6.81 us
  transfers between devices with their start and end apart: 5, of which 1 were waited for; matrix products, arithmetic and copies ran while one was open for 1% of the time, Pallas kernels for 38%

profile of v8, /device:TPU:0, one launch (start us, length us, event | category | flops | bytes accessed | tf_op | source)
XLA Modules:
  0.0 135.0 jit_solution(17599152317331672766)
XLA Ops:
  0.6 7.0 %project.1 = (bf16[16,384,128]{2,1,0:T(8,128)(2,1)}, bf16[256,256]{1,0:T(8,128)(2,1)}) custom-call(bf16[256,1024]{1,0:T(8,128)(2,1)} %x_hbm.1, f32[1,1024]{1,0:T(1,128)} %bitcast.3, s32[1,32]{1,0:T(1,128)} %slots_ref.3, bf16[1024,3072]{1,0:T(8,128)(2,1)} %wv_ref.1, bf16[1024,3072]{1,0:T(8,128)(2,1)} %wv_ref.1, bf16[1024,3072]{1,0:T(8,128)(2,1)} %wv_ref.1), custom_call_target="tpu_custom_call" | custom-call | tf_op jit(solution)/shard_map/project/pallas_call | solution.py:84
  7.6 8.1 %all-to-all-start = ((bf16[16,384,128]{2,1,0:T(8,128)(2,1)}), bf16[16,384,128]{2,1,0:T(8,128)(2,1)S(1)}, u32[]{:S(2)}, u32[]{:S(2)}) async-start(bf16[16,384,128]{2,1,0:T(8,128)(2,1)} %get-tuple-element.14), calls=%async_computation | async-start | bytes 3145728 | tf_op jit(solution)/shard_map/all_to_all | solution.py:408
  15.8 23.8 %all-to-all-done.mine_ref = bf16[16,384,128]{2,1,0:T(8,128)(2,1)S(1)} async-done(((bf16[16,384,128]{2,1,0:T(8,128)(2,1)}), bf16[16,384,128]{2,1,0:T(8,128)(2,1)S(1)}, u32[]{:S(2)}, u32[]{:S(2)}) %all-to-all-start) | async-done | bytes 1572896 | tf_op jit(solution)/shard_map/all_to_all | solution.py:408
  39.5 3.1 %collective-permute-start = (bf16[16,16,128]{2,1,0:T(8,128)(2,1)S(1)}, bf16[16,16,128]{2,1,0:T(8,128)(2,1)S(1)}, u32[]{:S(2)}, u32[]{:S(2)}) collective-permute-start(bf16[16,16,128]{2,1,0:T(8,128)(2,1)S(1)} %slice.8), channel_id=1, source_target_pairs={{0,1},{1,0},{2,3},{3,2},{4,5},{5,4},{6,7},{7,6},{8,9},{9,8},{10,11... | collective-permute-start | bytes 196616 | tf_op jit(solution)/shard_map/ppermute | solution.py:409
  42.7 1.0 slice.9
  43.7 0.5 collective-permute-start.1
  44.2 2.8 %attend_own_1.1 = (f32[512,128]{1,0:T(8,128)S(1)}, f32[8,128]{1,0:T(8,128)S(1)}) custom-call(bf16[16,384,128]{2,1,0:T(8,128)(2,1)S(1)} %all-to-all-done.mine_ref), custom_call_target="tpu_custom_call" | custom-call | flops 2147483648 | bytes 1048576 | tf_op jit(solution)/shard_map/attend_own_1/pallas_call | solution.py:229
  47.0 6.4 %attend_picks.1 = (bf16[16,2,32,128]{3,2,1,0:T(8,128)(2,1)}, f32[8,128]{1,0:T(8,128)S(1)}) custom-call(bf16[16,384,128]{2,1,0:T(8,128)(2,1)S(1)} %all-to-all-done.mine_ref, bf16[16,16,128]{2,1,0:T(8,128)(2,1)S(1)} %collective-permute-done.picks_ref, s32[1]{0:T(128)} %bitcast.me_ref, f32[8,128]{1,0:T(8,128)S(1)} %get-tuple-element.15.rest_0_), custom_call_target="tpu_custom_call" | custom-call | flops 4294967296 | bytes 1048576 | tf_op jit(solution)/shard_map/attend_picks/pallas_call | solution.py:240
  53.4 6.8 %all-to-all-start.1 = ((bf16[32,32,128]{2,1,0:T(8,128)(2,1)}), bf16[32,32,128]{2,1,0:T(8,128)(2,1)S(1)}, u32[]{:S(2)}, u32[]{:S(2)}) async-start(bf16[32,32,128]{2,1,0:T(8,128)(2,1)} %bitcast.2), calls=%async_computation.1 | async-start | bytes 524288 | tf_op jit(solution)/shard_map/all_to_all | solution.py:413
  60.2 0.0 copy-start
  60.2 0.0 copy-start.3
  60.3 0.0 copy-start.4
  60.3 0.0 copy-start.5
  60.3 10.6 %attend_own_2.1 = (f32[2048,128]{1,0:T(8,128)S(1)}, f32[8,128]{1,0:T(8,128)}) custom-call(bf16[16,384,128]{2,1,0:T(8,128)(2,1)S(1)} %all-to-all-done.mine_ref, f32[8,128]{1,0:T(8,128)S(1)} %get-tuple-element.18.rest_0_), custom_call_target="tpu_custom_call" | custom-call | flops 8589934592 | bytes 1048576 | tf_op jit(solution)/shard_map/attend_own_2/pallas_call | solution.py:229
  70.9 0.0 copy-start.6
  70.9 1.0 copy-done.6
  71.8 0.0 all-to-all-done.1.part_ref
  71.9 3.3 %track_rows.1 = (bf16[32,32,1024]{2,1,0:T(8,128)(2,1)}, bf16[32,1024]{1,0:T(8,128)(2,1)S(1)}) custom-call(bf16[32,32,128]{2,1,0:T(8,128)(2,1)S(1)} %all-to-all-done.1.part_ref, bf16[1024,1024]{1,0:T(8,128)(2,1)} %w_hbm.3, bf16[256,1024]{1,0:T(8,128)(2,1)S(1)} %copy-done, bf16[256,256]{1,0:T(8,128)(2,1)S(1)} %copy-done.1, s32[1,32]{1,0:T(1,128)S(1)} %copy-done.3, ...), custom_call_target="tpu_custom_call" | custom-call | flops 2147483648 | bytes 4194304 | tf_op jit(solution)/shard_map/track_rows/pallas_call | solution.py:320
  75.2 9.8 %all-to-all-start.2 = ((bf16[32,32,1024]{2,1,0:T(8,128)(2,1)}), bf16[32,32,1024]{2,1,0:T(8,128)(2,1)}, u32[]{:S(2)}, u32[]{:S(2)}) async-start(bf16[32,32,1024]{2,1,0:T(8,128)(2,1)} %get-tuple-element.23), calls=%async_computation.2 | async-start | bytes 4194304 | tf_op jit(solution)/shard_map/all_to_all | solution.py:420
  85.0 0.0 copy-start.7
  85.0 5.4 %attend_own_6.1 = (f32[1024,128]{1,0:T(8,128)S(1)}, f32[8,128]{1,0:T(8,128)}) custom-call(bf16[16,384,128]{2,1,0:T(8,128)(2,1)S(1)} %all-to-all-done.mine_ref, bf16[32,1024]{1,0:T(8,128)(2,1)S(1)} %get-tuple-element.20.rest_0_.att1_hbm), custom_call_target="tpu_custom_call" | custom-call | flops 4294967296 | bytes 1048576 | tf_op jit(solution)/shard_map/attend_own_6/pallas_call | solution.py:229
  90.4 22.5 %attend_other.1 = bf16[16,112,128]{2,1,0:T(8,128)(2,1)S(1)} custom-call(bf16[16,384,128]{2,1,0:T(8,128)(2,1)S(1)} %all-to-all-done.mine_ref, bf16[16,256,128]{2,1,0:T(8,128)(2,1)} %collective-permute-done.1.other_ref, f32[512,128]{1,0:T(8,128)S(1)} %get-tuple-element.21.rest_0_, f32[2048,128]{1,0:T(8,128)S(1)} %copy-done.7, ...), custom_call_target="tpu_custom_call" | custom-call | flops 15032385536 | bytes 1048576 | tf_op jit(solution)/shard_map/attend_other/pallas_call | solution.py:259
  113.0 16.7 %all_to_all.20.at2_hbm = bf16[16,112,128]{2,1,0:T(8,128)(2,1)} all-to-all(bf16[16,112,128]{2,1,0:T(8,128)(2,1)S(1)} %attend_other.1), channel_id=1, replica_groups={{0,2,4,6,8,10,12,14,16,18,20,22,24,26,28,30},{1,3,5,7,9,11,13,15,17,19,..., dimensions={0} | all-to-all | bytes 917504 | tf_op jit(solution)/shard_map/all_to_all | solution.py:424
  129.6 5.2 %finish.1 = (bf16[256,1024]{1,0:T(8,128)(2,1)}, f32[1,32,32,256]{3,2,1,0:T(8,128)}) custom-call(s32[32]{0:T(128)} %owner_ref.3, s32[1]{0:T(128)} %bitcast.me_ref, bf16[32,1024]{1,0:T(8,128)(2,1)} %copy-done.2, bf16[16,112,128]{2,1,0:T(8,128)(2,1)} %all_to_all.20.at2_hbm, bf16[256,256]{1,0:T(8,128)(2,1)} %get-tuple-element.17.place_ref.place_hbm, ...), custom_call_target="tpu_custom_call" | custom-call | tf_op jit(solution)/shard_map/finish/pallas_call | solution.py:382
  (13 shorter events, 0.0 us)
Async XLA Ops:
  7.6 31.9 %all-to-all-start = ((bf16[16,384,128]{2,1,0:T(8,128)(2,1)}), bf16[16,384,128]{2,1,0:T(8,128)(2,1)S(1)}, u32[]{:S(2)}, u32[]{:S(2)}) async-start(bf16[16,384,128]{2,1,0:T(8,128)(2,1)} %get-tuple-element.14), calls=%async_computation | async-start | bytes 3145728 | tf_op jit(solution)/shard_map/all_to_all | solution.py:408
  39.5 7.4 %collective-permute-start = (bf16[16,16,128]{2,1,0:T(8,128)(2,1)S(1)}, bf16[16,16,128]{2,1,0:T(8,128)(2,1)S(1)}, u32[]{:S(2)}, u32[]{:S(2)}) collective-permute-start(bf16[16,16,128]{2,1,0:T(8,128)(2,1)S(1)} %slice.8), channel_id=1, source_target_pairs={{0,1},{1,0},{2,3},{3,2},{4,5},{5,4},{6,7},{7,6},{8,9},{9,8},{10,11... | collective-permute-start | bytes 196616 | tf_op jit(solution)/shard_map/ppermute | solution.py:409
  43.7 46.7 %collective-permute-start.1 = (bf16[16,256,128]{2,1,0:T(8,128)(2,1)}, bf16[16,256,128]{2,1,0:T(8,128)(2,1)}, u32[]{:S(2)}, u32[]{:S(2)}) collective-permute-start(bf16[16,256,128]{2,1,0:T(8,128)(2,1)} %slice.9), channel_id=1, source_target_pairs={{0,1},{1,0},{2,3},{3,2},{4,5},{5,4},{6,7},{7,6},{8,9},{9,8},{10,11... | collective-permute-start | bytes 3145736 | tf_op jit(solution)/shard_map/ppermute | solution.py:410
  53.4 18.4 %all-to-all-start.1 = ((bf16[32,32,128]{2,1,0:T(8,128)(2,1)}), bf16[32,32,128]{2,1,0:T(8,128)(2,1)S(1)}, u32[]{:S(2)}, u32[]{:S(2)}) async-start(bf16[32,32,128]{2,1,0:T(8,128)(2,1)} %bitcast.2), calls=%async_computation.1 | async-start | bytes 524288 | tf_op jit(solution)/shard_map/all_to_all | solution.py:413
  60.2 11.6 %copy-start = (bf16[256,1024]{1,0:T(8,128)(2,1)S(1)}, bf16[256,1024]{1,0:T(8,128)(2,1)}, u32[]{:S(2)}) copy-start(bf16[256,1024]{1,0:T(8,128)(2,1)} %x_hbm.1) | copy-start | bytes 1572868
  60.2 11.6 %copy-start.1 = (bf16[256,256]{1,0:T(8,128)(2,1)S(1)}, bf16[256,256]{1,0:T(8,128)(2,1)}, u32[]{:S(2)}) copy-start(bf16[256,256]{1,0:T(8,128)(2,1)} %get-tuple-element.17.place_ref.place_hbm) | copy-start | bytes 393220
  60.2 11.6 %copy-start.3 = (s32[1,32]{1,0:T(1,128)S(1)}, s32[1,32]{1,0:T(1,128)}, u32[]{:S(2)}) copy-start(s32[1,32]{1,0:T(1,128)} %slots_ref.3) | copy-start | bytes 388
  60.3 11.6 %copy-start.4 = (s32[32]{0:T(128)S(1)}, s32[32]{0:T(128)}, u32[]{:S(2)}) copy-start(s32[32]{0:T(128)} %owner_ref.3) | copy-start | bytes 388
  60.3 11.6 %copy-start.5 = (s32[32]{0:T(128)S(1)}, s32[32]{0:T(128)}, u32[]{:S(2)}) copy-start(s32[32]{0:T(128)} %counts_ref.1) | copy-start | bytes 388
  70.9 1.0 copy-start.6
  75.2 9.8 %copy-start.2 = (bf16[32,1024]{1,0:T(8,128)(2,1)}, bf16[32,1024]{1,0:T(8,128)(2,1)S(1)}, u32[]{:S(2)}) copy-start(bf16[32,1024]{1,0:T(8,128)(2,1)S(1)} %get-tuple-element.20.rest_0_.att1_hbm) | copy-start | bytes 196612
  75.2 37.7 %all-to-all-start.2 = ((bf16[32,32,1024]{2,1,0:T(8,128)(2,1)}), bf16[32,32,1024]{2,1,0:T(8,128)(2,1)}, u32[]{:S(2)}, u32[]{:S(2)}) async-start(bf16[32,32,1024]{2,1,0:T(8,128)(2,1)} %get-tuple-element.23), calls=%async_computation.2 | async-start | bytes 4194304 | tf_op jit(solution)/shard_map/all_to_all | solution.py:420
  85.0 5.4 %copy-start.7 = (f32[2048,128]{1,0:T(8,128)S(1)}, f32[2048,128]{1,0:T(8,128)}, u32[]{:S(2)}) copy-start(f32[2048,128]{1,0:T(8,128)} %copy-done.6) | copy-start | bytes 3145732

commit v9 on v8

--- a/solution.py
+++ b/solution.py
@@ -223,6 +223,7 @@
 
 HBM = pl.BlockSpec(memory_space=pltpu.HBM)
 TICK = jax.ShapeDtypeStruct((8, LANES), F32)
+STATE_ROWS = 160 * ROWS
 
 
 def attend_own(mine, first, last, after=()):
@@ -230,7 +231,7 @@
         functools.partial(own_kernel, first),
         in_specs=[VMEM] * (1 + len(after)),
         out_specs=[pl.BlockSpec((ROWS, LANES), lambda i: (i, 0)), VMEM],
-        out_shape=[jax.ShapeDtypeStruct(((last - first) * ROWS, LANES), F32), TICK],
+        out_shape=[jax.ShapeDtypeStruct((STATE_ROWS, LANES), F32), TICK],
         name=f"attend_own_{first}",
         **attend_settings(last - first),
     )(mine, *after)
@@ -247,8 +248,7 @@
     )(mine, picks, me, *after)
 
 
-def attend_other(mine, other, states, after=()):
-    counts = [state.shape[0] // ROWS for state in states]
+def attend_other(mine, other, states, counts, after=()):
     chunks = sum(counts)
     starts = [CHUNKS - sum(counts[i:]) for i in range(len(counts))]
 
@@ -419,7 +419,9 @@
     )
     arrived = lax.all_to_all(send, "frame", 0, 0, tiled=True)
     state3, _ = attend_own(mine, SPLIT, CHUNKS, [att1])
-    rest = attend_other(mine, other, [state1, state2, state3])
+    rest = attend_other(
+        mine, other, [state1, state2, state3], [1, SPLIT - 2, CHUNKS - SPLIT]
+    )
     rest, arrived = lax.optimization_barrier((rest, arrived))
     att2 = lax.all_to_all(rest, "frame", 0, 0, tiled=True, axis_index_groups=groups)
     return tuple(finish(att1, att2, features, w_out, place, owner, me, arrived))

time: 136 us -> 138 us (1.015)
  Pallas kernels: 63.2 us -> 65.5 us
    pallas_call x3, Pallas kernels: 18.7 us -> 20.9 us  [attend_own(): pl.pallas_call(functools.partial(own_kernel, first), in_specs=[VMEM] * (1...]
  transfers between devices with their start and end apart: 5 -> 5, of which waited for: 1 -> 1; matrix products, arithmetic and copies ran while one was open for 1% -> 1% of each run, Pallas kernels for 38% -> 39%
where the time goes in v9:
time: 138 us; the launch traced here: 137 us
  Pallas kernels  65.5 us (47%)
  starting transfers between devices  28.4 us (21%)
  waiting for transfers between devices  23.8 us (17%)
  blocking collectives  16.7 us (12%)
  local copies, waits for them, and re-layouts  1.69 us (1%)
    all_to_all x1, waiting for transfers between devices, per_device(): lax.all_to_all(packed, 'frame', 0, 0, tiled=True, axis_index_groups=groups)  23.8 us
    pallas_call x1, Pallas kernels, attend_other(): pl.pallas_call(functools.partial(other_kernel, starts), in_specs=[VMEM, V...  22.7 us
    pallas_call x3, Pallas kernels, attend_own(): pl.pallas_call(functools.partial(own_kernel, first), in_specs=[VMEM] * (1...  20.9 us
    all_to_all x1, blocking collectives, per_device(): lax.all_to_all(rest, 'frame', 0, 0, tiled=True, axis_index_groups=groups)  16.7 us
    all_to_all x1, starting transfers between devices, per_device(): arrived = lax.all_to_all(send, 'frame', 0, 0, tiled=True)  9.87 us
    all_to_all x1, starting transfers between devices, per_device(): lax.all_to_all(packed, 'frame', 0, 0, tiled=True, axis_index_groups=groups)  8.13 us
    pallas_call x1, Pallas kernels, project(): pl.pallas_call(project_kernel, grid=(steps,), in_specs=[pl.BlockSpec((TOK...  6.99 us
    all_to_all x1, starting transfers between devices, per_device(): lax.all_to_all(parts.reshape(FRAMES, QMAX, LANES), 'frame', 0, 0, tiled=T...  6.81 us
  transfers between devices with their start and end apart: 5, of which 1 were waited for; matrix products, arithmetic and copies ran while one was open for 1% of the time, Pallas kernels for 39%

profile of v9, /device:TPU:0, one launch (start us, length us, event | category | flops | bytes accessed | tf_op | source)
XLA Modules:
  0.0 137.0 jit_solution(18188493441103646370)
XLA Ops:
  0.6 7.0 %project.1 = (bf16[16,384,128]{2,1,0:T(8,128)(2,1)}, bf16[256,256]{1,0:T(8,128)(2,1)}) custom-call(bf16[256,1024]{1,0:T(8,128)(2,1)} %x_hbm.1, f32[1,1024]{1,0:T(1,128)} %bitcast.3, s32[1,32]{1,0:T(1,128)} %slots_ref.3, bf16[1024,3072]{1,0:T(8,128)(2,1)} %wv_ref.1, bf16[1024,3072]{1,0:T(8,128)(2,1)} %wv_ref.1, bf16[1024,3072]{1,0:T(8,128)(2,1)} %wv_ref.1), custom_call_target="tpu_custom_call" | custom-call | tf_op jit(solution)/shard_map/project/pallas_call | solution.py:84
  7.6 8.1 %all-to-all-start = ((bf16[16,384,128]{2,1,0:T(8,128)(2,1)}), bf16[16,384,128]{2,1,0:T(8,128)(2,1)S(1)}, u32[]{:S(2)}, u32[]{:S(2)}) async-start(bf16[16,384,128]{2,1,0:T(8,128)(2,1)} %get-tuple-element.14), calls=%async_computation | async-start | bytes 3145728 | tf_op jit(solution)/shard_map/all_to_all | solution.py:408
  15.8 23.8 %all-to-all-done.mine_ref = bf16[16,384,128]{2,1,0:T(8,128)(2,1)S(1)} async-done(((bf16[16,384,128]{2,1,0:T(8,128)(2,1)}), bf16[16,384,128]{2,1,0:T(8,128)(2,1)S(1)}, u32[]{:S(2)}, u32[]{:S(2)}) %all-to-all-start) | async-done | bytes 1572896 | tf_op jit(solution)/shard_map/all_to_all | solution.py:408
  39.6 3.1 %collective-permute-start = (bf16[16,16,128]{2,1,0:T(8,128)(2,1)S(1)}, bf16[16,16,128]{2,1,0:T(8,128)(2,1)S(1)}, u32[]{:S(2)}, u32[]{:S(2)}) collective-permute-start(bf16[16,16,128]{2,1,0:T(8,128)(2,1)S(1)} %slice.8), channel_id=1, source_target_pairs={{0,1},{1,0},{2,3},{3,2},{4,5},{5,4},{6,7},{7,6},{8,9},{9,8},{10,11... | collective-permute-start | bytes 196616 | tf_op jit(solution)/shard_map/ppermute | solution.py:409
  42.7 1.0 slice.9
  43.7 0.5 collective-permute-start.1
  44.2 3.5 %attend_own_1.1 = (f32[81920,128]{1,0:T(8,128)}, f32[8,128]{1,0:T(8,128)S(1)}) custom-call(bf16[16,384,128]{2,1,0:T(8,128)(2,1)S(1)} %all-to-all-done.mine_ref), custom_call_target="tpu_custom_call" | custom-call | flops 2147483648 | bytes 1048576 | tf_op jit(solution)/shard_map/attend_own_1/pallas_call | solution.py:230
  47.7 0.0 collective-permute-done.picks_ref
  47.7 6.4 %attend_picks.1 = (bf16[16,2,32,128]{3,2,1,0:T(8,128)(2,1)}, f32[8,128]{1,0:T(8,128)S(1)}) custom-call(bf16[16,384,128]{2,1,0:T(8,128)(2,1)S(1)} %all-to-all-done.mine_ref, bf16[16,16,128]{2,1,0:T(8,128)(2,1)S(1)} %collective-permute-done.picks_ref, s32[1]{0:T(128)} %bitcast.me_ref, f32[8,128]{1,0:T(8,128)S(1)} %get-tuple-element.15.rest_0_), custom_call_target="tpu_custom_call" | custom-call | flops 4294967296 | bytes 1048576 | tf_op jit(solution)/shard_map/attend_picks/pallas_call | solution.py:241
  54.1 6.8 %all-to-all-start.1 = ((bf16[32,32,128]{2,1,0:T(8,128)(2,1)}), bf16[32,32,128]{2,1,0:T(8,128)(2,1)S(1)}, u32[]{:S(2)}, u32[]{:S(2)}) async-start(bf16[32,32,128]{2,1,0:T(8,128)(2,1)} %bitcast.2), calls=%async_computation.1 | async-start | bytes 524288 | tf_op jit(solution)/shard_map/all_to_all | solution.py:413
  60.9 0.0 copy-start
  60.9 0.0 copy-start.4
  60.9 0.0 copy-start.5
  60.9 0.0 copy-start.6
  60.9 11.3 %attend_own_2.1 = (f32[81920,128]{1,0:T(8,128)}, f32[8,128]{1,0:T(8,128)}) custom-call(bf16[16,384,128]{2,1,0:T(8,128)(2,1)S(1)} %all-to-all-done.mine_ref, f32[8,128]{1,0:T(8,128)S(1)} %get-tuple-element.18.rest_0_), custom_call_target="tpu_custom_call" | custom-call | flops 8589934592 | bytes 1048576 | tf_op jit(solution)/shard_map/attend_own_2/pallas_call | solution.py:230
  72.2 0.0 all-to-all-done.1.part_ref
  72.3 3.3 %track_rows.1 = (bf16[32,32,1024]{2,1,0:T(8,128)(2,1)}, bf16[32,1024]{1,0:T(8,128)(2,1)S(1)}) custom-call(bf16[32,32,128]{2,1,0:T(8,128)(2,1)S(1)} %all-to-all-done.1.part_ref, bf16[1024,1024]{1,0:T(8,128)(2,1)} %w_hbm.3, bf16[256,1024]{1,0:T(8,128)(2,1)S(1)} %copy-done, bf16[256,256]{1,0:T(8,128)(2,1)S(1)} %copy-done.1, s32[1,32]{1,0:T(1,128)S(1)} %copy-done.4, ...), custom_call_target="tpu_custom_call" | custom-call | flops 2147483648 | bytes 4194304 | tf_op jit(solution)/shard_map/track_rows/pallas_call | solution.py:320
  75.6 0.6 copy-done.2
  76.2 9.9 %all-to-all-start.2 = ((bf16[32,32,1024]{2,1,0:T(8,128)(2,1)}), bf16[32,32,1024]{2,1,0:T(8,128)(2,1)}, u32[]{:S(2)}, u32[]{:S(2)}) async-start(bf16[32,32,1024]{2,1,0:T(8,128)(2,1)} %get-tuple-element.23), calls=%async_computation.2 | async-start | bytes 4194304 | tf_op jit(solution)/shard_map/all_to_all | solution.py:420
  86.1 6.1 %attend_own_6.1 = (f32[81920,128]{1,0:T(8,128)}, f32[8,128]{1,0:T(8,128)}) custom-call(bf16[16,384,128]{2,1,0:T(8,128)(2,1)S(1)} %all-to-all-done.mine_ref, bf16[32,1024]{1,0:T(8,128)(2,1)S(1)} %copy-done.3), custom_call_target="tpu_custom_call" | custom-call | flops 4294967296 | bytes 1048576 | tf_op jit(solution)/shard_map/attend_own_6/pallas_call | solution.py:230
  92.2 22.7 %attend_other.1 = bf16[16,112,128]{2,1,0:T(8,128)(2,1)S(1)} custom-call(bf16[16,384,128]{2,1,0:T(8,128)(2,1)S(1)} %all-to-all-done.mine_ref, bf16[16,256,128]{2,1,0:T(8,128)(2,1)S(1)} %collective-permute-done.1.other_ref, f32[81920,128]{1,0:T(8,128)} %get-tuple-element.21.rest_0_, f32[81920,128]{1,0:T(8,128)} %get-tuple-element.19.rest_0_.rest_1_, ...), custom_call_target="tpu_custom_call" | custom-call | flops 15032385536 | bytes 1048576 | tf_op jit(solution)/shard_map/attend_other/pallas_call | solution.py:259
  115.0 0.0 all-to-all-done.2.rows_hbm
  115.0 16.7 %all_to_all.20.at2_hbm = bf16[16,112,128]{2,1,0:T(8,128)(2,1)} all-to-all(bf16[16,112,128]{2,1,0:T(8,128)(2,1)S(1)} %attend_other.1), channel_id=1, replica_groups={{0,2,4,6,8,10,12,14,16,18,20,22,24,26,28,30},{1,3,5,7,9,11,13,15,17,19,..., dimensions={0} | all-to-all | bytes 917504 | tf_op jit(solution)/shard_map/all_to_all | solution.py:426
  131.7 5.2 %finish.1 = (bf16[256,1024]{1,0:T(8,128)(2,1)}, f32[1,32,32,256]{3,2,1,0:T(8,128)}) custom-call(s32[32]{0:T(128)} %owner_ref.3, s32[1]{0:T(128)} %bitcast.me_ref, bf16[32,1024]{1,0:T(8,128)(2,1)} %copy-done.2, bf16[16,112,128]{2,1,0:T(8,128)(2,1)} %all_to_all.20.at2_hbm, bf16[256,256]{1,0:T(8,128)(2,1)} %get-tuple-element.17.place_ref.place_hbm, ...), custom_call_target="tpu_custom_call" | custom-call | tf_op jit(solution)/shard_map/finish/pallas_call | solution.py:382
  (11 shorter events, 0.0 us)
Async XLA Ops:
  7.6 31.9 %all-to-all-start = ((bf16[16,384,128]{2,1,0:T(8,128)(2,1)}), bf16[16,384,128]{2,1,0:T(8,128)(2,1)S(1)}, u32[]{:S(2)}, u32[]{:S(2)}) async-start(bf16[16,384,128]{2,1,0:T(8,128)(2,1)} %get-tuple-element.14), calls=%async_computation | async-start | bytes 3145728 | tf_op jit(solution)/shard_map/all_to_all | solution.py:408
  39.6 8.1 %collective-permute-start = (bf16[16,16,128]{2,1,0:T(8,128)(2,1)S(1)}, bf16[16,16,128]{2,1,0:T(8,128)(2,1)S(1)}, u32[]{:S(2)}, u32[]{:S(2)}) collective-permute-start(bf16[16,16,128]{2,1,0:T(8,128)(2,1)S(1)} %slice.8), channel_id=1, source_target_pairs={{0,1},{1,0},{2,3},{3,2},{4,5},{5,4},{6,7},{7,6},{8,9},{9,8},{10,11... | collective-permute-start | bytes 196616 | tf_op jit(solution)/shard_map/ppermute | solution.py:409
  43.7 48.5 %collective-permute-start.1 = (bf16[16,256,128]{2,1,0:T(8,128)(2,1)}, bf16[16,256,128]{2,1,0:T(8,128)(2,1)S(1)}, u32[]{:S(2)}, u32[]{:S(2)}) collective-permute-start(bf16[16,256,128]{2,1,0:T(8,128)(2,1)} %slice.9), channel_id=1, source_target_pairs={{0,1},{1,0},{2,3},{3,2},{4,5},{5,4},{6,7},{7,6},{8,9},{9,8},{10,11... | collective-permute-start | bytes 3145736 | tf_op jit(solution)/shard_map/ppermute | solution.py:410
  54.1 18.2 %all-to-all-start.1 = ((bf16[32,32,128]{2,1,0:T(8,128)(2,1)}), bf16[32,32,128]{2,1,0:T(8,128)(2,1)S(1)}, u32[]{:S(2)}, u32[]{:S(2)}) async-start(bf16[32,32,128]{2,1,0:T(8,128)(2,1)} %bitcast.2), calls=%async_computation.1 | async-start | bytes 524288 | tf_op jit(solution)/shard_map/all_to_all | solution.py:413
  60.9 11.3 %copy-start = (bf16[256,1024]{1,0:T(8,128)(2,1)S(1)}, bf16[256,1024]{1,0:T(8,128)(2,1)}, u32[]{:S(2)}) copy-start(bf16[256,1024]{1,0:T(8,128)(2,1)} %x_hbm.1) | copy-start | bytes 1572868
  60.9 11.3 %copy-start.1 = (bf16[256,256]{1,0:T(8,128)(2,1)S(1)}, bf16[256,256]{1,0:T(8,128)(2,1)}, u32[]{:S(2)}) copy-start(bf16[256,256]{1,0:T(8,128)(2,1)} %get-tuple-element.17.place_ref.place_hbm) | copy-start | bytes 393220
  60.9 11.3 %copy-start.4 = (s32[1,32]{1,0:T(1,128)S(1)}, s32[1,32]{1,0:T(1,128)}, u32[]{:S(2)}) copy-start(s32[1,32]{1,0:T(1,128)} %slots_ref.3) | copy-start | bytes 388
  60.9 11.3 %copy-start.5 = (s32[32]{0:T(128)S(1)}, s32[32]{0:T(128)}, u32[]{:S(2)}) copy-start(s32[32]{0:T(128)} %owner_ref.3) | copy-start | bytes 388
  60.9 11.3 %copy-start.6 = (s32[32]{0:T(128)S(1)}, s32[32]{0:T(128)}, u32[]{:S(2)}) copy-start(s32[32]{0:T(128)} %counts_ref.1) | copy-start | bytes 388
  75.6 0.6 copy-start.2
  76.2 9.9 %copy-start.3 = (bf16[32,1024]{1,0:T(8,128)(2,1)S(1)}, bf16[32,1024]{1,0:T(8,128)(2,1)}, u32[]{:S(2)}) copy-start(bf16[32,1024]{1,0:T(8,128)(2,1)} %copy-done.2) | copy-start | bytes 196612
  76.2 38.7 %all-to-all-start.2 = ((bf16[32,32,1024]{2,1,0:T(8,128)(2,1)}), bf16[32,32,1024]{2,1,0:T(8,128)(2,1)}, u32[]{:S(2)}, u32[]{:S(2)}) async-start(bf16[32,32,1024]{2,1,0:T(8,128)(2,1)} %get-tuple-element.23), calls=%async_computation.2 | async-start | bytes 4194304 | tf_op jit(solution)/shard_map/all_to_all | solution.py:420

commit v10 on v8

--- a/solution.py
+++ b/solution.py
@@ -130,8 +130,8 @@
     return kv_ref[pl.ds(j * count, count), :TOK].reshape(count * TOK, LANES)
 
 
-def fill_values(kv_ref, va_ref):
-    @pl.when(pl.program_id(0) == 0)
+def fill_values(kv_ref, va_ref, step=0):
+    @pl.when(pl.program_id(0) == step)
     def _():
         for j in range(GROUP):
             kv = kv_ref[j, :TOK]
@@ -167,19 +167,33 @@
     state_ref[...] = jnp.where(lane == 1, top, acc)
 
 
-def other_kernel(starts, mine_ref, other_ref, *rest):
-    state_refs = rest[: len(starts)]
-    o_ref, va_ref = rest[-2:]
-    fill_values(other_ref, va_ref)
-    chunk = pl.program_id(0) + starts[0]
-    q = load_queries(mine_ref, chunk)
-    state = state_refs[0][...]
-    for start, ref in zip(starts[1:], state_refs[1:], strict=True):
-        state = jnp.where(chunk >= start, ref[...], state)
-    top, acc = absorb(q, other_ref, va_ref, state[:, 1:2], state)
-    out = acc / acc[:, :1]
-    packed = jnp.where(low_half(ROWS // 2), swap(out[: ROWS // 2]), out[ROWS // 2 :])
-    o_ref[...] = packed.astype(BF16).reshape(o_ref.shape)
+def last_kernel(starts, mine_ref, other_ref, *rest):
+    o_ref, va_ref, keep_ref = rest[-3:]
+    late = keep_ref.shape[0]
+    step = pl.program_id(0)
+    fill_values(mine_ref, va_ref)
+    fill_values(other_ref, va_ref, late)
+
+    @pl.when(step < late)
+    def _():
+        q = load_queries(mine_ref, step + CHUNKS - late)
+        top, acc = absorb(q, mine_ref, va_ref, None, None)
+        lane = lax.broadcasted_iota(jnp.int32, acc.shape, 1)
+        keep_ref[step] = jnp.where(lane == 1, top, acc)
+
+    @pl.when(step >= late)
+    def _():
+        chunk = step - late + starts[0]
+        q = load_queries(mine_ref, chunk)
+        state = rest[0][...]
+        for n in range(1, len(starts)):
+            state = jnp.where(chunk >= starts[n], rest[n][...], state)
+        kept = keep_ref[jnp.maximum(chunk - (CHUNKS - late), 0)]
+        state = jnp.where(chunk >= CHUNKS - late, kept, state)
+        top, acc = absorb(q, other_ref, va_ref, state[:, 1:2], state)
+        out = acc / acc[:, :1]
+        packed = jnp.where(low_half(ROWS // 2), swap(out[: ROWS // 2]), out[ROWS // 2 :])
+        o_ref[...] = packed.astype(BF16).reshape(o_ref.shape)
 
 
 def picks_kernel(mine_ref, picks_ref, me_ref, *rest):
@@ -225,12 +239,12 @@
 TICK = jax.ShapeDtypeStruct((8, LANES), F32)
 
 
-def attend_own(mine, first, last, after=()):
+def attend_own(mine, first, last, after=(), in_hbm=False):
     return pl.pallas_call(
         functools.partial(own_kernel, first),
         in_specs=[VMEM] * (1 + len(after)),
         out_specs=[pl.BlockSpec((ROWS, LANES), lambda i: (i, 0)), VMEM],
-        out_shape=[jax.ShapeDtypeStruct(((last - first) * ROWS, LANES), F32), TICK],
+        out_shape=[jax.ShapeDtypeStruct(((160 if in_hbm else last - first) * ROWS, LANES), F32), TICK],
         name=f"attend_own_{first}",
         **attend_settings(last - first),
     )(mine, *after)
@@ -247,24 +261,25 @@
     )(mine, picks, me, *after)
 
 
-def attend_other(mine, other, states, after=()):
-    counts = [state.shape[0] // ROWS for state in states]
-    chunks = sum(counts)
-    starts = [CHUNKS - sum(counts[i:]) for i in range(len(counts))]
+def attend_last(mine, other, states, counts, after):
+    starts = [1 + sum(counts[:i]) for i in range(len(counts))]
+    late = CHUNKS - 1 - sum(counts)
+    settings = attend_settings(CHUNKS - 1 + late)
+    settings["scratch_shapes"] += [pltpu.VMEM((late, ROWS, LANES), F32)]
 
     def state_spec(start, count):
-        shift = start - starts[0]
+        shift = late + start - starts[0]
         return pl.BlockSpec((ROWS, LANES), lambda i: (jnp.clip(i - shift, 0, count - 1), 0))
 
     return pl.pallas_call(
-        functools.partial(other_kernel, starts),
+        functools.partial(last_kernel, starts),
         in_specs=[VMEM, VMEM]
         + [state_spec(*pair) for pair in zip(starts, counts, strict=True)]
         + [VMEM] * len(after),
-        out_specs=pl.BlockSpec((GROUP, CHUNK, LANES), lambda i: (0, i, 0)),
-        out_shape=jax.ShapeDtypeStruct((GROUP, chunks * CHUNK, LANES), BF16),
-        name="attend_other",
-        **attend_settings(chunks),
+        out_specs=pl.BlockSpec((GROUP, CHUNK, LANES), lambda i: (0, jnp.maximum(i - late, 0), 0)),
+        out_shape=jax.ShapeDtypeStruct((GROUP, (CHUNKS - 1) * CHUNK, LANES), BF16),
+        name="attend_last",
+        **settings,
     )(mine, other, *states, *after)
 
 
@@ -413,13 +428,12 @@
     parts_here = lax.all_to_all(
         parts.reshape(FRAMES, QMAX, LANES), "frame", 0, 0, tiled=True
     )
-    state2, _ = attend_own(mine, 2, SPLIT, [tick])
+    state2, _ = attend_own(mine, 2, SPLIT, [tick], in_hbm=True)
     send, att1 = track_rows(
         parts_here, w_out, features, place, query_index, counts, owner, me, [state2]
     )
     arrived = lax.all_to_all(send, "frame", 0, 0, tiled=True)
-    state3, _ = attend_own(mine, SPLIT, CHUNKS, [att1])
-    rest = attend_other(mine, other, [state1, state2, state3])
+    rest = attend_last(mine, other, [state1, state2], [1, SPLIT - 2], [att1])
     rest, arrived = lax.optimization_barrier((rest, arrived))
     att2 = lax.all_to_all(rest, "frame", 0, 0, tiled=True, axis_index_groups=groups)
     return tuple(finish(att1, att2, features, w_out, place, owner, me, arrived))

time: 136 us -> 136 us (level)
    pallas_call x1, Pallas kernels: 22.5 us -> 28.2 us  [attend_last(): pl.pallas_call(functools.partial(last_kernel, starts), in_specs=[VMEM, VM...]
    pallas_call x3 -> x2, Pallas kernels: 18.7 us -> 14.1 us  [attend_own(): pl.pallas_call(functools.partial(own_kernel, first), in_specs=[VMEM] * (1...]
  transfers between devices with their start and end apart: 5 -> 5, of which waited for: 1 -> 2; matrix products, arithmetic and copies ran while one was open for 1% -> 1% of each run, Pallas kernels for 38% -> 39%
where the time goes in v10:
time: 136 us; the launch traced here: 135 us
  Pallas kernels  64.2 us (47%)
  starting transfers between devices  28 us (21%)
  waiting for transfers between devices  24.1 us (18%)
  blocking collectives  16.7 us (12%)
    pallas_call x1, Pallas kernels, attend_last(): pl.pallas_call(functools.partial(last_kernel, starts), in_specs=[VMEM, VM...  28.2 us
    all_to_all x1, waiting for transfers between devices, per_device(): lax.all_to_all(packed, 'frame', 0, 0, tiled=True, axis_index_groups=groups)  23.8 us
    all_to_all x1, blocking collectives, per_device(): lax.all_to_all(rest, 'frame', 0, 0, tiled=True, axis_index_groups=groups)  16.7 us
    pallas_call x2, Pallas kernels, attend_own(): pl.pallas_call(functools.partial(own_kernel, first), in_specs=[VMEM] * (1...  14.1 us
    all_to_all x1, starting transfers between devices, per_device(): arrived = lax.all_to_all(send, 'frame', 0, 0, tiled=True)  9.48 us
    all_to_all x1, starting transfers between devices, per_device(): lax.all_to_all(packed, 'frame', 0, 0, tiled=True, axis_index_groups=groups)  8.13 us
    pallas_call x1, Pallas kernels, project(): pl.pallas_call(project_kernel, grid=(steps,), in_specs=[pl.BlockSpec((TOK...  7 us
    all_to_all x1, starting transfers between devices, per_device(): lax.all_to_all(parts.reshape(FRAMES, QMAX, LANES), 'frame', 0, 0, tiled=T...  6.82 us
  transfers between devices with their start and end apart: 5, of which 2 were waited for; matrix products, arithmetic and copies ran while one was open for 1% of the time, Pallas kernels for 39%

profile of v10, /device:TPU:0, one launch (start us, length us, event | category | flops | bytes accessed | tf_op | source)
XLA Modules:
  0.0 135.0 jit_solution(17703773792982863793)
XLA Ops:
  0.6 7.0 %project.1 = (bf16[16,384,128]{2,1,0:T(8,128)(2,1)}, bf16[256,256]{1,0:T(8,128)(2,1)}) custom-call(bf16[256,1024]{1,0:T(8,128)(2,1)} %x_hbm.1, f32[1,1024]{1,0:T(1,128)} %bitcast.3, s32[1,32]{1,0:T(1,128)} %slots_ref.3, bf16[1024,3072]{1,0:T(8,128)(2,1)} %wv_ref.1, bf16[1024,3072]{1,0:T(8,128)(2,1)} %wv_ref.1, bf16[1024,3072]{1,0:T(8,128)(2,1)} %wv_ref.1), custom_call_target="tpu_custom_call" | custom-call | tf_op jit(solution)/shard_map/project/pallas_call | solution.py:84
  7.6 8.1 %all-to-all-start = ((bf16[16,384,128]{2,1,0:T(8,128)(2,1)}), bf16[16,384,128]{2,1,0:T(8,128)(2,1)S(1)}, u32[]{:S(2)}, u32[]{:S(2)}) async-start(bf16[16,384,128]{2,1,0:T(8,128)(2,1)} %get-tuple-element.13), calls=%async_computation | async-start | bytes 3145728 | tf_op jit(solution)/shard_map/all_to_all | solution.py:423
  15.8 23.8 %all-to-all-done.mine_ref = bf16[16,384,128]{2,1,0:T(8,128)(2,1)S(1)} async-done(((bf16[16,384,128]{2,1,0:T(8,128)(2,1)}), bf16[16,384,128]{2,1,0:T(8,128)(2,1)S(1)}, u32[]{:S(2)}, u32[]{:S(2)}) %all-to-all-start) | async-done | bytes 1572896 | tf_op jit(solution)/shard_map/all_to_all | solution.py:423
  39.6 3.1 %collective-permute-start = (bf16[16,16,128]{2,1,0:T(8,128)(2,1)S(1)}, bf16[16,16,128]{2,1,0:T(8,128)(2,1)S(1)}, u32[]{:S(2)}, u32[]{:S(2)}) collective-permute-start(bf16[16,16,128]{2,1,0:T(8,128)(2,1)S(1)} %slice.8), channel_id=1, source_target_pairs={{0,1},{1,0},{2,3},{3,2},{4,5},{5,4},{6,7},{7,6},{8,9},{9,8},{10,11... | collective-permute-start | bytes 196616 | tf_op jit(solution)/shard_map/ppermute | solution.py:424
  42.7 1.0 slice.9
  43.7 0.5 collective-permute-start.1
  44.2 2.8 %attend_own_1.1 = (f32[512,128]{1,0:T(8,128)S(1)}, f32[8,128]{1,0:T(8,128)S(1)}) custom-call(bf16[16,384,128]{2,1,0:T(8,128)(2,1)S(1)} %all-to-all-done.mine_ref), custom_call_target="tpu_custom_call" | custom-call | flops 2147483648 | bytes 1048576 | tf_op jit(solution)/shard_map/attend_own_1/pallas_call | solution.py:243
  47.0 0.0 collective-permute-done.picks_ref
  47.0 6.4 %attend_picks.1 = (bf16[16,2,32,128]{3,2,1,0:T(8,128)(2,1)}, f32[8,128]{1,0:T(8,128)S(1)}) custom-call(bf16[16,384,128]{2,1,0:T(8,128)(2,1)S(1)} %all-to-all-done.mine_ref, bf16[16,16,128]{2,1,0:T(8,128)(2,1)S(1)} %collective-permute-done.picks_ref, s32[1]{0:T(128)} %bitcast.me_ref, f32[8,128]{1,0:T(8,128)S(1)} %get-tuple-element.14.rest_0_), custom_call_target="tpu_custom_call" | custom-call | flops 4294967296 | bytes 1048576 | tf_op jit(solution)/shard_map/attend_picks/pallas_call | solution.py:254
  53.4 6.8 %all-to-all-start.1 = ((bf16[32,32,128]{2,1,0:T(8,128)(2,1)}), bf16[32,32,128]{2,1,0:T(8,128)(2,1)S(1)}, u32[]{:S(2)}, u32[]{:S(2)}) async-start(bf16[32,32,128]{2,1,0:T(8,128)(2,1)} %bitcast.2), calls=%async_computation.1 | async-start | bytes 524288 | tf_op jit(solution)/shard_map/all_to_all | solution.py:428
  60.2 0.0 copy-start
  60.2 0.0 copy-start.3
  60.3 0.0 copy-start.4
  60.3 0.0 copy-start.5
  60.3 11.3 %attend_own_2.1 = (f32[81920,128]{1,0:T(8,128)}, f32[8,128]{1,0:T(8,128)}) custom-call(bf16[16,384,128]{2,1,0:T(8,128)(2,1)S(1)} %all-to-all-done.mine_ref, f32[8,128]{1,0:T(8,128)S(1)} %get-tuple-element.17.rest_0_), custom_call_target="tpu_custom_call" | custom-call | flops 8589934592 | bytes 1048576 | tf_op jit(solution)/shard_map/attend_own_2/pallas_call | solution.py:243
  71.6 0.3 all-to-all-done.1.part_ref
  71.9 0.0 copy-done.3
  71.9 3.3 %track_rows.1 = (bf16[32,32,1024]{2,1,0:T(8,128)(2,1)}, bf16[32,1024]{1,0:T(8,128)(2,1)S(1)}) custom-call(bf16[32,32,128]{2,1,0:T(8,128)(2,1)S(1)} %all-to-all-done.1.part_ref, bf16[1024,1024]{1,0:T(8,128)(2,1)} %w_hbm.3, bf16[256,1024]{1,0:T(8,128)(2,1)S(1)} %copy-done, bf16[256,256]{1,0:T(8,128)(2,1)S(1)} %copy-done.1, s32[1,32]{1,0:T(1,128)S(1)} %copy-done.3, ...), custom_call_target="tpu_custom_call" | custom-call | flops 2147483648 | bytes 4194304 | tf_op jit(solution)/shard_map/track_rows/pallas_call | solution.py:335
  75.2 9.5 %all-to-all-start.2 = ((bf16[32,32,1024]{2,1,0:T(8,128)(2,1)}), bf16[32,32,1024]{2,1,0:T(8,128)(2,1)}, u32[]{:S(2)}, u32[]{:S(2)}) async-start(bf16[32,32,1024]{2,1,0:T(8,128)(2,1)} %get-tuple-element.21), calls=%async_computation.2 | async-start | bytes 4194304 | tf_op jit(solution)/shard_map/all_to_all | solution.py:435
  84.7 0.0 collective-permute-done.1.other_ref
  84.8 28.2 %attend_last.1 = bf16[16,112,128]{2,1,0:T(8,128)(2,1)S(1)} custom-call(bf16[16,384,128]{2,1,0:T(8,128)(2,1)S(1)} %all-to-all-done.mine_ref, bf16[16,256,128]{2,1,0:T(8,128)(2,1)} %collective-permute-done.1.other_ref, f32[512,128]{1,0:T(8,128)S(1)} %get-tuple-element.20.rest_0_, f32[81920,128]{1,0:T(8,128)} %get-tuple-element.18.rest_0_.rest_1_, ...), custom_call_target="tpu_custom_call" | custom-call | flops 19327352832 | bytes 1048576 | tf_op jit(solution)/shard_map/attend_last/pallas_call | solution.py:274
  113.0 0.0 all-to-all-done.2.rows_hbm
  113.0 16.7 %all_to_all.20.at2_hbm = bf16[16,112,128]{2,1,0:T(8,128)(2,1)} all-to-all(bf16[16,112,128]{2,1,0:T(8,128)(2,1)S(1)} %attend_last.1), channel_id=1, replica_groups={{0,2,4,6,8,10,12,14,16,18,20,22,24,26,28,30},{1,3,5,7,9,11,13,15,17,19,..., dimensions={0} | all-to-all | bytes 917504 | tf_op jit(solution)/shard_map/all_to_all | solution.py:438
  129.7 5.2 %finish.1 = (bf16[256,1024]{1,0:T(8,128)(2,1)}, f32[1,32,32,256]{3,2,1,0:T(8,128)}) custom-call(s32[32]{0:T(128)} %owner_ref.3, s32[1]{0:T(128)} %bitcast.me_ref, bf16[32,1024]{1,0:T(8,128)(2,1)} %copy-done.2, bf16[16,112,128]{2,1,0:T(8,128)(2,1)} %all_to_all.20.at2_hbm, bf16[256,256]{1,0:T(8,128)(2,1)} %get-tuple-element.16.place_ref.place_hbm, ...), custom_call_target="tpu_custom_call" | custom-call | tf_op jit(solution)/shard_map/finish/pallas_call | solution.py:397
  (8 shorter events, 0.0 us)
Async XLA Ops:
  7.6 31.9 %all-to-all-start = ((bf16[16,384,128]{2,1,0:T(8,128)(2,1)}), bf16[16,384,128]{2,1,0:T(8,128)(2,1)S(1)}, u32[]{:S(2)}, u32[]{:S(2)}) async-start(bf16[16,384,128]{2,1,0:T(8,128)(2,1)} %get-tuple-element.13), calls=%async_computation | async-start | bytes 3145728 | tf_op jit(solution)/shard_map/all_to_all | solution.py:423
  39.6 7.4 %collective-permute-start = (bf16[16,16,128]{2,1,0:T(8,128)(2,1)S(1)}, bf16[16,16,128]{2,1,0:T(8,128)(2,1)S(1)}, u32[]{:S(2)}, u32[]{:S(2)}) collective-permute-start(bf16[16,16,128]{2,1,0:T(8,128)(2,1)S(1)} %slice.8), channel_id=1, source_target_pairs={{0,1},{1,0},{2,3},{3,2},{4,5},{5,4},{6,7},{7,6},{8,9},{9,8},{10,11... | collective-permute-start | bytes 196616 | tf_op jit(solution)/shard_map/ppermute | solution.py:424
  43.7 41.0 %collective-permute-start.1 = (bf16[16,256,128]{2,1,0:T(8,128)(2,1)}, bf16[16,256,128]{2,1,0:T(8,128)(2,1)}, u32[]{:S(2)}, u32[]{:S(2)}) collective-permute-start(bf16[16,256,128]{2,1,0:T(8,128)(2,1)} %slice.9), channel_id=1, source_target_pairs={{0,1},{1,0},{2,3},{3,2},{4,5},{5,4},{6,7},{7,6},{8,9},{9,8},{10,11... | collective-permute-start | bytes 3145736 | tf_op jit(solution)/shard_map/ppermute | solution.py:425
  53.4 18.5 %all-to-all-start.1 = ((bf16[32,32,128]{2,1,0:T(8,128)(2,1)}), bf16[32,32,128]{2,1,0:T(8,128)(2,1)S(1)}, u32[]{:S(2)}, u32[]{:S(2)}) async-start(bf16[32,32,128]{2,1,0:T(8,128)(2,1)} %bitcast.2), calls=%async_computation.1 | async-start | bytes 524288 | tf_op jit(solution)/shard_map/all_to_all | solution.py:428
  60.2 11.6 %copy-start = (bf16[256,1024]{1,0:T(8,128)(2,1)S(1)}, bf16[256,1024]{1,0:T(8,128)(2,1)}, u32[]{:S(2)}) copy-start(bf16[256,1024]{1,0:T(8,128)(2,1)} %x_hbm.1) | copy-start | bytes 1572868
  60.2 11.6 %copy-start.1 = (bf16[256,256]{1,0:T(8,128)(2,1)S(1)}, bf16[256,256]{1,0:T(8,128)(2,1)}, u32[]{:S(2)}) copy-start(bf16[256,256]{1,0:T(8,128)(2,1)} %get-tuple-element.16.place_ref.place_hbm) | copy-start | bytes 393220
  60.2 11.6 %copy-start.3 = (s32[1,32]{1,0:T(1,128)S(1)}, s32[1,32]{1,0:T(1,128)}, u32[]{:S(2)}) copy-start(s32[1,32]{1,0:T(1,128)} %slots_ref.3) | copy-start | bytes 388
  60.3 11.6 %copy-start.4 = (s32[32]{0:T(128)S(1)}, s32[32]{0:T(128)}, u32[]{:S(2)}) copy-start(s32[32]{0:T(128)} %owner_ref.3) | copy-start | bytes 388
  60.3 11.6 %copy-start.5 = (s32[32]{0:T(128)S(1)}, s32[32]{0:T(128)}, u32[]{:S(2)}) copy-start(s32[32]{0:T(128)} %counts_ref.1) | copy-start | bytes 388
  75.2 9.5 %copy-start.2 = (bf16[32,1024]{1,0:T(8,128)(2,1)}, bf16[32,1024]{1,0:T(8,128)(2,1)S(1)}, u32[]{:S(2)}) copy-start(bf16[32,1024]{1,0:T(8,128)(2,1)S(1)} %get-tuple-element.19.rest_2_.att1_hbm) | copy-start | bytes 196612
  75.2 37.7 %all-to-all-start.2 = ((bf16[32,32,1024]{2,1,0:T(8,128)(2,1)}), bf16[32,32,1024]{2,1,0:T(8,128)(2,1)}, u32[]{:S(2)}, u32[]{:S(2)}) async-start(bf16[32,32,1024]{2,1,0:T(8,128)(2,1)} %get-tuple-element.21), calls=%async_computation.2 | async-start | bytes 4194304 | tf_op jit(solution)/shard_map/all_to_all | solution.py:435

commit v11 on v8

--- a/solution.py
+++ b/solution.py
@@ -407,7 +407,7 @@
     packed, place = project(features, norm_gain, query_index, w_qkv)
     mine = lax.all_to_all(packed, "frame", 0, 0, tiled=True, axis_index_groups=groups)
     picks = lax.ppermute(mine[:, TOK : TOK + CHUNK], "frame", swap_sides)
-    other = lax.ppermute(mine[:, :TOK], "frame", swap_sides)
+    other = lax.ppermute(mine, "frame", swap_sides)
     state1, tick = attend_own(mine, 1, 2)
     parts, tick = attend_picks(mine, picks, me, [tick])
     parts_here = lax.all_to_all(

time: 136 us -> 145 us (1.066)
  waiting for transfers between devices: 23.8 us -> 37.6 us
  starting transfers between devices: 28.3 us -> 23.9 us
    all_to_all x1, waiting for transfers between devices: 0.02 us -> 13.9 us  [per_device(): lax.all_to_all(parts.reshape(FRAMES, QMAX, LANES), 'frame', 0, 0, tiled=T...]
    all_to_all x1, starting transfers between devices: 9.75 us -> 5.28 us  [per_device(): arrived = lax.all_to_all(send, 'frame', 0, 0, tiled=True)]
  transfers between devices with their start and end apart: 5 -> 5, of which waited for: 1 -> 2; matrix products, arithmetic and copies ran while one was open for 1% -> 0% of each run, Pallas kernels for 38% -> 36%
where the time goes in v11:
time: 145 us; the launch traced here: 144 us
  Pallas kernels  63.3 us (44%)
  waiting for transfers between devices  37.6 us (26%)
  starting transfers between devices  23.9 us (16%)
  blocking collectives  16.7 us (12%)
    all_to_all x1, waiting for transfers between devices, per_device(): lax.all_to_all(packed, 'frame', 0, 0, tiled=True, axis_index_groups=groups)  23.8 us
    pallas_call x1, Pallas kernels, attend_other(): pl.pallas_call(functools.partial(other_kernel, starts), in_specs=[VMEM, V...  22.7 us
    pallas_call x3, Pallas kernels, attend_own(): pl.pallas_call(functools.partial(own_kernel, first), in_specs=[VMEM] * (1...  18.7 us
    all_to_all x1, blocking collectives, per_device(): lax.all_to_all(rest, 'frame', 0, 0, tiled=True, axis_index_groups=groups)  16.7 us
    all_to_all x1, waiting for transfers between devices, per_device(): lax.all_to_all(parts.reshape(FRAMES, QMAX, LANES), 'frame', 0, 0, tiled=T...  13.9 us
    all_to_all x1, starting transfers between devices, per_device(): lax.all_to_all(packed, 'frame', 0, 0, tiled=True, axis_index_groups=groups)  8.13 us
    pallas_call x1, Pallas kernels, project(): pl.pallas_call(project_kernel, grid=(steps,), in_specs=[pl.BlockSpec((TOK...  6.99 us
    all_to_all x1, starting transfers between devices, per_device(): lax.all_to_all(parts.reshape(FRAMES, QMAX, LANES), 'frame', 0, 0, tiled=T...  6.81 us
  transfers between devices with their start and end apart: 5, of which 2 were waited for; matrix products, arithmetic and copies ran while one was open for 0% of the time, Pallas kernels for 36%

profile of v11, /device:TPU:0, one launch (start us, length us, event | category | flops | bytes accessed | tf_op | source)
XLA Modules:
  0.0 143.5 jit_solution(13558450567060125491)
XLA Ops:
  0.6 7.0 %project.1 = (bf16[16,384,128]{2,1,0:T(8,128)(2,1)}, bf16[256,256]{1,0:T(8,128)(2,1)}) custom-call(bf16[256,1024]{1,0:T(8,128)(2,1)} %x_hbm.1, f32[1,1024]{1,0:T(1,128)} %bitcast.3, s32[1,32]{1,0:T(1,128)} %slots_ref.3, bf16[1024,3072]{1,0:T(8,128)(2,1)} %wv_ref.1, bf16[1024,3072]{1,0:T(8,128)(2,1)} %wv_ref.1, bf16[1024,3072]{1,0:T(8,128)(2,1)} %wv_ref.1), custom_call_target="tpu_custom_call" | custom-call | tf_op jit(solution)/shard_map/project/pallas_call | solution.py:84
  7.6 8.1 %all-to-all-start = ((bf16[16,384,128]{2,1,0:T(8,128)(2,1)}), bf16[16,384,128]{2,1,0:T(8,128)(2,1)S(1)}, u32[]{:S(2)}, u32[]{:S(2)}) async-start(bf16[16,384,128]{2,1,0:T(8,128)(2,1)} %get-tuple-element.14), calls=%async_computation | async-start | bytes 3145728 | tf_op jit(solution)/shard_map/all_to_all | solution.py:408
  15.8 23.8 %all-to-all-done.mine_ref = bf16[16,384,128]{2,1,0:T(8,128)(2,1)S(1)} async-done(((bf16[16,384,128]{2,1,0:T(8,128)(2,1)}), bf16[16,384,128]{2,1,0:T(8,128)(2,1)S(1)}, u32[]{:S(2)}, u32[]{:S(2)}) %all-to-all-start) | async-done | bytes 1572896 | tf_op jit(solution)/shard_map/all_to_all | solution.py:408
  39.5 3.1 %collective-permute-start = (bf16[16,16,128]{2,1,0:T(8,128)(2,1)S(1)}, bf16[16,16,128]{2,1,0:T(8,128)(2,1)S(1)}, u32[]{:S(2)}, u32[]{:S(2)}) collective-permute-start(bf16[16,16,128]{2,1,0:T(8,128)(2,1)S(1)} %slice.4), channel_id=1, source_target_pairs={{0,1},{1,0},{2,3},{3,2},{4,5},{5,4},{6,7},{7,6},{8,9},{9,8},{10,11... | collective-permute-start | bytes 196616 | tf_op jit(solution)/shard_map/ppermute | solution.py:409
  42.7 2.8 %attend_own_1.1 = (f32[512,128]{1,0:T(8,128)S(1)}, f32[8,128]{1,0:T(8,128)S(1)}) custom-call(bf16[16,384,128]{2,1,0:T(8,128)(2,1)S(1)} %all-to-all-done.mine_ref), custom_call_target="tpu_custom_call" | custom-call | flops 2147483648 | bytes 1048576 | tf_op jit(solution)/shard_map/attend_own_1/pallas_call | solution.py:229
  45.4 0.6 collective-permute-start.1
  46.0 6.4 %attend_picks.1 = (bf16[16,2,32,128]{3,2,1,0:T(8,128)(2,1)}, f32[8,128]{1,0:T(8,128)S(1)}) custom-call(bf16[16,384,128]{2,1,0:T(8,128)(2,1)S(1)} %all-to-all-done.mine_ref, bf16[16,16,128]{2,1,0:T(8,128)(2,1)S(1)} %collective-permute-done.picks_ref, s32[1]{0:T(128)} %bitcast.me_ref, f32[8,128]{1,0:T(8,128)S(1)} %get-tuple-element.15.rest_0_), custom_call_target="tpu_custom_call" | custom-call | flops 4294967296 | bytes 1048576 | tf_op jit(solution)/shard_map/attend_picks/pallas_call | solution.py:240
  52.4 6.8 %all-to-all-start.1 = ((bf16[32,32,128]{2,1,0:T(8,128)(2,1)}), bf16[32,32,128]{2,1,0:T(8,128)(2,1)S(1)}, u32[]{:S(2)}, u32[]{:S(2)}) async-start(bf16[32,32,128]{2,1,0:T(8,128)(2,1)} %bitcast.2), calls=%async_computation.1 | async-start | bytes 524288 | tf_op jit(solution)/shard_map/all_to_all | solution.py:413
  59.2 0.0 copy-start
  59.3 0.0 copy-start.3
  59.3 0.0 copy-start.4
  59.3 0.0 copy-start.5
  59.3 10.6 %attend_own_2.1 = (f32[2048,128]{1,0:T(8,128)S(1)}, f32[8,128]{1,0:T(8,128)}) custom-call(bf16[16,384,128]{2,1,0:T(8,128)(2,1)S(1)} %all-to-all-done.mine_ref, f32[8,128]{1,0:T(8,128)S(1)} %get-tuple-element.18.rest_0_), custom_call_target="tpu_custom_call" | custom-call | flops 8589934592 | bytes 1048576 | tf_op jit(solution)/shard_map/attend_own_2/pallas_call | solution.py:229
  69.9 0.0 copy-start.6
  69.9 1.0 copy-done.6
  70.8 13.9 %all-to-all-done.1.part_ref = bf16[32,32,128]{2,1,0:T(8,128)(2,1)S(1)} async-done(((bf16[32,32,128]{2,1,0:T(8,128)(2,1)}), bf16[32,32,128]{2,1,0:T(8,128)(2,1)S(1)}, u32[]{:S(2)}, u32[]{:S(2)}) %all-to-all-start.1) | async-done | bytes 262176 | tf_op jit(solution)/shard_map/all_to_all | solution.py:413
  84.7 3.3 %track_rows.1 = (bf16[32,32,1024]{2,1,0:T(8,128)(2,1)}, bf16[32,1024]{1,0:T(8,128)(2,1)S(1)}) custom-call(bf16[32,32,128]{2,1,0:T(8,128)(2,1)S(1)} %all-to-all-done.1.part_ref, bf16[1024,1024]{1,0:T(8,128)(2,1)} %w_hbm.3, bf16[256,1024]{1,0:T(8,128)(2,1)S(1)} %copy-done, bf16[256,256]{1,0:T(8,128)(2,1)S(1)} %copy-done.1, s32[1,32]{1,0:T(1,128)S(1)} %copy-done.3, ...), custom_call_target="tpu_custom_call" | custom-call | flops 2147483648 | bytes 4194304 | tf_op jit(solution)/shard_map/track_rows/pallas_call | solution.py:320
  88.1 5.3 %all-to-all-start.2 = ((bf16[32,32,1024]{2,1,0:T(8,128)(2,1)}), bf16[32,32,1024]{2,1,0:T(8,128)(2,1)}, u32[]{:S(2)}, u32[]{:S(2)}) async-start(bf16[32,32,1024]{2,1,0:T(8,128)(2,1)} %get-tuple-element.23), calls=%async_computation.2 | async-start | bytes 4194304 | tf_op jit(solution)/shard_map/all_to_all | solution.py:420
  93.4 0.0 copy-start.7
  93.4 5.4 %attend_own_6.1 = (f32[1024,128]{1,0:T(8,128)S(1)}, f32[8,128]{1,0:T(8,128)}) custom-call(bf16[16,384,128]{2,1,0:T(8,128)(2,1)S(1)} %all-to-all-done.mine_ref, bf16[32,1024]{1,0:T(8,128)(2,1)S(1)} %get-tuple-element.20.rest_0_.att1_hbm), custom_call_target="tpu_custom_call" | custom-call | flops 4294967296 | bytes 1048576 | tf_op jit(solution)/shard_map/attend_own_6/pallas_call | solution.py:229
  98.8 22.7 %attend_other.1 = bf16[16,112,128]{2,1,0:T(8,128)(2,1)S(1)} custom-call(bf16[16,384,128]{2,1,0:T(8,128)(2,1)S(1)} %all-to-all-done.mine_ref, bf16[16,384,128]{2,1,0:T(8,128)(2,1)} %collective-permute-done.1.other_ref, f32[512,128]{1,0:T(8,128)S(1)} %get-tuple-element.21.rest_0_, f32[2048,128]{1,0:T(8,128)S(1)} %copy-done.7, ...), custom_call_target="tpu_custom_call" | custom-call | flops 15032385536 | bytes 1048576 | tf_op jit(solution)/shard_map/attend_other/pallas_call | solution.py:259
  121.5 0.0 all-to-all-done.2.rows_hbm
  121.5 16.7 %all_to_all.20.at2_hbm = bf16[16,112,128]{2,1,0:T(8,128)(2,1)} all-to-all(bf16[16,112,128]{2,1,0:T(8,128)(2,1)S(1)} %attend_other.1), channel_id=1, replica_groups={{0,2,4,6,8,10,12,14,16,18,20,22,24,26,28,30},{1,3,5,7,9,11,13,15,17,19,..., dimensions={0} | all-to-all | bytes 917504 | tf_op jit(solution)/shard_map/all_to_all | solution.py:424
  138.2 5.2 %finish.1 = (bf16[256,1024]{1,0:T(8,128)(2,1)}, f32[1,32,32,256]{3,2,1,0:T(8,128)}) custom-call(s32[32]{0:T(128)} %owner_ref.3, s32[1]{0:T(128)} %bitcast.me_ref, bf16[32,1024]{1,0:T(8,128)(2,1)} %copy-done.2, bf16[16,112,128]{2,1,0:T(8,128)(2,1)} %all_to_all.20.at2_hbm, bf16[256,256]{1,0:T(8,128)(2,1)} %get-tuple-element.17.place_ref.place_hbm, ...), custom_call_target="tpu_custom_call" | custom-call | tf_op jit(solution)/shard_map/finish/pallas_call | solution.py:382
  (12 shorter events, 0.0 us)
Async XLA Ops:
  7.6 31.9 %all-to-all-start = ((bf16[16,384,128]{2,1,0:T(8,128)(2,1)}), bf16[16,384,128]{2,1,0:T(8,128)(2,1)S(1)}, u32[]{:S(2)}, u32[]{:S(2)}) async-start(bf16[16,384,128]{2,1,0:T(8,128)(2,1)} %get-tuple-element.14), calls=%async_computation | async-start | bytes 3145728 | tf_op jit(solution)/shard_map/all_to_all | solution.py:408
  39.5 6.5 %collective-permute-start = (bf16[16,16,128]{2,1,0:T(8,128)(2,1)S(1)}, bf16[16,16,128]{2,1,0:T(8,128)(2,1)S(1)}, u32[]{:S(2)}, u32[]{:S(2)}) collective-permute-start(bf16[16,16,128]{2,1,0:T(8,128)(2,1)S(1)} %slice.4), channel_id=1, source_target_pairs={{0,1},{1,0},{2,3},{3,2},{4,5},{5,4},{6,7},{7,6},{8,9},{9,8},{10,11... | collective-permute-start | bytes 196616 | tf_op jit(solution)/shard_map/ppermute | solution.py:409
  45.4 53.3 %collective-permute-start.1 = (bf16[16,384,128]{2,1,0:T(8,128)(2,1)S(1)}, bf16[16,384,128]{2,1,0:T(8,128)(2,1)}, u32[]{:S(2)}, u32[]{:S(2)}) collective-permute-start(bf16[16,384,128]{2,1,0:T(8,128)(2,1)S(1)} %all-to-all-done.mine_ref), channel_id=1, source_target_pairs={{0,1},{1,0},{2,3},{3,2},{4,5},{5,4},{6,7},{7,6},{8,9},{9,8},{10,11... | collective-permute-start | bytes 4718600 | tf_op jit(solution)/shard_map/ppermute | solution.py:410
  52.4 32.3 %all-to-all-start.1 = ((bf16[32,32,128]{2,1,0:T(8,128)(2,1)}), bf16[32,32,128]{2,1,0:T(8,128)(2,1)S(1)}, u32[]{:S(2)}, u32[]{:S(2)}) async-start(bf16[32,32,128]{2,1,0:T(8,128)(2,1)} %bitcast.2), calls=%async_computation.1 | async-start | bytes 524288 | tf_op jit(solution)/shard_map/all_to_all | solution.py:413
  59.2 25.5 %copy-start = (bf16[256,1024]{1,0:T(8,128)(2,1)S(1)}, bf16[256,1024]{1,0:T(8,128)(2,1)}, u32[]{:S(2)}) copy-start(bf16[256,1024]{1,0:T(8,128)(2,1)} %x_hbm.1) | copy-start | bytes 1572868
  59.2 25.5 %copy-start.1 = (bf16[256,256]{1,0:T(8,128)(2,1)S(1)}, bf16[256,256]{1,0:T(8,128)(2,1)}, u32[]{:S(2)}) copy-start(bf16[256,256]{1,0:T(8,128)(2,1)} %get-tuple-element.17.place_ref.place_hbm) | copy-start | bytes 393220
  59.3 25.5 %copy-start.3 = (s32[1,32]{1,0:T(1,128)S(1)}, s32[1,32]{1,0:T(1,128)}, u32[]{:S(2)}) copy-start(s32[1,32]{1,0:T(1,128)} %slots_ref.3) | copy-start | bytes 388
  59.3 25.4 %copy-start.4 = (s32[32]{0:T(128)S(1)}, s32[32]{0:T(128)}, u32[]{:S(2)}) copy-start(s32[32]{0:T(128)} %owner_ref.3) | copy-start | bytes 388
  59.3 25.4 %copy-start.5 = (s32[32]{0:T(128)S(1)}, s32[32]{0:T(128)}, u32[]{:S(2)}) copy-start(s32[32]{0:T(128)} %counts_ref.1) | copy-start | bytes 388
  69.9 1.0 copy-start.6
  88.1 5.3 %copy-start.2 = (bf16[32,1024]{1,0:T(8,128)(2,1)}, bf16[32,1024]{1,0:T(8,128)(2,1)S(1)}, u32[]{:S(2)}) copy-start(bf16[32,1024]{1,0:T(8,128)(2,1)S(1)} %get-tuple-element.20.rest_0_.att1_hbm) | copy-start | bytes 196612
  88.1 33.4 %all-to-all-start.2 = ((bf16[32,32,1024]{2,1,0:T(8,128)(2,1)}), bf16[32,32,1024]{2,1,0:T(8,128)(2,1)}, u32[]{:S(2)}, u32[]{:S(2)}) async-start(bf16[32,32,1024]{2,1,0:T(8,128)(2,1)} %get-tuple-element.23), calls=%async_computation.2 | async-start | bytes 4194304 | tf_op jit(solution)/shard_map/all_to_all | solution.py:420
  93.4 5.4 %copy-start.7 = (f32[2048,128]{1,0:T(8,128)S(1)}, f32[2048,128]{1,0:T(8,128)}, u32[]{:S(2)}) copy-start(f32[2048,128]{1,0:T(8,128)} %copy-done.6) | copy-start | bytes 3145732
